TPU v7x, 32 devices: a whole 2x2x4 slice. The times are simulated.
32 devices in a mesh: member: 1, tile: 32 (over z, y, x, core).
Axes of the slice: x: 2, y: 2, z: 4, core: 2. Of those that a mesh axis runs over, the one named last changes fastest.
Arguments:
- forcing: bfloat16 [128, 8, 10, 128], P(('member', 'tile')), may hold values from -6 to 6
- ice_state: bfloat16 [1024, 128, 128], P(('member', 'tile')), may hold values from -6 to 6
- sensitivity: bfloat16 [1024, 128, 128], P(('member', 'tile')), may hold values from -6 to 6
- owner_device: int32 [1024, 4], P('tile'), may hold values from 0 to 31, all different within a row; in each aligned block of 32 rows (0 to 31, 32 to 63, ...) at most 8 rows name the same one
- panel_slot: int32 [1024, 4], P('tile'), may hold values from 0 to 3
- row_offset: int32 [1024, 4], P('tile'), may hold values from 0 to 7
- intersection_weight: float32 [1024, 4], P('tile'), may hold values from 0.2 to 1
- col_map: float32 [128, 128], replicated, may hold values from 0 to 1
- ocean_mask: int32 [1024, 128], P('tile'), may hold values 0 or 1
- lift_weight: bfloat16 [10, 128], replicated, may hold values from -1 to 1
- conv_weight: bfloat16 [3, 3, 3, 128, 128], replicated, may hold values from -0.1875 to 0.1875
- conv_bias: float32 [3, 128], replicated, may hold values from -3 to 3
Outputs:
- imitated: bfloat16 [1024, 128, 128], P(('member', 'tile'))
- state_grad: bfloat16 [1024, 128, 128], P(('member', 'tile'))
- forcing_grad: float32 [128, 8, 10, 128], P(('member', 'tile'))
Inputs may be any that keep to these rules, and one draw needn't show every extreme that they name: `owner_device`: each ice row names 4 different owners; in the rows of one device no owner is named by more than 8 intersections, and that count is reached.
All inputs are finite; a program needn't handle non-finite values. No bound on the sum of `ocean_mask` on one device may be relied on, other than what follows from the above.
Results may differ from a plain program's by a relative error of at most 0.015.
Values may be sent and summed in bfloat16 or wider, within the bound.
No kernel may reach another device: no remote copies, remote signals or barrier semaphores. Data moves between devices by JAX's collectives and lax.ppermute only.
A program may use at most 128 MiB of HBM per device.

v0:
```python
import functools

import jax
import jax.numpy as jnp
from jax import lax
from jax.experimental import pallas as pl
from jax.experimental.pallas import tpu as pltpu
from jax.sharding import PartitionSpec as P

F = 10
FP = 16
K = 4
C = 128
ROWS = 32
EXT = 48
PAD = 8
GROUP = 8
PAIR = 2 * C
TAPS = 3 * C
BF = jnp.bfloat16
F32 = jnp.float32
MIB = 1 << 20


def params(mib):
    return pltpu.CompilerParams(vmem_limit_bytes=mib * MIB)


def dot(a, b, dims=(((1,), (0,)), ((), ()))):
    return lax.dot_general(a, b, dims, preferred_element_type=F32)


def split(x):
    high = x.astype(BF)
    return high, (x - high.astype(F32)).astype(BF)


def fine_dot(a, b, dims=(((1,), (0,)), ((), ()))):
    ah, al = split(a)
    bh, bl = split(b)
    return dot(ah, bh, dims) + (dot(ah, bl, dims) + dot(al, bh, dims))


def pair_rows(index, count=1):
    start = index * C
    if not isinstance(index, int):
        start = pl.multiple_of(start, C)
    return pl.ds(start, count * C)


def store_pair(xp, index, value):
    column = lax.broadcasted_iota(jnp.int32, (C, PAIR), 0)
    before = jnp.where(column == 0, 0.0, pltpu.roll(value, 1, 0)).astype(BF)
    after = jnp.where(column == C - 1, 0.0, pltpu.roll(value, C - 1, 0)).astype(BF)
    value = value.astype(BF)
    rows = pair_rows(index)
    for half in range(2):
        lanes = slice(half * C, half * C + C)
        for tap, part in enumerate((before, value, after)):
            start = half * TAPS + tap * C
            xp[rows, start : start + C] = part[:, lanes]


def centre(xp, index):
    low = xp[pair_rows(index), TAPS + C : TAPS + 2 * C]
    high = xp[pair_rows(index + 1), C : 2 * C]
    return jnp.concatenate([low, high], axis=1).astype(F32)


def two_rows(ref, row):
    start = row * C
    if not isinstance(row, int):
        start = pl.multiple_of(start, C)
    low = ref[pl.ds(start, C), :]
    high = ref[pl.ds(start + C, C), :]
    return jnp.concatenate([low, high], axis=1).astype(F32)


def layer(xp, weight, count, step, finish):
    def chunk(first, size):
        total = dot(xp[pair_rows(first, size), :], weight[: 2 * TAPS, :])
        total += dot(xp[pair_rows(first + 1, size), :], weight[2 * TAPS :, :])
        for j in range(size):
            finish(first + j, total[j * C : (j + 1) * C])

    full = count // step

    def body(i, carry):
        chunk(i * step, step)
        return carry

    lax.fori_loop(0, full, body, 0)
    if count % step:
        chunk(full * step, count % step)


def prep_kernel(forcing, owner, slot, offset, weight, fields, table):
    rows = forcing[...].reshape(ROWS, F, C).astype(F32)
    for f in range(F):
        fields[f * ROWS : (f + 1) * ROWS, :] = rows[:, f, :].astype(BF)
    ident = ((owner[...] * 4 + slot[...]) * 8 + offset[...]).astype(F32)
    lane = lax.broadcasted_iota(jnp.int32, (ROWS, C), 1)
    row = lax.broadcasted_iota(jnp.int32, (ROWS, C), 0)

    def spread(value):
        total = jnp.zeros((1, C), F32)
        for k in range(K):
            here = jnp.where(lane == k * ROWS + row, value[:, k : k + 1], 0.0)
            total += jnp.sum(here, axis=0, keepdims=True)
        return total

    block = jnp.concatenate(
        [spread(ident), spread(weight[...]), jnp.zeros((6, C), F32)], axis=0
    )
    table[...] = jnp.broadcast_to(block[None], table.shape)


def message_kernel(planes, table, *refs):
    blocks, outs, scatter, wide = refs[:planes], refs[planes:-2], refs[-2], refs[-1]
    me = lax.axis_index("tile")
    plane, spot = me // GROUP, me % GROUP
    count = planes * GROUP
    for z in range(planes):
        for f in range(F):
            wide[z * ROWS : (z + 1) * ROWS, f * C : (f + 1) * C] = blocks[z][
                f * ROWS : (f + 1) * ROWS, :
            ]
    sources = planes * ROWS
    lane = lax.broadcasted_iota(jnp.int32, (1, sources), 1)
    from_plane = lax.rem(plane - lane // ROWS + planes, planes)
    ident = ((from_plane * GROUP + spot) * ROWS + lane % ROWS).astype(F32)
    idents, weights = [], []
    for s in range(GROUP):
        mate = plane * GROUP + (spot ^ s)
        for step in (-1, 0, 1):
            device = mate + step
            inside = jnp.logical_and(device >= 0, device < count)
            entry = table[jnp.clip(device, 0, count - 1)]
            idents.append(entry[0:1])
            weights.append(jnp.where(inside, entry[1:2], 0.0))
    fill = [jnp.zeros((C - 3 * GROUP, C), F32)]
    idents = jnp.concatenate(idents + fill, axis=0).T
    weights = jnp.concatenate(weights + fill, axis=0).T
    picks = []
    for s in range(GROUP):
        parts = []
        for step, start, size in ((0, ROWS - PAD, PAD), (1, 0, ROWS), (2, 0, PAD)):
            col = 3 * s + step
            total = jnp.zeros((size, sources), F32)
            for k in range(K):
                rows = slice(k * ROWS + start, k * ROWS + start + size)
                named = idents[rows, col : col + 1] == ident
                total += jnp.where(named, weights[rows, col : col + 1], 0.0)
            parts.append(total)
        picks.append(jnp.concatenate(parts, axis=0))
    every = jnp.concatenate(picks, axis=0).astype(BF)
    for f in range(F):
        found = dot(every, wide[:, f * C : (f + 1) * C]).astype(BF)
        for s in range(GROUP):
            outs[s][f * EXT : (f + 1) * EXT, :] = found[s * EXT : (s + 1) * EXT]
    own = jnp.concatenate([pick[PAD : PAD + ROWS] for pick in picks], axis=0)
    scatter[...] = own.T.astype(BF)


def weight_kernel(weight, *outs):
    zero = jnp.zeros((TAPS, C), BF)
    for l in range(3):
        for back in range(2):
            out = outs[2 * l + back]
            out[0:TAPS, C:] = zero
            out[3 * TAPS :, :C] = zero
            for a in range(3):
                for b in range(3):
                    if back:
                        block = weight[l, 2 - a, 2 - b].astype(F32).T.astype(BF)
                    else:
                        block = weight[l, a, b]
                    for half in range(2):
                        start = (a + half) * TAPS + b * C
                        out[start : start + C, half * C : half * C + C] = block


def first_kernel(ice, low, high, mask, weight, bias, hidden, slope, ocean, xp):
    def ice_row(r):
        if r < 0:
            return low[(r + 6) * C : (r + 7) * C, :]
        if r >= ROWS:
            return high[(r - ROWS) * C : (r - ROWS + 1) * C, :]
        return ice[r]

    for p in range(22):
        row = 2 * p - 6
        store_pair(xp, p, jnp.concatenate([ice_row(row), ice_row(row + 1)], axis=1).astype(F32))
    edge = 9 * C
    cells = jnp.concatenate(
        [low[edge : edge + 8, :].astype(F32), mask[...].astype(F32), high[edge : edge + 8, :].astype(F32)],
        axis=0,
    )
    cells = jnp.concatenate([cells, jnp.zeros((C - EXT, C), F32)], axis=0).T
    for r in range(-5, 37):
        column = jnp.broadcast_to(cells[:, r + PAD : r + PAD + 1], (C, C))
        ocean[(r + 5) * C : (r + 6) * C, :] = column.astype(BF)
    both = jnp.concatenate([bias[0:1, :], bias[0:1, :]], axis=1)

    def finish(p, total):
        tangent = jnp.tanh(total + both)
        cell = two_rows(ocean, 2 * p)
        slope[pair_rows(p), :] = (cell * (1.0 - tangent * tangent)).astype(BF)
        hidden[pair_rows(p), :] = (centre(xp, p) + cell * tangent).astype(BF)

    layer(xp, weight, 21, 7, finish)


def main_kernel(*refs):
    messages = refs[:GROUP]
    (col_map, lift, bias, hidden, slope0, ocean, sens, low, high, w1f, w2f, w2b, w1b) = refs[
        GROUP : GROUP + 13
    ]
    imitated, act0, grad1, project = refs[GROUP + 13 : GROUP + 17]
    ice, lifted, diag, xa, xb, slope1, slope2, grads, out_rows, turned = refs[GROUP + 17 :]
    ice[...] = jnp.zeros(ice.shape, F32)
    for f in range(F):
        rows = slice(f * EXT, (f + 1) * EXT)
        total = messages[0][rows, :].astype(F32)
        for s in range(1, GROUP):
            total += messages[s][rows, :].astype(F32)
        ice[:, f, :] = fine_dot(total, col_map[...])
    diag[...] = jnp.zeros(diag.shape, BF)
    for j in range(GROUP):
        diag[j * FP : j * FP + F, j * C : (j + 1) * C] = lift[...]
    for group in range(EXT // GROUP):
        block = ice[group * GROUP : (group + 1) * GROUP].reshape(C, C)
        turned[group * C : (group + 1) * C, :] = block.T.astype(BF)
    for group in range(EXT // GROUP):
        lifted[group * C : (group + 1) * C, :] = dot(
            turned[group * C : (group + 1) * C, :], diag[...]
        )

    def lifted_row(r):
        e = r + PAD
        return lifted[(e // 8) * C : (e // 8 + 1) * C, (e % 8) * C : (e % 8 + 1) * C]

    for p in range(21):
        row = 2 * p - 5
        add = jnp.concatenate([lifted_row(row), lifted_row(row + 1)], axis=1)
        value = (hidden[pair_rows(p), :].astype(F32) + add).astype(BF)
        store_pair(xa, p, value.astype(F32))

    def bias_of(l):
        return jnp.concatenate([bias[l : l + 1, :], bias[l : l + 1, :]], axis=1)

    bias1, bias2 = bias_of(1), bias_of(2)

    def finish1(p, total):
        tangent = jnp.tanh(total + bias1)
        cell = two_rows(ocean, 2 * p + 1)
        slope1[pair_rows(p), :] = (cell * (1.0 - tangent * tangent)).astype(BF)
        value = (centre(xa, p) + cell * tangent).astype(BF)
        store_pair(xb, p, value.astype(F32))

    layer(xa, w1f, 20, 5, finish1)

    def finish2(p, total):
        tangent = jnp.tanh(total + bias2)
        cell = two_rows(ocean, 2 * p + 2)
        slope2[pair_rows(p), :] = (cell * (1.0 - tangent * tangent)).astype(BF)
        value = (centre(xb, p) + cell * tangent).astype(BF)
        out_rows[pair_rows(2 * p), :] = value[:, :C]
        out_rows[pair_rows(2 * p + 1), :] = value[:, C:]

    layer(xb, w2f, 19, 5, finish2)
    imitated[...] = out_rows[3 * C : 35 * C, :].reshape(ROWS, C, C)

    def sens_row(r):
        if r < 0:
            return low[(r + 9) * C : (r + 10) * C, :]
        if r >= ROWS:
            return high[(r - ROWS + 6) * C : (r - ROWS + 7) * C, :]
        return sens[r]

    for p in range(19):
        row = 2 * p - 3
        value = jnp.concatenate([sens_row(row), sens_row(row + 1)], axis=1).astype(F32)
        store_pair(xa, p, value * slope2[pair_rows(p), :].astype(F32))
        out_rows[pair_rows(2 * p), :] = sens_row(row)
        out_rows[pair_rows(2 * p + 1), :] = sens_row(row + 1)

    def finish3(p, total):
        total += two_rows(out_rows, 2 * p + 1)
        grads[pair_rows(2 * p), :] = total[:, :C]
        grads[pair_rows(2 * p + 1), :] = total[:, C:]
        store_pair(xb, p, total * slope1[pair_rows(p + 1), :].astype(F32))

    layer(xa, w2b, 18, 6, finish3)

    def finish4(p, total):
        total += two_rows(grads, 2 * p + 1)
        act0[pair_rows(p), :] = (total * slope0[pair_rows(p + 2), :].astype(F32)).astype(BF)
        grad1[pair_rows(2 * p), :] = total[:, :C]
        grad1[pair_rows(2 * p + 1), :] = total[:, C:]

    layer(xb, w1b, 17, 6, finish4)
    short = jnp.concatenate([lift[...].astype(F32), jnp.zeros((FP - F, C), F32)], axis=0).astype(BF)
    nt = (((1,), (1,)), ((), ()))
    for r in range(ROWS):
        part = dot(short, grad1[(r + 1) * C : (r + 2) * C, :].astype(BF), nt)
        ice[r, :, :] = part
    ice[0:ROWS] = fine_dot(ice[0:ROWS].reshape(ROWS * FP, C), col_map[...], nt).reshape(ROWS, FP, C)
    for f in range(F):
        project[f * ROWS : (f + 1) * ROWS, :] = ice[0:ROWS, f, :].astype(BF)


def last_kernel(act0, grad1, weight, out, xp):
    for p in range(17):
        store_pair(xp, p, act0[pair_rows(p), :].astype(F32))

    def finish(p, total):
        total += two_rows(grad1, 2 * p + 1)
        out[2 * p] = total[:, :C].astype(BF)
        out[2 * p + 1] = total[:, C:].astype(BF)

    layer(xp, weight, 16, 4, finish)


def scatter_kernel(planes, scatter, *refs):
    blocks, outs, wide = refs[:GROUP], refs[GROUP:-1], refs[-1]
    for s in range(GROUP):
        for f in range(F):
            wide[s * ROWS : (s + 1) * ROWS, f * C : (f + 1) * C] = blocks[s][
                f * ROWS : (f + 1) * ROWS, :
            ]
    for f in range(F):
        found = dot(scatter[...], wide[:, f * C : (f + 1) * C]).astype(BF)
        for z in range(planes):
            outs[z][f * ROWS : (f + 1) * ROWS, :] = found[z * ROWS : (z + 1) * ROWS]


def sum_kernel(planes, *refs):
    blocks, out = refs[:planes], refs[planes]
    for f in range(F):
        rows = slice(f * ROWS, (f + 1) * ROWS)
        total = blocks[0][rows, :].astype(F32)
        for z in range(1, planes):
            total += blocks[z][rows, :].astype(F32)
        out[:, f, :] = total


def shape(*dims, dtype=BF):
    return jax.ShapeDtypeStruct(dims, dtype)


def body(
    forcing,
    ice_state,
    sensitivity,
    owner_device,
    panel_slot,
    row_offset,
    intersection_weight,
    col_map,
    ocean_mask,
    lift_weight,
    conv_weight,
    conv_bias,
):
    count = lax.axis_size("tile")
    planes = count // GROUP

    def by_plane(step):
        return [(i, (i + GROUP * step) % count) for i in range(count)]

    def by_mate(step):
        return [(i, i ^ step) for i in range(count)]

    fields, table = pl.pallas_call(
        prep_kernel,
        out_shape=(shape(F * ROWS, C), shape(count, 8, C, dtype=F32)),
        name="prep",
    )(forcing, owner_device, panel_slot, row_offset, intersection_weight)
    blocks = [fields] + [lax.ppermute(fields, "tile", by_plane(z)) for z in range(1, planes)]
    table = lax.all_to_all(table, "tile", 0, 0, tiled=True)

    mask = ocean_mask.astype(BF)
    flat_ice = ice_state.reshape(ROWS * C, C)
    flat_sens = sensitivity.reshape(ROWS * C, C)
    to_next = jnp.concatenate([flat_ice[26 * C :], flat_sens[29 * C :], mask[24:], mask[24:]], axis=0)
    to_last = jnp.concatenate([flat_ice[: 6 * C], flat_sens[: 3 * C], mask[:8], mask[:8]], axis=0)
    forward = [(i, i + 1) for i in range(count - 1)]
    low = lax.ppermute(to_next, "tile", forward)
    high = lax.ppermute(to_last, "tile", [(b, a) for a, b in forward])

    weights = pl.pallas_call(
        weight_kernel,
        out_shape=tuple(shape(4 * TAPS, PAIR) for _ in range(6)),
        compiler_params=params(32),
        name="taps",
        cost_estimate=pl.CostEstimate(flops=0, bytes_accessed=6 * MIB, transcendentals=0),
    )(conv_weight)

    *messages, scatter = pl.pallas_call(
        functools.partial(message_kernel, planes),
        out_shape=tuple(shape(F * EXT, C) for _ in range(GROUP)) + (shape(planes * ROWS, GROUP * ROWS),),
        scratch_shapes=[pltpu.VMEM((planes * ROWS, F * C), BF)],
        compiler_params=params(32),
        name="messages",
    )(table, *blocks)
    messages = messages[:1] + [
        lax.ppermute(messages[s], "tile", by_mate(s)) for s in range(1, GROUP)
    ]

    hidden, slope0, ocean = pl.pallas_call(
        first_kernel,
        out_shape=(shape(21 * C, PAIR), shape(21 * C, PAIR), shape(42 * C, C)),
        scratch_shapes=[pltpu.VMEM((22 * C, 2 * TAPS), BF)],
        compiler_params=params(48),
        name="first_layer",
        cost_estimate=pl.CostEstimate(flops=4 * 10**9, bytes_accessed=8 * MIB, transcendentals=10**6),
    )(ice_state, low, high, ocean_mask, weights[0], conv_bias)

    imitated, act0, grad1, project = pl.pallas_call(
        main_kernel,
        out_shape=(
            shape(ROWS, C, C),
            shape(17 * C, PAIR),
            shape(34 * C, C, dtype=F32),
            shape(F * ROWS, C),
        ),
        scratch_shapes=[
            pltpu.VMEM((EXT, FP, C), F32),
            pltpu.VMEM((EXT // GROUP * C, GROUP * C), F32),
            pltpu.VMEM((C, GROUP * C), BF),
            pltpu.VMEM((21 * C, 2 * TAPS), BF),
            pltpu.VMEM((20 * C, 2 * TAPS), BF),
            pltpu.VMEM((20 * C, PAIR), BF),
            pltpu.VMEM((19 * C, PAIR), BF),
            pltpu.VMEM((36 * C, C), F32),
            pltpu.VMEM((38 * C, C), BF),
            pltpu.VMEM((EXT // GROUP * C, C), BF),
        ],
        compiler_params=params(56),
        name="middle_layers",
        cost_estimate=pl.CostEstimate(flops=12 * 10**9, bytes_accessed=16 * MIB, transcendentals=10**6),
    )(
        *messages,
        col_map,
        lift_weight,
        conv_bias,
        hidden,
        slope0,
        ocean,
        sensitivity,
        low,
        high,
        weights[2],
        weights[4],
        weights[5],
        weights[3],
    )
    projects = [project] + [lax.ppermute(project, "tile", by_mate(s)) for s in range(1, GROUP)]

    state_grad = pl.pallas_call(
        last_kernel,
        out_shape=shape(ROWS, C, C),
        scratch_shapes=[pltpu.VMEM((17 * C, 2 * TAPS), BF)],
        compiler_params=params(48),
        name="last_adjoint",
        cost_estimate=pl.CostEstimate(flops=3 * 10**9, bytes_accessed=6 * MIB, transcendentals=0),
    )(act0, grad1, weights[1])

    sums = pl.pallas_call(
        functools.partial(scatter_kernel, planes),
        out_shape=tuple(shape(F * ROWS, C) for _ in range(planes)),
        scratch_shapes=[pltpu.VMEM((GROUP * ROWS, F * C), BF)],
        compiler_params=params(32),
        name="scatter",
    )(scatter, *projects)
    sums = [sums[0]] + [lax.ppermute(sums[z], "tile", by_plane(-z)) for z in range(1, planes)]
    panel_grad = pl.pallas_call(
        functools.partial(sum_kernel, planes),
        out_shape=shape(ROWS, F, C, dtype=F32),
        name="total",
    )(*sums)
    return imitated, state_grad, panel_grad.reshape(forcing.shape)


def solution(mesh):
    in_specs = (
        P(("member", "tile"), None, None, None),
        P(("member", "tile"), None, None),
        P(("member", "tile"), None, None),
        P("tile", None),
        P("tile", None),
        P("tile", None),
        P("tile", None),
        P(),
        P("tile", None),
        P(),
        P(),
        P(),
    )
    out_specs = (
        P(("member", "tile"), None, None),
        P(("member", "tile"), None, None),
        P(("member", "tile"), None, None, None),
    )
    return jax.shard_map(body, mesh=mesh, in_specs=in_specs, out_specs=out_specs, check_vma=False)
```

profile of v0, /device:TPU:0, one launch (start us, length us, event | category | flops | bytes accessed | tf_op | source)
XLA Modules:
  0.0 108.8 jit_solution(14944735831099884551)
XLA Ops:
  0.6 1.5 %copy.16.owner = s32[32,4]{1,0:T(8,128)} copy(s32[32,4]{0,1:T(4,128)} %param.15) | data formatting | bytes 1024 | tf_op args[3]
  2.1 1.4 %copy.17.slot = s32[32,4]{1,0:T(8,128)} copy(s32[32,4]{0,1:T(4,128)} %param.16) | data formatting | bytes 1024 | tf_op args[4]
  3.5 1.4 %copy.18.offset = s32[32,4]{1,0:T(8,128)} copy(s32[32,4]{0,1:T(4,128)} %param.17) | data formatting | bytes 1024 | tf_op args[5]
  4.8 1.4 %copy.19.weight = f32[32,4]{1,0:T(8,128)} copy(f32[32,4]{0,1:T(4,128)} %param.18) | data formatting | bytes 1024 | tf_op args[6]
  6.2 1.6 %copy.15.forcing = bf16[4,8,10,128]{3,2,1,0:T(8,128)(2,1)} copy(bf16[4,8,10,128]{3,1,2,0:T(8,128)(2,1)} %param.12) | data formatting | bytes 163840 | tf_op args[0]
  7.8 1.8 %prep.1 = (bf16[320,128]{1,0:T(8,128)(2,1)}, f32[32,8,128]{2,1,0:T(8,128)}) custom-call(bf16[4,8,10,128]{3,2,1,0:T(8,128)(2,1)} %copy.15.forcing, s32[32,4]{1,0:T(8,128)} %copy.16.owner, s32[32,4]{1,0:T(8,128)} %copy.17.slot, s32[32,4]{1,0:T(8,128)} %copy.18.offset, f32[32,4]{1,0:T(8,128)} %copy.19.weight), custom_call_target="tpu_custom_call" | custom-call | tf_op jit(solution)/shard_map/prep/pallas_call | solution.py:375
  9.5 7.3 %all-to-all-start = ((f32[32,8,128]{2,1,0:T(8,128)}), f32[32,8,128]{2,1,0:T(8,128)S(1)}, u32[]{:S(2)}, u32[]{:S(2)}) async-start(f32[32,8,128]{2,1,0:T(8,128)} %get-tuple-element.31), calls=%async_computation | async-start | bytes 262144 | tf_op jit(solution)/shard_map/all_to_all | solution.py:381
  18.7 1.3 %collective-permute-start.11 = (bf16[1168,128]{1,0:T(8,128)(2,1)S(1)}, bf16[1168,128]{1,0:T(8,128)(2,1)S(1)}, u32[]{:S(2)}, u32[]{:S(2)}) collective-permute-start(bf16[1168,128]{1,0:T(8,128)(2,1)S(1)} %pad_maximum_fusion.1), channel_id=1, source_target_pairs={{1,0},{2,1},{3,2},{4,3},{5,4},{6,5},{7,6},{8,7},{9,8},{10,9},{11,1... | collective-permute-start | bytes 897032 | tf_op jit(solution)/shard_map/ppermute | solution.py:390
  20.7 3.0 %collective-permute-start.10 = (bf16[1168,128]{1,0:T(8,128)(2,1)}, bf16[1168,128]{1,0:T(8,128)(2,1)S(1)}, u32[]{:S(2)}, u32[]{:S(2)}) collective-permute-start(bf16[1168,128]{1,0:T(8,128)(2,1)} %pad_maximum_fusion), channel_id=1, source_target_pairs={{0,1},{1,2},{2,3},{3,4},{4,5},{5,6},{6,7},{7,8},{8,9},{9,10},{10,1... | collective-permute-start | bytes 897032 | tf_op jit(solution)/shard_map/ppermute | solution.py:389
  23.8 5.3 %collective-permute-start.2 = (bf16[320,128]{1,0:T(8,128)(2,1)S(1)}, bf16[320,128]{1,0:T(8,128)(2,1)S(1)}, u32[]{:S(2)}, u32[]{:S(2)}) collective-permute-start(bf16[320,128]{1,0:T(8,128)(2,1)S(1)} %copy-done.2), channel_id=1, source_target_pairs={{0,24},{1,25},{2,26},{3,27},{4,28},{5,29},{6,30},{7,31},{8,0},{9,1... | collective-permute-start | bytes 245768 | tf_op jit(solution)/shard_map/ppermute | solution.py:380
  30.1 1.8 %collective-permute-done.2.refs_3_ = bf16[320,128]{1,0:T(8,128)(2,1)S(1)} collective-permute-done((bf16[320,128]{1,0:T(8,128)(2,1)S(1)}, bf16[320,128]{1,0:T(8,128)(2,1)S(1)}, u32[]{:S(2)}, u32[]{:S(2)}) %collective-permute-start.2) | collective-permute-done | bytes 81952 | tf_op jit(solution)/shard_map/ppermute | solution.py:380
  31.9 5.3 %collective-permute-done.1.refs_2_ = bf16[320,128]{1,0:T(8,128)(2,1)S(1)} collective-permute-done((bf16[320,128]{1,0:T(8,128)(2,1)S(1)}, bf16[320,128]{1,0:T(8,128)(2,1)S(1)}, u32[]{:S(2)}, u32[]{:S(2)}) %collective-permute-start.1) | collective-permute-done | bytes 81952 | tf_op jit(solution)/shard_map/ppermute | solution.py:380
  42.7 1.4 %collective-permute-start.5 = (bf16[480,128]{1,0:T(8,128)(2,1)S(1)}, bf16[480,128]{1,0:T(8,128)(2,1)S(1)}, u32[]{:S(2)}, u32[]{:S(2)}) collective-permute-start(bf16[480,128]{1,0:T(8,128)(2,1)S(1)} %get-tuple-element.36), channel_id=1, source_target_pairs={{0,3},{1,2},{2,1},{3,0},{4,7},{5,6},{6,5},{7,4},{8,11},{9,10},{10,... | collective-permute-start | bytes 368648 | tf_op jit(solution)/shard_map/ppermute | solution.py:408
  44.2 1.3 %collective-permute-start.6 = (bf16[480,128]{1,0:T(8,128)(2,1)S(1)}, bf16[480,128]{1,0:T(8,128)(2,1)S(1)}, u32[]{:S(2)}, u32[]{:S(2)}) collective-permute-start(bf16[480,128]{1,0:T(8,128)(2,1)S(1)} %get-tuple-element.37), channel_id=1, source_target_pairs={{0,4},{1,5},{2,6},{3,7},{4,0},{5,1},{6,2},{7,3},{8,12},{9,13},{10,... | collective-permute-start | bytes 368648 | tf_op jit(solution)/shard_map/ppermute | solution.py:408
  45.8 1.7 %collective-permute-start.8 = (bf16[480,128]{1,0:T(8,128)(2,1)S(1)}, bf16[480,128]{1,0:T(8,128)(2,1)S(1)}, u32[]{:S(2)}, u32[]{:S(2)}) collective-permute-start(bf16[480,128]{1,0:T(8,128)(2,1)S(1)} %get-tuple-element.39), channel_id=1, source_target_pairs={{0,6},{1,7},{2,4},{3,5},{4,2},{5,3},{6,0},{7,1},{8,14},{9,15},{10,... | collective-permute-start | bytes 368648 | tf_op jit(solution)/shard_map/ppermute | solution.py:408
  48.6 6.1 %first_layer.1 = (bf16[2688,256]{1,0:T(8,128)(2,1)S(1)}, bf16[2688,256]{1,0:T(8,128)(2,1)S(1)}, bf16[5376,128]{1,0:T(8,128)(2,1)}) custom-call(bf16[32,128,128]{2,1,0:T(8,128)(2,1)S(1)} %copy-done.1, bf16[1168,128]{1,0:T(8,128)(2,1)S(1)} %collective-permute-done.10.low.refs_15_, bf16[1168,128]{1,0:T(8,128)(2,1)S(1)} %collective-permute-done.11.high.refs_16_, ...), custom_call_target="tpu_custom_call" | custom-call | flops 4000000000 | bytes 8388608 | tf_op jit(solution)/shard_map/first_layer/pallas_call | solution.py:411
  54.7 1.1 %copy-done.16 = bf16[2688,256]{1,0:T(8,128)(2,1)} copy-done((bf16[2688,256]{1,0:T(8,128)(2,1)}, bf16[2688,256]{1,0:T(8,128)(2,1)S(1)}, u32[]{:S(2)}) %copy-start.16) | copy-done | bytes 1376280
  55.8 1.1 %copy-done.17 = bf16[2688,256]{1,0:T(8,128)(2,1)} copy-done((bf16[2688,256]{1,0:T(8,128)(2,1)}, bf16[2688,256]{1,0:T(8,128)(2,1)S(1)}, u32[]{:S(2)}) %copy-start.17) | copy-done | bytes 1376280
  57.7 20.7 %middle_layers.1 = (bf16[32,128,128]{2,1,0:T(8,128)(2,1)}, bf16[2176,256]{1,0:T(8,128)(2,1)}, f32[4352,128]{1,0:T(8,128)}, bf16[320,128]{1,0:T(8,128)(2,1)}) custom-call(bf16[480,128]{1,0:T(8,128)(2,1)} %copy-done.12, bf16[480,128]{1,0:T(8,128)(2,1)} %copy-done.21, bf16[480,128]{1,0:T(8,128)(2,1)} %copy-done.22, bf16[480,128]{1,0:T(8,128)(2,1)} %copy-done.23, ...), custom_call_target="tpu_custom_call" | custom-call | flops 12000000000 | bytes 16777216 | tf_op jit(solution)/shard_map/middle_layers/pallas_call | solution.py:420
  78.5 1.8 %collective-permute-start.18 = (bf16[320,128]{1,0:T(8,128)(2,1)}, bf16[320,128]{1,0:T(8,128)(2,1)S(1)}, u32[]{:S(2)}, u32[]{:S(2)}) collective-permute-start(bf16[320,128]{1,0:T(8,128)(2,1)} %get-tuple-element.54.refs_0_), channel_id=1, source_target_pairs={{0,7},{1,6},{2,5},{3,4},{4,3},{5,2},{6,1},{7,0},{8,15},{9,14},{10,... | collective-permute-start | bytes 245768 | tf_op jit(solution)/shard_map/ppermute | solution.py:459
  80.2 1.3 %collective-permute-start.17 = (bf16[320,128]{1,0:T(8,128)(2,1)}, bf16[320,128]{1,0:T(8,128)(2,1)S(1)}, u32[]{:S(2)}, u32[]{:S(2)}) collective-permute-start(bf16[320,128]{1,0:T(8,128)(2,1)} %get-tuple-element.54.refs_0_), channel_id=1, source_target_pairs={{0,6},{1,7},{2,4},{3,5},{4,2},{5,3},{6,0},{7,1},{8,14},{9,15},{10,... | collective-permute-start | bytes 245768 | tf_op jit(solution)/shard_map/ppermute | solution.py:459
  83.8 1.2 %collective-permute-start.13 = (bf16[320,128]{1,0:T(8,128)(2,1)}, bf16[320,128]{1,0:T(8,128)(2,1)S(1)}, u32[]{:S(2)}, u32[]{:S(2)}) collective-permute-start(bf16[320,128]{1,0:T(8,128)(2,1)} %get-tuple-element.54.refs_0_), channel_id=1, source_target_pairs={{0,2},{1,3},{2,0},{3,1},{4,6},{5,7},{6,4},{7,5},{8,10},{9,11},{10,... | collective-permute-start | bytes 245768 | tf_op jit(solution)/shard_map/ppermute | solution.py:459
  85.0 1.2 %collective-permute-done.17.refs_6_ = bf16[320,128]{1,0:T(8,128)(2,1)S(1)} collective-permute-done((bf16[320,128]{1,0:T(8,128)(2,1)}, bf16[320,128]{1,0:T(8,128)(2,1)S(1)}, u32[]{:S(2)}, u32[]{:S(2)}) %collective-permute-start.17) | collective-permute-done | bytes 81952 | tf_op jit(solution)/shard_map/ppermute | solution.py:459
  86.2 1.6 %collective-permute-done.16.refs_5_ = bf16[320,128]{1,0:T(8,128)(2,1)S(1)} collective-permute-done((bf16[320,128]{1,0:T(8,128)(2,1)}, bf16[320,128]{1,0:T(8,128)(2,1)S(1)}, u32[]{:S(2)}, u32[]{:S(2)}) %collective-permute-start.16) | collective-permute-done | bytes 81952 | tf_op jit(solution)/shard_map/ppermute | solution.py:459
  87.9 1.7 %collective-permute-done.15.refs_4_ = bf16[320,128]{1,0:T(8,128)(2,1)S(1)} collective-permute-done((bf16[320,128]{1,0:T(8,128)(2,1)}, bf16[320,128]{1,0:T(8,128)(2,1)S(1)}, u32[]{:S(2)}, u32[]{:S(2)}) %collective-permute-start.15) | collective-permute-done | bytes 81952 | tf_op jit(solution)/shard_map/ppermute | solution.py:459
  91.5 4.3 %collective-permute-start.19 = (bf16[320,128]{1,0:T(8,128)(2,1)S(1)}, bf16[320,128]{1,0:T(8,128)(2,1)S(1)}, u32[]{:S(2)}, u32[]{:S(2)}) collective-permute-start(bf16[320,128]{1,0:T(8,128)(2,1)S(1)} %get-tuple-element.56), channel_id=1, source_target_pairs={{0,24},{1,25},{2,26},{3,27},{4,28},{5,29},{6,30},{7,31},{8,0},{9,1... | collective-permute-start | bytes 245768 | tf_op jit(solution)/shard_map/ppermute | solution.py:477
  95.8 2.0 %collective-permute-start.21 = (bf16[320,128]{1,0:T(8,128)(2,1)S(1)}, bf16[320,128]{1,0:T(8,128)(2,1)S(1)}, u32[]{:S(2)}, u32[]{:S(2)}) collective-permute-start(bf16[320,128]{1,0:T(8,128)(2,1)S(1)} %get-tuple-element.58), channel_id=1, source_target_pairs={{0,8},{1,9},{2,10},{3,11},{4,12},{5,13},{6,14},{7,15},{8,16},{9,17... | collective-permute-start | bytes 245768 | tf_op jit(solution)/shard_map/ppermute | solution.py:477
  97.8 1.6 %copy-done.14 = f32[4352,128]{1,0:T(8,128)S(1)} copy-done((f32[4352,128]{1,0:T(8,128)S(1)}, f32[4352,128]{1,0:T(8,128)}, u32[]{:S(2)}) %copy-start.14) | copy-done | bytes 2228248
  99.5 1.2 %copy-done.15 = bf16[2176,256]{1,0:T(8,128)(2,1)S(1)} copy-done((bf16[2176,256]{1,0:T(8,128)(2,1)S(1)}, bf16[2176,256]{1,0:T(8,128)(2,1)}, u32[]{:S(2)}) %copy-start.15) | copy-done | bytes 1114136
  100.7 3.9 %last_adjoint.1 = bf16[32,128,128]{2,1,0:T(8,128)(2,1)} custom-call(bf16[2176,256]{1,0:T(8,128)(2,1)S(1)} %copy-done.15, f32[4352,128]{1,0:T(8,128)S(1)} %copy-done.14, bf16[1536,256]{1,0:T(8,128)(2,1)S(1)} %get-tuple-element.52.weight), custom_call_target="tpu_custom_call" | custom-call | flops 3000000000 | bytes 6291456 | tf_op jit(solution)/shard_map/last_adjoint/pallas_call | solution.py:461
  105.3 1.8 %total.1 = f32[32,10,128]{2,1,0:T(8,128)} custom-call(bf16[320,128]{1,0:T(8,128)(2,1)} %copy-done.3, bf16[320,128]{1,0:T(8,128)(2,1)} %copy-done.18, bf16[320,128]{1,0:T(8,128)(2,1)} %copy-done.19, bf16[320,128]{1,0:T(8,128)(2,1)} %copy-done.20), custom_call_target="tpu_custom_call" | custom-call | tf_op jit(solution)/shard_map/total/pallas_call | solution.py:478
  107.1 1.7 %copy.20 = f32[4,8,10,128]{3,1,2,0:T(8,128)} copy(f32[4,8,10,128]{3,2,1,0:T(8,128)} %bitcast.5) | data formatting | bytes 327680
  (90 shorter events, 16.4 us)
Async XLA Ops:
  0.6 18.0 %copy-start.1 = (bf16[32,128,128]{2,1,0:T(8,128)(2,1)S(1)}, bf16[32,128,128]{2,1,0:T(8,128)(2,1)}, u32[]{:S(2)}) copy-start(bf16[32,128,128]{2,1,0:T(8,128)(2,1)} %ice.1) | copy-start | bytes 3145732
  9.5 14.3 %copy-start.2 = (bf16[320,128]{1,0:T(8,128)(2,1)S(1)}, bf16[320,128]{1,0:T(8,128)(2,1)}, u32[]{:S(2)}) copy-start(bf16[320,128]{1,0:T(8,128)(2,1)} %get-tuple-element.32.refs_0_) | copy-start | bytes 245764
  9.5 27.6 %all-to-all-start = ((f32[32,8,128]{2,1,0:T(8,128)}), f32[32,8,128]{2,1,0:T(8,128)S(1)}, u32[]{:S(2)}, u32[]{:S(2)}) async-start(f32[32,8,128]{2,1,0:T(8,128)} %get-tuple-element.31), calls=%async_computation | async-start | bytes 262144 | tf_op jit(solution)/shard_map/all_to_all | solution.py:381
  17.5 21.8 %copy-start = (bf16[3,3,3,128,128]{4,3,2,1,0:T(8,128)(2,1)S(1)}, bf16[3,3,3,128,128]{4,3,2,1,0:T(8,128)(2,1)}, u32[]{:S(2)}) copy-start(bf16[3,3,3,128,128]{4,3,2,1,0:T(8,128)(2,1)} %weight.2) | copy-start | bytes 2654212
  18.6 29.9 %copy-start.5 = (s32[32,128]{1,0:T(8,128)S(1)}, s32[32,128]{1,0:T(8,128)}, u32[]{:S(2)}) copy-start(s32[32,128]{1,0:T(8,128)} %mask.1) | copy-start | bytes 49156
  18.6 29.9 %copy-start.13 = (f32[3,128]{1,0:T(4,128)S(1)}, f32[3,128]{1,0:T(4,128)}, u32[]{:S(2)}) copy-start(f32[3,128]{1,0:T(4,128)} %refs_10_.1) | copy-start | bytes 4612
  18.7 25.5 %collective-permute-start.11 = (bf16[1168,128]{1,0:T(8,128)(2,1)S(1)}, bf16[1168,128]{1,0:T(8,128)(2,1)S(1)}, u32[]{:S(2)}, u32[]{:S(2)}) collective-permute-start(bf16[1168,128]{1,0:T(8,128)(2,1)S(1)} %pad_maximum_fusion.1), channel_id=1, source_target_pairs={{1,0},{2,1},{3,2},{4,3},{5,4},{6,5},{7,6},{8,7},{9,8},{10,9},{11,1... | collective-permute-start | bytes 897032 | tf_op jit(solution)/shard_map/ppermute | solution.py:390
  20.7 24.7 %collective-permute-start.10 = (bf16[1168,128]{1,0:T(8,128)(2,1)}, bf16[1168,128]{1,0:T(8,128)(2,1)S(1)}, u32[]{:S(2)}, u32[]{:S(2)}) collective-permute-start(bf16[1168,128]{1,0:T(8,128)(2,1)} %pad_maximum_fusion), channel_id=1, source_target_pairs={{0,1},{1,2},{2,3},{3,4},{4,5},{5,6},{6,7},{7,8},{8,9},{9,10},{10,1... | collective-permute-start | bytes 897032 | tf_op jit(solution)/shard_map/ppermute | solution.py:389
  23.8 8.1 %collective-permute-start.2 = (bf16[320,128]{1,0:T(8,128)(2,1)S(1)}, bf16[320,128]{1,0:T(8,128)(2,1)S(1)}, u32[]{:S(2)}, u32[]{:S(2)}) collective-permute-start(bf16[320,128]{1,0:T(8,128)(2,1)S(1)} %copy-done.2), channel_id=1, source_target_pairs={{0,24},{1,25},{2,26},{3,27},{4,28},{5,29},{6,30},{7,31},{8,0},{9,1... | collective-permute-start | bytes 245768 | tf_op jit(solution)/shard_map/ppermute | solution.py:380
  29.0 8.1 %collective-permute-start.1 = (bf16[320,128]{1,0:T(8,128)(2,1)S(1)}, bf16[320,128]{1,0:T(8,128)(2,1)S(1)}, u32[]{:S(2)}, u32[]{:S(2)}) collective-permute-start(bf16[320,128]{1,0:T(8,128)(2,1)S(1)} %copy-done.2), channel_id=1, source_target_pairs={{0,16},{1,17},{2,18},{3,19},{4,20},{5,21},{6,22},{7,23},{8,24},{9,... | collective-permute-start | bytes 245768 | tf_op jit(solution)/shard_map/ppermute | solution.py:380
  29.0 8.1 %collective-permute-start = (bf16[320,128]{1,0:T(8,128)(2,1)S(1)}, bf16[320,128]{1,0:T(8,128)(2,1)S(1)}, u32[]{:S(2)}, u32[]{:S(2)}) collective-permute-start(bf16[320,128]{1,0:T(8,128)(2,1)S(1)} %copy-done.2), channel_id=1, source_target_pairs={{0,8},{1,9},{2,10},{3,11},{4,12},{5,13},{6,14},{7,15},{8,16},{9,17... | collective-permute-start | bytes 245768 | tf_op jit(solution)/shard_map/ppermute | solution.py:380
  38.9 6.9 %collective-permute-start.3 = (bf16[480,128]{1,0:T(8,128)(2,1)S(1)}, bf16[480,128]{1,0:T(8,128)(2,1)S(1)}, u32[]{:S(2)}, u32[]{:S(2)}) collective-permute-start(bf16[480,128]{1,0:T(8,128)(2,1)S(1)} %get-tuple-element.34), channel_id=1, source_target_pairs={{0,1},{1,0},{2,3},{3,2},{4,5},{5,4},{6,7},{7,6},{8,9},{9,8},{10,11... | collective-permute-start | bytes 368648 | tf_op jit(solution)/shard_map/ppermute | solution.py:408
  38.9 8.6 %collective-permute-start.4 = (bf16[480,128]{1,0:T(8,128)(2,1)S(1)}, bf16[480,128]{1,0:T(8,128)(2,1)S(1)}, u32[]{:S(2)}, u32[]{:S(2)}) collective-permute-start(bf16[480,128]{1,0:T(8,128)(2,1)S(1)} %get-tuple-element.35), channel_id=1, source_target_pairs={{0,2},{1,3},{2,0},{3,1},{4,6},{5,7},{6,4},{7,5},{8,10},{9,11},{10,... | collective-permute-start | bytes 368648 | tf_op jit(solution)/shard_map/ppermute | solution.py:408
  42.7 11.9 %copy-start.9 = (bf16[1536,256]{1,0:T(8,128)(2,1)}, bf16[1536,256]{1,0:T(8,128)(2,1)S(1)}, u32[]{:S(2)}) copy-start(bf16[1536,256]{1,0:T(8,128)(2,1)S(1)} %get-tuple-element.47.refs_19_) | copy-start | bytes 2359300
  42.7 14.1 %collective-permute-start.5 = (bf16[480,128]{1,0:T(8,128)(2,1)S(1)}, bf16[480,128]{1,0:T(8,128)(2,1)S(1)}, u32[]{:S(2)}, u32[]{:S(2)}) collective-permute-start(bf16[480,128]{1,0:T(8,128)(2,1)S(1)} %get-tuple-element.36), channel_id=1, source_target_pairs={{0,3},{1,2},{2,1},{3,0},{4,7},{5,6},{6,5},{7,4},{8,11},{9,10},{10,... | collective-permute-start | bytes 368648 | tf_op jit(solution)/shard_map/ppermute | solution.py:408
  44.2 10.5 %copy-start.10 = (bf16[1168,128]{1,0:T(8,128)(2,1)}, bf16[1168,128]{1,0:T(8,128)(2,1)S(1)}, u32[]{:S(2)}) copy-start(bf16[1168,128]{1,0:T(8,128)(2,1)S(1)} %collective-permute-done.11.high.refs_16_) | copy-start | bytes 897028
  44.2 12.7 %collective-permute-start.6 = (bf16[480,128]{1,0:T(8,128)(2,1)S(1)}, bf16[480,128]{1,0:T(8,128)(2,1)S(1)}, u32[]{:S(2)}, u32[]{:S(2)}) collective-permute-start(bf16[480,128]{1,0:T(8,128)(2,1)S(1)} %get-tuple-element.37), channel_id=1, source_target_pairs={{0,4},{1,5},{2,6},{3,7},{4,0},{5,1},{6,2},{7,3},{8,12},{9,13},{10,... | collective-permute-start | bytes 368648 | tf_op jit(solution)/shard_map/ppermute | solution.py:408
  45.4 9.2 %copy-start.11 = (bf16[1168,128]{1,0:T(8,128)(2,1)}, bf16[1168,128]{1,0:T(8,128)(2,1)S(1)}, u32[]{:S(2)}) copy-start(bf16[1168,128]{1,0:T(8,128)(2,1)S(1)} %collective-permute-done.10.low.refs_15_) | copy-start | bytes 897028
  45.4 11.5 %collective-permute-start.7 = (bf16[480,128]{1,0:T(8,128)(2,1)S(1)}, bf16[480,128]{1,0:T(8,128)(2,1)S(1)}, u32[]{:S(2)}, u32[]{:S(2)}) collective-permute-start(bf16[480,128]{1,0:T(8,128)(2,1)S(1)} %get-tuple-element.38), channel_id=1, source_target_pairs={{0,5},{1,4},{2,7},{3,6},{4,1},{5,0},{6,3},{7,2},{8,13},{9,12},{10,... | collective-permute-start | bytes 368648 | tf_op jit(solution)/shard_map/ppermute | solution.py:408
  45.8 8.8 %copy-start.21 = (bf16[480,128]{1,0:T(8,128)(2,1)}, bf16[480,128]{1,0:T(8,128)(2,1)S(1)}, u32[]{:S(2)}) copy-start(bf16[480,128]{1,0:T(8,128)(2,1)S(1)} %collective-permute-done.3.refs_1_) | copy-start | bytes 368644
  45.8 11.1 %collective-permute-start.8 = (bf16[480,128]{1,0:T(8,128)(2,1)S(1)}, bf16[480,128]{1,0:T(8,128)(2,1)S(1)}, u32[]{:S(2)}, u32[]{:S(2)}) collective-permute-start(bf16[480,128]{1,0:T(8,128)(2,1)S(1)} %get-tuple-element.39), channel_id=1, source_target_pairs={{0,6},{1,7},{2,4},{3,5},{4,2},{5,3},{6,0},{7,1},{8,14},{9,15},{10,... | collective-permute-start | bytes 368648 | tf_op jit(solution)/shard_map/ppermute | solution.py:408
  47.5 9.4 %collective-permute-start.9 = (bf16[480,128]{1,0:T(8,128)(2,1)S(1)}, bf16[480,128]{1,0:T(8,128)(2,1)S(1)}, u32[]{:S(2)}, u32[]{:S(2)}) collective-permute-start(bf16[480,128]{1,0:T(8,128)(2,1)S(1)} %get-tuple-element.40), channel_id=1, source_target_pairs={{0,7},{1,6},{2,5},{3,4},{4,3},{5,2},{6,1},{7,0},{8,15},{9,14},{10,... | collective-permute-start | bytes 368648 | tf_op jit(solution)/shard_map/ppermute | solution.py:408
  78.5 5.3 %collective-permute-start.18 = (bf16[320,128]{1,0:T(8,128)(2,1)}, bf16[320,128]{1,0:T(8,128)(2,1)S(1)}, u32[]{:S(2)}, u32[]{:S(2)}) collective-permute-start(bf16[320,128]{1,0:T(8,128)(2,1)} %get-tuple-element.54.refs_0_), channel_id=1, source_target_pairs={{0,7},{1,6},{2,5},{3,4},{4,3},{5,2},{6,1},{7,0},{8,15},{9,14},{10,... | collective-permute-start | bytes 245768 | tf_op jit(solution)/shard_map/ppermute | solution.py:459
  80.2 6.0 %collective-permute-start.17 = (bf16[320,128]{1,0:T(8,128)(2,1)}, bf16[320,128]{1,0:T(8,128)(2,1)S(1)}, u32[]{:S(2)}, u32[]{:S(2)}) collective-permute-start(bf16[320,128]{1,0:T(8,128)(2,1)} %get-tuple-element.54.refs_0_), channel_id=1, source_target_pairs={{0,6},{1,7},{2,4},{3,5},{4,2},{5,3},{6,0},{7,1},{8,14},{9,15},{10,... | collective-permute-start | bytes 245768 | tf_op jit(solution)/shard_map/ppermute | solution.py:459
  81.5 6.4 %collective-permute-start.16 = (bf16[320,128]{1,0:T(8,128)(2,1)}, bf16[320,128]{1,0:T(8,128)(2,1)S(1)}, u32[]{:S(2)}, u32[]{:S(2)}) collective-permute-start(bf16[320,128]{1,0:T(8,128)(2,1)} %get-tuple-element.54.refs_0_), channel_id=1, source_target_pairs={{0,5},{1,4},{2,7},{3,6},{4,1},{5,0},{6,3},{7,2},{8,13},{9,12},{10,... | collective-permute-start | bytes 245768 | tf_op jit(solution)/shard_map/ppermute | solution.py:459
  82.2 7.4 %collective-permute-start.15 = (bf16[320,128]{1,0:T(8,128)(2,1)}, bf16[320,128]{1,0:T(8,128)(2,1)S(1)}, u32[]{:S(2)}, u32[]{:S(2)}) collective-permute-start(bf16[320,128]{1,0:T(8,128)(2,1)} %get-tuple-element.54.refs_0_), channel_id=1, source_target_pairs={{0,4},{1,5},{2,6},{3,7},{4,0},{5,1},{6,2},{7,3},{8,12},{9,13},{10,... | collective-permute-start | bytes 245768 | tf_op jit(solution)/shard_map/ppermute | solution.py:459
  82.9 6.7 %collective-permute-start.14 = (bf16[320,128]{1,0:T(8,128)(2,1)}, bf16[320,128]{1,0:T(8,128)(2,1)S(1)}, u32[]{:S(2)}, u32[]{:S(2)}) collective-permute-start(bf16[320,128]{1,0:T(8,128)(2,1)} %get-tuple-element.54.refs_0_), channel_id=1, source_target_pairs={{0,3},{1,2},{2,1},{3,0},{4,7},{5,6},{6,5},{7,4},{8,11},{9,10},{10,... | collective-permute-start | bytes 245768 | tf_op jit(solution)/shard_map/ppermute | solution.py:459
  83.8 5.8 %collective-permute-start.13 = (bf16[320,128]{1,0:T(8,128)(2,1)}, bf16[320,128]{1,0:T(8,128)(2,1)S(1)}, u32[]{:S(2)}, u32[]{:S(2)}) collective-permute-start(bf16[320,128]{1,0:T(8,128)(2,1)} %get-tuple-element.54.refs_0_), channel_id=1, source_target_pairs={{0,2},{1,3},{2,0},{3,1},{4,6},{5,7},{6,4},{7,5},{8,10},{9,11},{10,... | collective-permute-start | bytes 245768 | tf_op jit(solution)/shard_map/ppermute | solution.py:459
  86.2 3.4 %collective-permute-start.12 = (bf16[320,128]{1,0:T(8,128)(2,1)}, bf16[320,128]{1,0:T(8,128)(2,1)S(1)}, u32[]{:S(2)}, u32[]{:S(2)}) collective-permute-start(bf16[320,128]{1,0:T(8,128)(2,1)} %get-tuple-element.54.refs_0_), channel_id=1, source_target_pairs={{0,1},{1,0},{2,3},{3,2},{4,5},{5,4},{6,7},{7,6},{8,9},{9,8},{10,11... | collective-permute-start | bytes 245768 | tf_op jit(solution)/shard_map/ppermute | solution.py:459
  91.5 13.0 %collective-permute-start.19 = (bf16[320,128]{1,0:T(8,128)(2,1)S(1)}, bf16[320,128]{1,0:T(8,128)(2,1)S(1)}, u32[]{:S(2)}, u32[]{:S(2)}) collective-permute-start(bf16[320,128]{1,0:T(8,128)(2,1)S(1)} %get-tuple-element.56), channel_id=1, source_target_pairs={{0,24},{1,25},{2,26},{3,27},{4,28},{5,29},{6,30},{7,31},{8,0},{9,1... | collective-permute-start | bytes 245768 | tf_op jit(solution)/shard_map/ppermute | solution.py:477
  95.8 8.8 %collective-permute-start.20 = (bf16[320,128]{1,0:T(8,128)(2,1)S(1)}, bf16[320,128]{1,0:T(8,128)(2,1)S(1)}, u32[]{:S(2)}, u32[]{:S(2)}) collective-permute-start(bf16[320,128]{1,0:T(8,128)(2,1)S(1)} %get-tuple-element.57), channel_id=1, source_target_pairs={{0,16},{1,17},{2,18},{3,19},{4,20},{5,21},{6,22},{7,23},{8,24},{9,... | collective-permute-start | bytes 245768 | tf_op jit(solution)/shard_map/ppermute | solution.py:477
  95.8 8.8 %collective-permute-start.21 = (bf16[320,128]{1,0:T(8,128)(2,1)S(1)}, bf16[320,128]{1,0:T(8,128)(2,1)S(1)}, u32[]{:S(2)}, u32[]{:S(2)}) collective-permute-start(bf16[320,128]{1,0:T(8,128)(2,1)S(1)} %get-tuple-element.58), channel_id=1, source_target_pairs={{0,8},{1,9},{2,10},{3,11},{4,12},{5,13},{6,14},{7,15},{8,16},{9,17... | collective-permute-start | bytes 245768 | tf_op jit(solution)/shard_map/ppermute | solution.py:477
  (19 other events, 22.7 us)
where the time goes:
time: 109 us
  starting transfers between devices  36.7 us (34%)
  Pallas kernels  36.4 us (33%)
  local copies, waits for them, and re-layouts  21.3 us (20%)
  waiting for transfers between devices  12 us (11%)
  other arithmetic  1.48 us (1%)
    pallas_call x1, Pallas kernels, body(): pl.pallas_call(main_kernel, out_shape=(shape(ROWS, C, C), shape(17 * C, P...  20.7 us
    unnamed x62, local copies, waits for them, and re-layouts  20.2 us
    all_to_all x1, starting transfers between devices, body(): table = lax.all_to_all(table, 'tile', 0, 0, tiled=True)  7.3 us
    ppermute x3, waiting for transfers between devices, body(): lax.ppermute(fields, 'tile', by_plane(z))  7.02 us
    ppermute x3, starting transfers between devices, body(): lax.ppermute(fields, 'tile', by_plane(z))  6.35 us
    ppermute x3, starting transfers between devices, body(): lax.ppermute(sums[z], 'tile', by_plane(-z))  6.3 us
    ppermute x7, starting transfers between devices, body(): lax.ppermute(messages[s], 'tile', by_mate(s))  6.25 us
    ppermute x7, starting transfers between devices, body(): lax.ppermute(project, 'tile', by_mate(s))  6.18 us
  transfers between devices with their start and end apart: 23, of which 6 were waited for; matrix products, arithmetic and copies ran while one was open for 2% of the time, Pallas kernels for 11%

commit v1 on v0

v1 whole, which is shorter than its diff:
```python
import functools

import jax
import jax.numpy as jnp
from jax import lax
from jax.experimental import pallas as pl
from jax.experimental.pallas import tpu as pltpu
from jax.sharding import PartitionSpec as P

F = 10
FP = 16
K = 4
C = 128
ROWS = 32
EXT = 48
PAD = 8
GROUP = 8
SENT = GROUP // 2
PAIR = 2 * C
TAPS = 3 * C
BF = jnp.bfloat16
F32 = jnp.float32
MIB = 1 << 20


def params(mib):
    return pltpu.CompilerParams(vmem_limit_bytes=mib * MIB)


def dot(a, b, dims=(((1,), (0,)), ((), ()))):
    return lax.dot_general(a, b, dims, preferred_element_type=F32)


def split(x):
    high = x.astype(BF)
    return high, (x - high.astype(F32)).astype(BF)


def fine_dot(a, b, dims=(((1,), (0,)), ((), ()))):
    ah, al = split(a)
    bh, bl = split(b)
    return dot(ah, bh, dims) + (dot(ah, bl, dims) + dot(al, bh, dims))


def pair_rows(index, count=1):
    start = index * C
    if not isinstance(index, int):
        start = pl.multiple_of(start, C)
    return pl.ds(start, count * C)


def store_pair(xp, index, value):
    column = lax.broadcasted_iota(jnp.int32, (C, PAIR), 0)
    before = jnp.where(column == 0, 0.0, pltpu.roll(value, 1, 0)).astype(BF)
    after = jnp.where(column == C - 1, 0.0, pltpu.roll(value, C - 1, 0)).astype(BF)
    value = value.astype(BF)
    rows = pair_rows(index)
    for half in range(2):
        lanes = slice(half * C, half * C + C)
        for tap, part in enumerate((before, value, after)):
            start = half * TAPS + tap * C
            xp[rows, start : start + C] = part[:, lanes]


def centre(xp, index):
    low = xp[pair_rows(index), TAPS + C : TAPS + 2 * C]
    high = xp[pair_rows(index + 1), C : 2 * C]
    return jnp.concatenate([low, high], axis=1).astype(F32)


def two_rows(ref, row):
    start = row * C
    if not isinstance(row, int):
        start = pl.multiple_of(start, C)
    low = ref[pl.ds(start, C), :]
    high = ref[pl.ds(start + C, C), :]
    return jnp.concatenate([low, high], axis=1).astype(F32)


def layer(xp, weight, count, step, finish):
    for first in range(0, count, step):
        size = min(step, count - first)
        total = dot(xp[pair_rows(first, size), :], weight[: 2 * TAPS, :])
        total += dot(xp[pair_rows(first + 1, size), :], weight[2 * TAPS :, :])
        for j in range(size):
            finish(first + j, total[j * C : (j + 1) * C])


def by_field(value, field):
    panels = value.shape[0] // (F * 8)
    part = value.reshape(panels, F, 8, C)[:, field]
    return part.reshape(panels * 8, C)


def column_tables(table, devices):
    entries = [table[jnp.clip(device, 0, table.shape[0] - 1)] for device in devices]
    fill = jnp.zeros((C - 2 * K * len(entries), C), F32)
    return jnp.concatenate(entries + [fill], axis=0).T


def picked(columns, place, ident, start, size):
    total = jnp.zeros((size, ident.shape[1]), F32)
    part = columns[start : start + size]
    for k in range(K):
        at = place * 2 * K + k
        total += jnp.where(part[:, at : at + 1] == ident, part[:, at + K : at + K + 1], 0.0)
    return total


def source_ident(planes, plane, spot, sides):
    lane = lax.broadcasted_iota(jnp.int32, (1, sides * planes * ROWS), 1)
    from_plane = lax.rem(plane - (lane // ROWS) % planes + planes, planes)
    from_spot = jnp.where(lane < planes * ROWS, spot, spot ^ 1)
    return ((from_plane * GROUP + from_spot) * ROWS + lane % ROWS).astype(F32)


def pick_kernel(planes, table, picks, scatter):
    me = lax.axis_index("tile")
    plane, spot = me // GROUP, me % GROUP
    count = planes * GROUP
    ident = source_ident(planes, plane, spot, 2)
    devices = [plane * GROUP + (spot ^ s) + step for s in range(0, GROUP, 2) for step in (-1, 0, 1)]
    columns = column_tables(table, devices)
    parts = []
    for place, device in enumerate(devices):
        start, size = ((ROWS - PAD, PAD), (0, ROWS), (0, PAD))[place % 3]
        inside = jnp.logical_and(device >= 0, device < count)
        parts.append(jnp.where(inside, picked(columns, place, ident, start, size), 0.0))
    picks[...] = jnp.concatenate(parts, axis=0).astype(BF)
    ident = source_ident(planes, plane, spot, 1)
    columns = column_tables(table, [plane * GROUP + (spot ^ s) for s in range(GROUP)])
    parts = [picked(columns, s, ident, 0, ROWS) for s in range(GROUP)]
    scatter[...] = jnp.concatenate(parts, axis=0).T.astype(BF)


def message_kernel(planes, picks, own, mate, *refs):
    outs, wide = refs[:-1], refs[-1]
    sources = planes * ROWS
    for side, block in enumerate((own, mate)):
        value = block[...].astype(F32)
        for f in range(F):
            wide[side * sources : (side + 1) * sources, f * C : (f + 1) * C] = by_field(
                value, f
            ).astype(BF)
    for f in range(F):
        found = dot(picks[...], wide[:, f * C : (f + 1) * C]).astype(BF)
        for n, out in enumerate(outs):
            out[f * EXT : (f + 1) * EXT, :] = found[n * EXT : (n + 1) * EXT]


def fill_taps(taps, weight, l, back):
    zero = jnp.zeros((TAPS, C), BF)
    taps[0:TAPS, C:] = zero
    taps[3 * TAPS :, :C] = zero
    for a in range(3):
        for b in range(3):
            if back:
                block = weight[l, 2 - a, 2 - b].astype(F32).T.astype(BF)
            else:
                block = weight[l, a, b]
            for half in range(2):
                start = (a + half) * TAPS + b * C
                taps[start : start + C, half * C : half * C + C] = block


def first_kernel(ice, low, high, mask, weight, bias, hidden, slope, ocean, xp, taps):
    fill_taps(taps, weight, 0, False)

    def ice_row(r):
        if r < 0:
            return low[r + 6]
        if r >= ROWS:
            return high[r - ROWS]
        return ice[r]

    for p in range(22):
        row = 2 * p - 6
        store_pair(xp, p, jnp.concatenate([ice_row(row), ice_row(row + 1)], axis=1).astype(F32))
    before = low[9, 0:ROWS, :].astype(F32)[ROWS - PAD :]
    after = high[9, 0:ROWS, :].astype(F32)[:PAD]
    cells = jnp.concatenate([before, mask[...].astype(F32), after], axis=0)
    cells = jnp.concatenate([cells, jnp.zeros((C - EXT, C), F32)], axis=0).T
    for r in range(-5, 37):
        column = jnp.broadcast_to(cells[:, r + PAD : r + PAD + 1], (C, C))
        ocean[(r + 5) * C : (r + 6) * C, :] = column.astype(BF)
    both = jnp.concatenate([bias[0:1, :], bias[0:1, :]], axis=1)

    def finish(p, total):
        tangent = jnp.tanh(total + both)
        cell = two_rows(ocean, 2 * p)
        moved = cell * tangent
        slope[pair_rows(p), :] = (cell - moved * tangent).astype(BF)
        hidden[pair_rows(p), :] = (centre(xp, p) + moved).astype(BF)

    layer(xp, taps, 21, 4, finish)


def main_kernel(*refs):
    messages = refs[:SENT]
    (col_map, lift, bias, hidden, slope0, ocean, sens, low, high, weight) = refs[SENT : SENT + 10]
    imitated, act0, grad1, project = refs[SENT + 10 : SENT + 14]
    ice, lifted, diag, xa, xb, slope1, slope2, grads, out_rows, turned, *taps = refs[SENT + 14 :]
    w1f, w2f, w2b, w1b = taps
    for n, (l, back) in enumerate(((1, False), (2, False), (2, True), (1, True))):
        fill_taps(taps[n], weight, l, back)
    ice[...] = jnp.zeros(ice.shape, F32)
    for f in range(F):
        rows = slice(f * EXT, (f + 1) * EXT)
        total = messages[0][rows, :].astype(F32)
        for s in range(1, SENT):
            total += messages[s][rows, :].astype(F32)
        ice[:, f, :] = fine_dot(total, col_map[...])
    diag[...] = jnp.zeros(diag.shape, BF)
    for j in range(GROUP):
        diag[j * FP : j * FP + F, j * C : (j + 1) * C] = lift[...]
    for group in range(EXT // GROUP):
        block = ice[group * GROUP : (group + 1) * GROUP].reshape(C, C)
        turned[group * C : (group + 1) * C, :] = block.T.astype(BF)
    for group in range(EXT // GROUP):
        lifted[group * C : (group + 1) * C, :] = dot(
            turned[group * C : (group + 1) * C, :], diag[...]
        )

    def lifted_row(r):
        e = r + PAD
        return lifted[(e // 8) * C : (e // 8 + 1) * C, (e % 8) * C : (e % 8 + 1) * C]

    for p in range(21):
        row = 2 * p - 5
        add = jnp.concatenate([lifted_row(row), lifted_row(row + 1)], axis=1)
        value = (hidden[pair_rows(p), :].astype(F32) + add).astype(BF)
        store_pair(xa, p, value.astype(F32))

    def bias_of(l):
        return jnp.concatenate([bias[l : l + 1, :], bias[l : l + 1, :]], axis=1)

    bias1, bias2 = bias_of(1), bias_of(2)

    def finish1(p, total):
        tangent = jnp.tanh(total + bias1)
        cell = two_rows(ocean, 2 * p + 1)
        moved = cell * tangent
        slope1[pair_rows(p), :] = (cell - moved * tangent).astype(BF)
        value = (centre(xa, p) + moved).astype(BF)
        store_pair(xb, p, value.astype(F32))

    layer(xa, w1f, 20, 4, finish1)

    def finish2(p, total):
        tangent = jnp.tanh(total + bias2)
        cell = two_rows(ocean, 2 * p + 2)
        moved = cell * tangent
        slope2[pair_rows(p), :] = (cell - moved * tangent).astype(BF)
        value = (centre(xb, p) + moved).astype(BF)
        out_rows[pair_rows(2 * p), :] = value[:, :C]
        out_rows[pair_rows(2 * p + 1), :] = value[:, C:]

    layer(xb, w2f, 19, 4, finish2)
    imitated[...] = out_rows[3 * C : 35 * C, :].reshape(ROWS, C, C)

    def sens_row(r):
        if r < 0:
            return low[r + 9]
        if r >= ROWS:
            return high[r - ROWS + 6]
        return sens[r]

    for p in range(19):
        row = 2 * p - 3
        value = jnp.concatenate([sens_row(row), sens_row(row + 1)], axis=1).astype(F32)
        store_pair(xa, p, value * slope2[pair_rows(p), :].astype(F32))
        out_rows[pair_rows(2 * p), :] = sens_row(row)
        out_rows[pair_rows(2 * p + 1), :] = sens_row(row + 1)

    def finish3(p, total):
        total += two_rows(out_rows, 2 * p + 1)
        grads[pair_rows(2 * p), :] = total[:, :C]
        grads[pair_rows(2 * p + 1), :] = total[:, C:]
        store_pair(xb, p, total * slope1[pair_rows(p + 1), :].astype(F32))

    layer(xa, w2b, 18, 4, finish3)

    def finish4(p, total):
        total += two_rows(grads, 2 * p + 1)
        act0[pair_rows(p), :] = (total * slope0[pair_rows(p + 2), :].astype(F32)).astype(BF)
        grad1[pair_rows(2 * p), :] = total[:, :C]
        grad1[pair_rows(2 * p + 1), :] = total[:, C:]

    layer(xb, w1b, 17, 4, finish4)
    short = jnp.concatenate([lift[...].astype(F32), jnp.zeros((FP - F, C), F32)], axis=0).astype(BF)
    nt = (((1,), (1,)), ((), ()))
    for r in range(ROWS):
        part = dot(short, grad1[(r + 1) * C : (r + 2) * C, :].astype(BF), nt)
        ice[r, :, :] = part
    ice[0:ROWS] = fine_dot(ice[0:ROWS].reshape(ROWS * FP, C), col_map[...], nt).reshape(ROWS, FP, C)
    for f in range(F):
        project[f * ROWS : (f + 1) * ROWS, :] = ice[0:ROWS, f, :].astype(BF)


def last_kernel(act0, grad1, weight, out, xp, taps):
    fill_taps(taps, weight, 0, True)
    for p in range(17):
        store_pair(xp, p, act0[pair_rows(p), :].astype(F32))

    def finish(p, total):
        total += two_rows(grad1, 2 * p + 1)
        out[2 * p] = total[:, :C].astype(BF)
        out[2 * p + 1] = total[:, C:].astype(BF)

    layer(xp, taps, 16, 4, finish)


def scatter_kernel(planes, scatter, own, mate, *refs):
    outs, wide, found = refs[:-2], refs[-2], refs[-1]
    for s in range(GROUP):
        block, row = (own, mate)[s % 2], (s // 2) * F * ROWS
        for f in range(F):
            wide[s * ROWS : (s + 1) * ROWS, f * C : (f + 1) * C] = block[
                row + f * ROWS : row + (f + 1) * ROWS, :
            ]
    for f in range(F):
        part = dot(scatter[...], wide[:, f * C : (f + 1) * C])
        for panel in range(planes * ROWS // 8):
            row = (panel * F + f) * 8
            found[row : row + 8, :] = part[panel * 8 : panel * 8 + 8]
    for z in range(planes):
        outs[z][...] = found[z * F * ROWS : (z + 1) * F * ROWS, :].astype(BF)


def shape(*dims, dtype=BF):
    return jax.ShapeDtypeStruct(dims, dtype)


def body(
    forcing,
    ice_state,
    sensitivity,
    owner_device,
    panel_slot,
    row_offset,
    intersection_weight,
    col_map,
    ocean_mask,
    lift_weight,
    conv_weight,
    conv_bias,
):
    count = lax.axis_size("tile")
    planes = count // GROUP

    def by_plane(step):
        return [(i, (i + GROUP * step) % count) for i in range(count)]

    def by_mate(step):
        return [(i, i ^ step) for i in range(count)]

    fields = forcing.transpose(0, 2, 1, 3).reshape(F * ROWS, C)
    blocks = [fields] + [lax.ppermute(fields, "tile", by_plane(z)) for z in range(1, planes)]

    ident = (owner_device * 4 + panel_slot) * 8 + row_offset
    table = jnp.concatenate([ident.T.astype(F32), intersection_weight.T], axis=0)
    table = jnp.pad(table, ((0, 0), (0, C - ROWS)))
    table = jnp.broadcast_to(table[None], (count, 2 * K, C))
    ready = table
    table = lax.all_to_all(table, "tile", 0, 0, tiled=True)
    own_column = jnp.concatenate(blocks, axis=0)
    mate_column = lax.ppermute(own_column, "tile", by_mate(1))

    cells = jnp.pad(ocean_mask, ((0, C - ROWS), (0, 0)))[None].astype(BF)
    to_next = jnp.concatenate([ice_state[ROWS - 6 :], sensitivity[ROWS - 3 :], cells], axis=0)
    to_last = jnp.concatenate([ice_state[:6], sensitivity[:3], cells], axis=0)
    picks, scatter = pl.pallas_call(
        functools.partial(pick_kernel, planes),
        out_shape=(shape(SENT * EXT, 2 * planes * ROWS), shape(planes * ROWS, GROUP * ROWS)),
        compiler_params=params(4),
        name="picks",
        cost_estimate=pl.CostEstimate(flops=10**10, bytes_accessed=MIB, transcendentals=0),
    )(table)
    messages = pl.pallas_call(
        functools.partial(message_kernel, planes),
        out_shape=tuple(shape(F * EXT, C) for _ in range(SENT)),
        scratch_shapes=[pltpu.VMEM((2 * planes * ROWS, F * C), BF)],
        compiler_params=params(10),
        name="messages",
    )(picks, own_column, mate_column)
    to_next, to_last, _ = lax.optimization_barrier((to_next, to_last, ready))
    forward = [(i, i + 1) for i in range(count - 1)]
    low = lax.ppermute(to_next, "tile", forward)
    high = lax.ppermute(to_last, "tile", [(b, a) for a, b in forward])
    messages = [messages[0]] + [
        lax.ppermute(messages[s], "tile", by_mate(2 * s)) for s in range(1, SENT)
    ]
    hidden, slope0, ocean = pl.pallas_call(
        first_kernel,
        out_shape=(shape(21 * C, PAIR), shape(21 * C, PAIR), shape(42 * C, C)),
        scratch_shapes=[pltpu.VMEM((22 * C, 2 * TAPS), BF), pltpu.VMEM((4 * TAPS, PAIR), BF)],
        compiler_params=params(14),
        name="first_layer",
        cost_estimate=pl.CostEstimate(flops=4 * 10**9, bytes_accessed=8 * MIB, transcendentals=10**6),
    )(ice_state, low, high, ocean_mask, conv_weight, conv_bias)

    imitated, act0, grad1, project = pl.pallas_call(
        main_kernel,
        out_shape=(
            shape(ROWS, C, C),
            shape(17 * C, PAIR),
            shape(34 * C, C, dtype=F32),
            shape(F * ROWS, C),
        ),
        scratch_shapes=[
            pltpu.VMEM((EXT, FP, C), F32),
            pltpu.VMEM((EXT // GROUP * C, GROUP * C), F32),
            pltpu.VMEM((C, GROUP * C), BF),
            pltpu.VMEM((21 * C, 2 * TAPS), BF),
            pltpu.VMEM((20 * C, 2 * TAPS), BF),
            pltpu.VMEM((20 * C, PAIR), BF),
            pltpu.VMEM((19 * C, PAIR), BF),
            pltpu.VMEM((36 * C, C), F32),
            pltpu.VMEM((38 * C, C), BF),
            pltpu.VMEM((EXT // GROUP * C, C), BF),
        ]
        + [pltpu.VMEM((4 * TAPS, PAIR), BF)] * 4,
        compiler_params=params(32),
        name="middle_layers",
        cost_estimate=pl.CostEstimate(flops=12 * 10**9, bytes_accessed=16 * MIB, transcendentals=10**6),
    )(
        *messages,
        col_map,
        lift_weight,
        conv_bias,
        hidden,
        slope0,
        ocean,
        sensitivity,
        low,
        high,
        conv_weight,
    )
    projects = [project] + [lax.ppermute(project, "tile", by_mate(2 * s)) for s in range(1, SENT)]
    own_projects = jnp.concatenate(projects, axis=0)
    mate_projects = lax.ppermute(own_projects, "tile", by_mate(1))

    sums = pl.pallas_call(
        functools.partial(scatter_kernel, planes),
        out_shape=tuple(shape(F * ROWS, C) for _ in range(planes)),
        scratch_shapes=[
            pltpu.VMEM((GROUP * ROWS, F * C), BF),
            pltpu.VMEM((planes * F * ROWS, C), F32),
        ],
        compiler_params=params(8),
        name="scatter",
    )(scatter, own_projects, mate_projects)
    act0, *sums = lax.optimization_barrier((act0, *sums))
    sums = [sums[0]] + [lax.ppermute(sums[z], "tile", by_plane(-z)) for z in range(1, planes)]
    state_grad = pl.pallas_call(
        last_kernel,
        out_shape=shape(ROWS, C, C),
        scratch_shapes=[pltpu.VMEM((17 * C, 2 * TAPS), BF), pltpu.VMEM((4 * TAPS, PAIR), BF)],
        compiler_params=params(14),
        name="last_adjoint",
        cost_estimate=pl.CostEstimate(flops=3 * 10**9, bytes_accessed=6 * MIB, transcendentals=0),
    )(act0, grad1, conv_weight)

    panel_grad = sum(block.astype(F32) for block in sums)
    panels = forcing.shape[0]
    panel_grad = panel_grad.reshape(panels, F, 8, C).transpose(0, 2, 1, 3)
    return imitated, state_grad, panel_grad


def solution(mesh):
    in_specs = (
        P(("member", "tile"), None, None, None),
        P(("member", "tile"), None, None),
        P(("member", "tile"), None, None),
        P("tile", None),
        P("tile", None),
        P("tile", None),
        P("tile", None),
        P(),
        P("tile", None),
        P(),
        P(),
        P(),
    )
    out_specs = (
        P(("member", "tile"), None, None),
        P(("member", "tile"), None, None),
        P(("member", "tile"), None, None, None),
    )
    return jax.shard_map(body, mesh=mesh, in_specs=in_specs, out_specs=out_specs, check_vma=False)
```

time: 109 us -> 71.4 us (0.66)
  local copies, waits for them, and re-layouts: 21.3 us -> 2.77 us
  Pallas kernels: 36.4 us -> 20.4 us
  starting transfers between devices: 36.7 us -> 30 us
  other arithmetic: 1.48 us -> 3.78 us
  waiting for transfers between devices: 12 us -> 13.2 us
    unnamed x62 -> x19, local copies, waits for them, and re-layouts: 20.2 us -> 0.08 us
    pallas_call x1, Pallas kernels: 20.7 us -> 12.5 us  [body(): pl.pallas_call(main_kernel, out_shape=(shape(ROWS, C, C), shape(17 * C, P...]
    ppermute x3, waiting for transfers between devices: 7.02 us -> 0.01 us  [body(): lax.ppermute(fields, 'tile', by_plane(z))]
    ppermute x14 -> x8, waiting for transfers between devices: 5 us -> 9.31 us  [the longest x3 3.8 us: body(): lax.ppermute(project, 'tile', by_mate(2 * s))]
    ppermute x3, waiting for transfers between devices: 0.01 us -> 3.85 us  [body(): lax.ppermute(sums[z], 'tile', by_plane(-z))]
    pallas_call x3 -> x1, Pallas kernels: 4.26 us -> 0.88 us  [body(): pl.pallas_call(functools.partial(pick_kernel, planes), out_shape=(shape(S...]
    pallas_call x1, Pallas kernels: 6.05 us -> 3.13 us  [body(): pl.pallas_call(first_kernel, out_shape=(shape(21 * C, PAIR), shape(21 * C...]
    all_to_all x1, starting transfers between devices: 7.3 us -> 5.06 us  [body(): table = lax.all_to_all(table, 'tile', 0, 0, tiled=True)]
  transfers between devices with their start and end apart: 23 -> 17, of which waited for: 6 -> 6; matrix products, arithmetic and copies ran while one was open for 2% -> 8% of each run, Pallas kernels for 11% -> 11%
where the time goes in v1:
time: 71.4 us; the launch traced here: 71 us
  starting transfers between devices  30 us (42%)
  Pallas kernels  20.4 us (29%)
  waiting for transfers between devices  13.2 us (18%)
  other arithmetic  3.78 us (5%)
  local copies, waits for them, and re-layouts  2.77 us (4%)
  between operations  0.85 us (1%)
    pallas_call x1, Pallas kernels, body(): pl.pallas_call(main_kernel, out_shape=(shape(ROWS, C, C), shape(17 * C, P...  12.5 us
    ppermute x3, starting transfers between devices, body(): lax.ppermute(fields, 'tile', by_plane(z))  6.11 us
    all_to_all x1, starting transfers between devices, body(): table = lax.all_to_all(table, 'tile', 0, 0, tiled=True)  5.06 us
    ppermute x3, starting transfers between devices, body(): lax.ppermute(sums[z], 'tile', by_plane(-z))  4.58 us
    ppermute x3, starting transfers between devices, body(): lax.ppermute(messages[s], 'tile', by_mate(2 * s))  4.37 us
    ppermute x3, starting transfers between devices, body(): lax.ppermute(project, 'tile', by_mate(2 * s))  4.07 us
    ppermute x3, waiting for transfers between devices, body(): lax.ppermute(sums[z], 'tile', by_plane(-z))  3.85 us
    ppermute x3, waiting for transfers between devices, body(): lax.ppermute(project, 'tile', by_mate(2 * s))  3.8 us
  transfers between devices with their start and end apart: 17, of which 6 were waited for; matrix products, arithmetic and copies ran while one was open for 8% of the time, Pallas kernels for 11%

profile of v1, /device:TPU:0, one launch (start us, length us, event | category | flops | bytes accessed | tf_op | source)
XLA Modules:
  0.0 71.0 jit_solution(3893443581924434534)
XLA Ops:
  0.6 5.1 %collective-permute-start.2 = (bf16[320,128]{1,0:T(8,128)(2,1)}, bf16[320,128]{1,0:T(8,128)(2,1)S(1)}, u32[]{:S(2)}, u32[]{:S(2)}) collective-permute-start(bf16[320,128]{1,0:T(8,128)(2,1)} %bitcast.12), channel_id=1, source_target_pairs={{0,24},{1,25},{2,26},{3,27},{4,28},{5,29},{6,30},{7,31},{8,0},{9,1... | collective-permute-start | bytes 245768 | tf_op jit(solution)/shard_map/ppermute | solution.py:358
  5.7 1.0 %collective-permute-start = (bf16[320,128]{1,0:T(8,128)(2,1)}, bf16[320,128]{1,0:T(8,128)(2,1)S(1)}, u32[]{:S(2)}, u32[]{:S(2)}) collective-permute-start(bf16[320,128]{1,0:T(8,128)(2,1)} %bitcast.14), channel_id=1, source_target_pairs={{0,8},{1,9},{2,10},{3,11},{4,12},{5,13},{6,14},{7,15},{8,16},{9,17... | collective-permute-start | bytes 245768 | tf_op jit(solution)/shard_map/ppermute | solution.py:358
  6.7 0.7 %convert_bitcast_fusion = f32[4,32]{1,0:T(4,128)S(1)} fusion(s32[32,4]{0,1:T(4,128)} %param.17, s32[32,4]{0,1:T(4,128)} %param.16, s32[32,4]{0,1:T(4,128)} %param.15), kind=kLoop, calls=%fused_computation.11 | loop fusion | flops 640 | bytes 2048 | tf_op jit(solution)/shard_map/convert_element_type | solution.py:361
  7.5 0.7 select_maximum_fusion
  8.2 0.7 broadcast_in_dim.2
  8.8 5.1 %all-to-all-start = ((f32[32,8,128]{2,1,0:T(8,128)}), f32[32,8,128]{2,1,0:T(8,128)S(1)}, u32[]{:S(2)}, u32[]{:S(2)}) async-start(f32[32,8,128]{2,1,0:T(8,128)} %broadcast_in_dim.2), calls=%async_computation | async-start | bytes 262144 | tf_op jit(solution)/shard_map/all_to_all | solution.py:365
  13.9 0.7 %convert.4 = bf16[32,128]{1,0:T(8,128)(2,1)S(1)} convert(s32[32,128]{1,0:T(8,128)} %mask.1) | non-fusion elementwise | flops 4096 | bytes 24576 | tf_op jit(solution)/shard_map/convert
  14.6 1.0 %fusion.1 = (bf16[3,128,128]{2,1,0:T(8,128)(2,1)S(1)}, bf16[3,128,128]{2,1,0:T(8,128)(2,1)S(1)}) fusion(bf16[32,128,128]{2,1,0:T(8,128)(2,1)} %refs_10_.1), kind=kLoop, calls=%fused_computation.13 | loop fusion | bytes 393216 | tf_op jit(solution)/shard_map/slice | solution.py:371
  15.6 1.1 %fusion = (bf16[6,128,128]{2,1,0:T(8,128)(2,1)S(1)}, bf16[6,128,128]{2,1,0:T(8,128)(2,1)S(1)}) fusion(bf16[32,128,128]{2,1,0:T(8,128)(2,1)} %ice.1), kind=kLoop, calls=%fused_computation.12 | loop fusion | bytes 786432 | tf_op jit(solution)/shard_map/slice | solution.py:371
  16.6 0.9 %pad_maximum_fusion = (bf16[10,128,128]{2,1,0:T(8,128)(2,1)}, bf16[10,128,128]{2,1,0:T(8,128)(2,1)}) fusion(bf16[1,128,128]{2,1,0:T(8,128)(2,1)S(1)} %pad_bitcast_fusion, bf16[3,128,128]{2,1,0:T(8,128)(2,1)S(1)} %get-tuple-element.53, bf16[6,128,128]{2,1,0:T(8,128)(2,1)S(1)} %get-tuple-element.51, bf16[3,128,128]{2,1,0:T(8,128)(2,1)S(1)} %get-tuple-element.54, ...), kind=kLoop, calls=%fused_computation | loop fusion | flops 655360 | bytes 1277952 | tf_op jit(solution)/shard_map/concatenate | solution.py:371
  17.6 2.2 %collective-permute-start.7 = (bf16[10,128,128]{2,1,0:T(8,128)(2,1)}, bf16[10,128,128]{2,1,0:T(8,128)(2,1)S(1)}, u32[]{:S(2)}, u32[]{:S(2)}) collective-permute-start(bf16[10,128,128]{2,1,0:T(8,128)(2,1)} %get-tuple-element.32), channel_id=1, source_target_pairs={{0,1},{1,2},{2,3},{3,4},{4,5},{5,6},{6,7},{7,8},{8,9},{9,10},{10,1... | collective-permute-start | bytes 983048 | tf_op jit(solution)/shard_map/ppermute | solution.py:388
  19.7 1.3 %collective-permute-start.8 = (bf16[10,128,128]{2,1,0:T(8,128)(2,1)}, bf16[10,128,128]{2,1,0:T(8,128)(2,1)S(1)}, u32[]{:S(2)}, u32[]{:S(2)}) collective-permute-start(bf16[10,128,128]{2,1,0:T(8,128)(2,1)} %get-tuple-element.33), channel_id=1, source_target_pairs={{1,0},{2,1},{3,2},{4,3},{5,4},{6,5},{7,6},{8,7},{9,8},{10,9},{11,1... | collective-permute-start | bytes 983048 | tf_op jit(solution)/shard_map/ppermute | solution.py:389
  21.1 2.3 %collective-permute-start.3 = (bf16[1280,128]{1,0:T(8,128)(2,1)S(1)}, bf16[1280,128]{1,0:T(8,128)(2,1)S(1)}, u32[]{:S(2)}, u32[]{:S(2)}) collective-permute-start(bf16[1280,128]{1,0:T(8,128)(2,1)S(1)} %pad_maximum_fusion.2.own), channel_id=1, source_target_pairs={{0,1},{1,0},{2,3},{3,2},{4,5},{5,4},{6,7},{7,6},{8,9},{9,8},{10,11... | collective-permute-start | bytes 983048 | tf_op jit(solution)/shard_map/ppermute | solution.py:367
  23.5 0.9 %picks.1 = (bf16[192,256]{1,0:T(8,128)(2,1)S(1)}, bf16[128,256]{1,0:T(8,128)(2,1)S(1)}) custom-call(f32[32,8,128]{2,1,0:T(8,128)S(1)} %all-to-all-done.table), custom_call_target="tpu_custom_call" | custom-call | flops 10000000000 | bytes 1048576 | tf_op jit(solution)/shard_map/picks/pallas_call | solution.py:372
  24.3 0.5 collective-permute-done.3.mate
  24.8 0.5 messages.1
  25.3 1.9 %collective-permute-start.4 = (bf16[480,128]{1,0:T(8,128)(2,1)S(1)}, bf16[480,128]{1,0:T(8,128)(2,1)S(1)}, u32[]{:S(2)}, u32[]{:S(2)}) collective-permute-start(bf16[480,128]{1,0:T(8,128)(2,1)S(1)} %get-tuple-element.29), channel_id=1, source_target_pairs={{0,2},{1,3},{2,0},{3,1},{4,6},{5,7},{6,4},{7,5},{8,10},{9,11},{10,... | collective-permute-start | bytes 368648 | tf_op jit(solution)/shard_map/ppermute | solution.py:391
  27.3 1.5 %collective-permute-start.5 = (bf16[480,128]{1,0:T(8,128)(2,1)S(1)}, bf16[480,128]{1,0:T(8,128)(2,1)S(1)}, u32[]{:S(2)}, u32[]{:S(2)}) collective-permute-start(bf16[480,128]{1,0:T(8,128)(2,1)S(1)} %get-tuple-element.30), channel_id=1, source_target_pairs={{0,4},{1,5},{2,6},{3,7},{4,0},{5,1},{6,2},{7,3},{8,12},{9,13},{10,... | collective-permute-start | bytes 368648 | tf_op jit(solution)/shard_map/ppermute | solution.py:391
  28.7 1.0 %collective-permute-start.6 = (bf16[480,128]{1,0:T(8,128)(2,1)S(1)}, bf16[480,128]{1,0:T(8,128)(2,1)S(1)}, u32[]{:S(2)}, u32[]{:S(2)}) collective-permute-start(bf16[480,128]{1,0:T(8,128)(2,1)S(1)} %get-tuple-element.31), channel_id=1, source_target_pairs={{0,6},{1,7},{2,4},{3,5},{4,2},{5,3},{6,0},{7,1},{8,14},{9,15},{10,... | collective-permute-start | bytes 368648 | tf_op jit(solution)/shard_map/ppermute | solution.py:391
  29.7 3.1 %first_layer.1 = (bf16[2688,256]{1,0:T(8,128)(2,1)S(1)}, bf16[2688,256]{1,0:T(8,128)(2,1)S(1)}, bf16[5376,128]{1,0:T(8,128)(2,1)S(1)}) custom-call(bf16[32,128,128]{2,1,0:T(8,128)(2,1)S(1)} %copy-done, bf16[10,128,128]{2,1,0:T(8,128)(2,1)S(1)} %collective-permute-done.7.low.refs_11_, bf16[10,128,128]{2,1,0:T(8,128)(2,1)S(1)} %collective-permute-done.8.high.refs_12_, ...), custom_call_target="tpu_custom_call" | custom-call | flops 4000000000 | bytes 8388608 | tf_op jit(solution)/shard_map/first_layer/pallas_call | solution.py:393
  32.9 1.9 %collective-permute-done.4.refs_1_ = bf16[480,128]{1,0:T(8,128)(2,1)S(1)} collective-permute-done((bf16[480,128]{1,0:T(8,128)(2,1)S(1)}, bf16[480,128]{1,0:T(8,128)(2,1)S(1)}, u32[]{:S(2)}, u32[]{:S(2)}) %collective-permute-start.4) | collective-permute-done | bytes 122912 | tf_op jit(solution)/shard_map/ppermute | solution.py:391
  34.8 1.5 %collective-permute-done.6.refs_3_ = bf16[480,128]{1,0:T(8,128)(2,1)S(1)} collective-permute-done((bf16[480,128]{1,0:T(8,128)(2,1)S(1)}, bf16[480,128]{1,0:T(8,128)(2,1)S(1)}, u32[]{:S(2)}, u32[]{:S(2)}) %collective-permute-start.6) | collective-permute-done | bytes 122912 | tf_op jit(solution)/shard_map/ppermute | solution.py:391
  36.3 12.5 %middle_layers.1 = (bf16[32,128,128]{2,1,0:T(8,128)(2,1)}, bf16[2176,256]{1,0:T(8,128)(2,1)S(1)}, f32[4352,128]{1,0:T(8,128)S(1)}, bf16[320,128]{1,0:T(8,128)(2,1)S(1)}) custom-call(bf16[480,128]{1,0:T(8,128)(2,1)S(1)} %get-tuple-element.28.refs_0_, bf16[480,128]{1,0:T(8,128)(2,1)S(1)} %collective-permute-done.4.refs_1_, ...), custom_call_target="tpu_custom_call" | custom-call | flops 12000000000 | bytes 16777216 | tf_op jit(solution)/shard_map/middle_layers/pallas_call | solution.py:402
  48.8 3.4 %collective-permute-start.11 = (bf16[320,128]{1,0:T(8,128)(2,1)S(1)}, bf16[320,128]{1,0:T(8,128)(2,1)S(1)}, u32[]{:S(2)}, u32[]{:S(2)}) collective-permute-start(bf16[320,128]{1,0:T(8,128)(2,1)S(1)} %get-tuple-element.40), channel_id=1, source_target_pairs={{0,6},{1,7},{2,4},{3,5},{4,2},{5,3},{6,0},{7,1},{8,14},{9,15},{10,... | collective-permute-start | bytes 245768 | tf_op jit(solution)/shard_map/ppermute | solution.py:439
  52.2 0.6 collective-permute-start.9
  52.9 3.8 %collective-permute-done.9 = bf16[320,128]{1,0:T(8,128)(2,1)S(1)} collective-permute-done((bf16[320,128]{1,0:T(8,128)(2,1)S(1)}, bf16[320,128]{1,0:T(8,128)(2,1)S(1)}, u32[]{:S(2)}, u32[]{:S(2)}) %collective-permute-start.9) | collective-permute-done | bytes 81952 | tf_op jit(solution)/shard_map/ppermute | solution.py:439
  56.8 1.6 %collective-permute-done.12.mate = bf16[1280,128]{1,0:T(8,128)(2,1)S(1)} collective-permute-done((bf16[1280,128]{1,0:T(8,128)(2,1)S(1)}, bf16[1280,128]{1,0:T(8,128)(2,1)S(1)}, u32[]{:S(2)}, u32[]{:S(2)}) %collective-permute-start.12) | collective-permute-done | bytes 327712 | tf_op jit(solution)/shard_map/ppermute | solution.py:441
  58.8 3.5 %collective-permute-start.13 = (bf16[320,128]{1,0:T(8,128)(2,1)S(1)}, bf16[320,128]{1,0:T(8,128)(2,1)S(1)}, u32[]{:S(2)}, u32[]{:S(2)}) collective-permute-start(bf16[320,128]{1,0:T(8,128)(2,1)S(1)} %get-tuple-element.48), channel_id=1, source_target_pairs={{0,24},{1,25},{2,26},{3,27},{4,28},{5,29},{6,30},{7,31},{8,0},{9,1... | collective-permute-start | bytes 245768 | tf_op jit(solution)/shard_map/ppermute | solution.py:454
  62.3 1.1 %collective-permute-start.15 = (bf16[320,128]{1,0:T(8,128)(2,1)S(1)}, bf16[320,128]{1,0:T(8,128)(2,1)S(1)}, u32[]{:S(2)}, u32[]{:S(2)}) collective-permute-start(bf16[320,128]{1,0:T(8,128)(2,1)S(1)} %get-tuple-element.50), channel_id=1, source_target_pairs={{0,8},{1,9},{2,10},{3,11},{4,12},{5,13},{6,14},{7,15},{8,16},{9,17... | collective-permute-start | bytes 245768 | tf_op jit(solution)/shard_map/ppermute | solution.py:454
  63.4 3.1 %last_adjoint.1 = bf16[32,128,128]{2,1,0:T(8,128)(2,1)} custom-call(bf16[2176,256]{1,0:T(8,128)(2,1)S(1)} %get-tuple-element.45.act0, f32[4352,128]{1,0:T(8,128)S(1)} %get-tuple-element.46.grad1, bf16[3,3,3,128,128]{4,3,2,1,0:T(8,128)(2,1)S(1)} %copy-done.3), custom_call_target="tpu_custom_call" | custom-call | flops 3000000000 | bytes 6291456 | tf_op jit(solution)/shard_map/last_adjoint/pallas_call | solution.py:455
  66.5 3.8 %collective-permute-done.14 = bf16[320,128]{1,0:T(8,128)(2,1)S(1)} collective-permute-done((bf16[320,128]{1,0:T(8,128)(2,1)S(1)}, bf16[320,128]{1,0:T(8,128)(2,1)S(1)}, u32[]{:S(2)}, u32[]{:S(2)}) %collective-permute-start.14) | collective-permute-done | bytes 81952 | tf_op jit(solution)/shard_map/ppermute | solution.py:454
  70.3 0.7 convert_add_fusion
  (38 shorter events, 0.6 us)
Async XLA Ops:
  0.6 20.4 %collective-permute-start.2 = (bf16[320,128]{1,0:T(8,128)(2,1)}, bf16[320,128]{1,0:T(8,128)(2,1)S(1)}, u32[]{:S(2)}, u32[]{:S(2)}) collective-permute-start(bf16[320,128]{1,0:T(8,128)(2,1)} %bitcast.12), channel_id=1, source_target_pairs={{0,24},{1,25},{2,26},{3,27},{4,28},{5,29},{6,30},{7,31},{8,0},{9,1... | collective-permute-start | bytes 245768 | tf_op jit(solution)/shard_map/ppermute | solution.py:358
  5.7 15.3 %collective-permute-start.1 = (bf16[320,128]{1,0:T(8,128)(2,1)}, bf16[320,128]{1,0:T(8,128)(2,1)S(1)}, u32[]{:S(2)}, u32[]{:S(2)}) collective-permute-start(bf16[320,128]{1,0:T(8,128)(2,1)} %bitcast.13), channel_id=1, source_target_pairs={{0,16},{1,17},{2,18},{3,19},{4,20},{5,21},{6,22},{7,23},{8,24},{9,... | collective-permute-start | bytes 245768 | tf_op jit(solution)/shard_map/ppermute | solution.py:358
  5.7 15.3 %collective-permute-start = (bf16[320,128]{1,0:T(8,128)(2,1)}, bf16[320,128]{1,0:T(8,128)(2,1)S(1)}, u32[]{:S(2)}, u32[]{:S(2)}) collective-permute-start(bf16[320,128]{1,0:T(8,128)(2,1)} %bitcast.14), channel_id=1, source_target_pairs={{0,8},{1,9},{2,10},{3,11},{4,12},{5,13},{6,14},{7,15},{8,16},{9,17... | collective-permute-start | bytes 245768 | tf_op jit(solution)/shard_map/ppermute | solution.py:358
  8.8 12.2 %copy-start.7 = (bf16[4,8,10,128]{3,1,2,0:T(8,128)(2,1)S(1)}, bf16[4,8,10,128]{3,1,2,0:T(8,128)(2,1)}, u32[]{:S(2)}) copy-start(bf16[4,8,10,128]{3,1,2,0:T(8,128)(2,1)} %param.12) | copy-start | bytes 245764
  8.8 14.6 %all-to-all-start = ((f32[32,8,128]{2,1,0:T(8,128)}), f32[32,8,128]{2,1,0:T(8,128)S(1)}, u32[]{:S(2)}, u32[]{:S(2)}) async-start(f32[32,8,128]{2,1,0:T(8,128)} %broadcast_in_dim.2), calls=%async_computation | async-start | bytes 262144 | tf_op jit(solution)/shard_map/all_to_all | solution.py:365
  17.6 12.2 %collective-permute-start.7 = (bf16[10,128,128]{2,1,0:T(8,128)(2,1)}, bf16[10,128,128]{2,1,0:T(8,128)(2,1)S(1)}, u32[]{:S(2)}, u32[]{:S(2)}) collective-permute-start(bf16[10,128,128]{2,1,0:T(8,128)(2,1)} %get-tuple-element.32), channel_id=1, source_target_pairs={{0,1},{1,2},{2,3},{3,4},{4,5},{5,6},{6,7},{7,8},{8,9},{9,10},{10,1... | collective-permute-start | bytes 983048 | tf_op jit(solution)/shard_map/ppermute | solution.py:388
  19.7 10.0 %collective-permute-start.8 = (bf16[10,128,128]{2,1,0:T(8,128)(2,1)}, bf16[10,128,128]{2,1,0:T(8,128)(2,1)S(1)}, u32[]{:S(2)}, u32[]{:S(2)}) collective-permute-start(bf16[10,128,128]{2,1,0:T(8,128)(2,1)} %get-tuple-element.33), channel_id=1, source_target_pairs={{1,0},{2,1},{3,2},{4,3},{5,4},{6,5},{7,6},{8,7},{9,8},{10,9},{11,1... | collective-permute-start | bytes 983048 | tf_op jit(solution)/shard_map/ppermute | solution.py:389
  21.1 8.6 %copy-start = (bf16[32,128,128]{2,1,0:T(8,128)(2,1)S(1)}, bf16[32,128,128]{2,1,0:T(8,128)(2,1)}, u32[]{:S(2)}) copy-start(bf16[32,128,128]{2,1,0:T(8,128)(2,1)} %ice.1) | copy-start | bytes 3145732
  21.1 8.6 %copy-start.2 = (s32[32,128]{1,0:T(8,128)S(1)}, s32[32,128]{1,0:T(8,128)}, u32[]{:S(2)}) copy-start(s32[32,128]{1,0:T(8,128)} %mask.1) | copy-start | bytes 49156
  21.1 8.6 %copy-start.3 = (bf16[3,3,3,128,128]{4,3,2,1,0:T(8,128)(2,1)S(1)}, bf16[3,3,3,128,128]{4,3,2,1,0:T(8,128)(2,1)}, u32[]{:S(2)}) copy-start(bf16[3,3,3,128,128]{4,3,2,1,0:T(8,128)(2,1)} %weight.3) | copy-start | bytes 2654212
  21.1 8.6 %copy-start.6 = (f32[3,128]{1,0:T(4,128)S(1)}, f32[3,128]{1,0:T(4,128)}, u32[]{:S(2)}) copy-start(f32[3,128]{1,0:T(4,128)} %refs_6_.1) | copy-start | bytes 4612
  21.1 3.7 %collective-permute-start.3 = (bf16[1280,128]{1,0:T(8,128)(2,1)S(1)}, bf16[1280,128]{1,0:T(8,128)(2,1)S(1)}, u32[]{:S(2)}, u32[]{:S(2)}) collective-permute-start(bf16[1280,128]{1,0:T(8,128)(2,1)S(1)} %pad_maximum_fusion.2.own), channel_id=1, source_target_pairs={{0,1},{1,0},{2,3},{3,2},{4,5},{5,4},{6,7},{7,6},{8,9},{9,8},{10,11... | collective-permute-start | bytes 983048 | tf_op jit(solution)/shard_map/ppermute | solution.py:367
  25.3 9.5 %collective-permute-start.4 = (bf16[480,128]{1,0:T(8,128)(2,1)S(1)}, bf16[480,128]{1,0:T(8,128)(2,1)S(1)}, u32[]{:S(2)}, u32[]{:S(2)}) collective-permute-start(bf16[480,128]{1,0:T(8,128)(2,1)S(1)} %get-tuple-element.29), channel_id=1, source_target_pairs={{0,2},{1,3},{2,0},{3,1},{4,6},{5,7},{6,4},{7,5},{8,10},{9,11},{10,... | collective-permute-start | bytes 368648 | tf_op jit(solution)/shard_map/ppermute | solution.py:391
  27.3 7.6 %collective-permute-start.5 = (bf16[480,128]{1,0:T(8,128)(2,1)S(1)}, bf16[480,128]{1,0:T(8,128)(2,1)S(1)}, u32[]{:S(2)}, u32[]{:S(2)}) collective-permute-start(bf16[480,128]{1,0:T(8,128)(2,1)S(1)} %get-tuple-element.30), channel_id=1, source_target_pairs={{0,4},{1,5},{2,6},{3,7},{4,0},{5,1},{6,2},{7,3},{8,12},{9,13},{10,... | collective-permute-start | bytes 368648 | tf_op jit(solution)/shard_map/ppermute | solution.py:391
  28.7 7.6 %copy-start.1 = (bf16[32,128,128]{2,1,0:T(8,128)(2,1)S(1)}, bf16[32,128,128]{2,1,0:T(8,128)(2,1)}, u32[]{:S(2)}) copy-start(bf16[32,128,128]{2,1,0:T(8,128)(2,1)} %refs_10_.1) | copy-start | bytes 3145732
  28.7 7.6 %copy-start.4 = (f32[128,128]{1,0:T(8,128)S(1)}, f32[128,128]{1,0:T(8,128)}, u32[]{:S(2)}) copy-start(f32[128,128]{1,0:T(8,128)} %refs_4_.1) | copy-start | bytes 196612
  28.7 7.6 %copy-start.5 = (bf16[10,128]{1,0:T(8,128)(2,1)S(1)}, bf16[10,128]{1,0:T(8,128)(2,1)}, u32[]{:S(2)}) copy-start(bf16[10,128]{1,0:T(8,128)(2,1)} %refs_5_.1) | copy-start | bytes 7684
  28.7 7.6 %collective-permute-start.6 = (bf16[480,128]{1,0:T(8,128)(2,1)S(1)}, bf16[480,128]{1,0:T(8,128)(2,1)S(1)}, u32[]{:S(2)}, u32[]{:S(2)}) collective-permute-start(bf16[480,128]{1,0:T(8,128)(2,1)S(1)} %get-tuple-element.31), channel_id=1, source_target_pairs={{0,6},{1,7},{2,4},{3,5},{4,2},{5,3},{6,0},{7,1},{8,14},{9,15},{10,... | collective-permute-start | bytes 368648 | tf_op jit(solution)/shard_map/ppermute | solution.py:391
  48.8 7.9 %collective-permute-start.11 = (bf16[320,128]{1,0:T(8,128)(2,1)S(1)}, bf16[320,128]{1,0:T(8,128)(2,1)S(1)}, u32[]{:S(2)}, u32[]{:S(2)}) collective-permute-start(bf16[320,128]{1,0:T(8,128)(2,1)S(1)} %get-tuple-element.40), channel_id=1, source_target_pairs={{0,6},{1,7},{2,4},{3,5},{4,2},{5,3},{6,0},{7,1},{8,14},{9,15},{10,... | collective-permute-start | bytes 245768 | tf_op jit(solution)/shard_map/ppermute | solution.py:439
  52.2 4.5 %collective-permute-start.10 = (bf16[320,128]{1,0:T(8,128)(2,1)S(1)}, bf16[320,128]{1,0:T(8,128)(2,1)S(1)}, u32[]{:S(2)}, u32[]{:S(2)}) collective-permute-start(bf16[320,128]{1,0:T(8,128)(2,1)S(1)} %get-tuple-element.40), channel_id=1, source_target_pairs={{0,4},{1,5},{2,6},{3,7},{4,0},{5,1},{6,2},{7,3},{8,12},{9,13},{10,... | collective-permute-start | bytes 245768 | tf_op jit(solution)/shard_map/ppermute | solution.py:439
  52.2 4.4 %collective-permute-start.9 = (bf16[320,128]{1,0:T(8,128)(2,1)S(1)}, bf16[320,128]{1,0:T(8,128)(2,1)S(1)}, u32[]{:S(2)}, u32[]{:S(2)}) collective-permute-start(bf16[320,128]{1,0:T(8,128)(2,1)S(1)} %get-tuple-element.40), channel_id=1, source_target_pairs={{0,2},{1,3},{2,0},{3,1},{4,6},{5,7},{6,4},{7,5},{8,10},{9,11},{10,... | collective-permute-start | bytes 245768 | tf_op jit(solution)/shard_map/ppermute | solution.py:439
  56.7 1.7 %collective-permute-start.12 = (bf16[1280,128]{1,0:T(8,128)(2,1)S(1)}, bf16[1280,128]{1,0:T(8,128)(2,1)S(1)}, u32[]{:S(2)}, u32[]{:S(2)}) collective-permute-start(bf16[1280,128]{1,0:T(8,128)(2,1)S(1)} %constant_dynamic-update-slice_fusion.own), channel_id=1, source_target_pairs={{0,1},{1,0},{2,3},{3,2},{4,5},{5,4},{6,7},{7,6},{8,9},{9,8},{10,11... | collective-permute-start | bytes 983048 | tf_op jit(solution)/shard_map/ppermute | solution.py:441
  58.8 7.7 %collective-permute-start.13 = (bf16[320,128]{1,0:T(8,128)(2,1)S(1)}, bf16[320,128]{1,0:T(8,128)(2,1)S(1)}, u32[]{:S(2)}, u32[]{:S(2)}) collective-permute-start(bf16[320,128]{1,0:T(8,128)(2,1)S(1)} %get-tuple-element.48), channel_id=1, source_target_pairs={{0,24},{1,25},{2,26},{3,27},{4,28},{5,29},{6,30},{7,31},{8,0},{9,1... | collective-permute-start | bytes 245768 | tf_op jit(solution)/shard_map/ppermute | solution.py:454
  62.3 8.0 %collective-permute-start.14 = (bf16[320,128]{1,0:T(8,128)(2,1)S(1)}, bf16[320,128]{1,0:T(8,128)(2,1)S(1)}, u32[]{:S(2)}, u32[]{:S(2)}) collective-permute-start(bf16[320,128]{1,0:T(8,128)(2,1)S(1)} %get-tuple-element.49), channel_id=1, source_target_pairs={{0,16},{1,17},{2,18},{3,19},{4,20},{5,21},{6,22},{7,23},{8,24},{9,... | collective-permute-start | bytes 245768 | tf_op jit(solution)/shard_map/ppermute | solution.py:454
  62.3 8.0 %collective-permute-start.15 = (bf16[320,128]{1,0:T(8,128)(2,1)S(1)}, bf16[320,128]{1,0:T(8,128)(2,1)S(1)}, u32[]{:S(2)}, u32[]{:S(2)}) collective-permute-start(bf16[320,128]{1,0:T(8,128)(2,1)S(1)} %get-tuple-element.50), channel_id=1, source_target_pairs={{0,8},{1,9},{2,10},{3,11},{4,12},{5,13},{6,14},{7,15},{8,16},{9,17... | collective-permute-start | bytes 245768 | tf_op jit(solution)/shard_map/ppermute | solution.py:454

commit v2 on v1

--- a/solution.py
+++ b/solution.py
@@ -16,8 +16,8 @@
 PAD = 8
 GROUP = 8
 SENT = GROUP // 2
+STEP = 1
 PAIR = 2 * C
-TAPS = 3 * C
 BF = jnp.bfloat16
 F32 = jnp.float32
 MIB = 1 << 20
@@ -50,21 +50,12 @@
 
 
 def store_pair(xp, index, value):
-    column = lax.broadcasted_iota(jnp.int32, (C, PAIR), 0)
-    before = jnp.where(column == 0, 0.0, pltpu.roll(value, 1, 0)).astype(BF)
-    after = jnp.where(column == C - 1, 0.0, pltpu.roll(value, C - 1, 0)).astype(BF)
-    value = value.astype(BF)
-    rows = pair_rows(index)
-    for half in range(2):
-        lanes = slice(half * C, half * C + C)
-        for tap, part in enumerate((before, value, after)):
-            start = half * TAPS + tap * C
-            xp[rows, start : start + C] = part[:, lanes]
+    xp[pair_rows(index), :] = value.astype(BF)
 
 
 def centre(xp, index):
-    low = xp[pair_rows(index), TAPS + C : TAPS + 2 * C]
-    high = xp[pair_rows(index + 1), C : 2 * C]
+    low = xp[pair_rows(index), C:]
+    high = xp[pair_rows(index + 1), :C]
     return jnp.concatenate([low, high], axis=1).astype(F32)
 
 
@@ -77,13 +68,21 @@
     return jnp.concatenate([low, high], axis=1).astype(F32)
 
 
-def layer(xp, weight, count, step, finish):
+def layer(xp, taps, count, step, finish):
+    sub_row = lax.broadcasted_iota(jnp.int32, (8, PAIR), 0)
     for first in range(0, count, step):
         size = min(step, count - first)
-        total = dot(xp[pair_rows(first, size), :], weight[: 2 * TAPS, :])
-        total += dot(xp[pair_rows(first + 1, size), :], weight[2 * TAPS :, :])
+        seen = jnp.concatenate(
+            [xp[pair_rows(first, size), :], xp[pair_rows(first + 1, size), :]], axis=1
+        )
+        parts = [dot(seen, taps[:, b * PAIR : (b + 1) * PAIR]) for b in range(3)]
         for j in range(size):
-            finish(first + j, total[j * C : (j + 1) * C])
+            rows = slice(j * C, (j + 1) * C)
+            before = pltpu.roll(parts[0][rows], 1, 0)
+            before = jnp.concatenate([jnp.where(sub_row == 0, 0.0, before[:8]), before[8:]], axis=0)
+            after = pltpu.roll(parts[2][rows], C - 1, 0)
+            after = jnp.concatenate([after[:-8], jnp.where(sub_row == 7, 0.0, after[-8:])], axis=0)
+            finish(first + j, parts[1][rows] + before + after)
 
 
 def by_field(value, field):
@@ -149,18 +148,18 @@
 
 
 def fill_taps(taps, weight, l, back):
-    zero = jnp.zeros((TAPS, C), BF)
-    taps[0:TAPS, C:] = zero
-    taps[3 * TAPS :, :C] = zero
-    for a in range(3):
-        for b in range(3):
+    zero = jnp.zeros((C, C), BF)
+    for b in range(3):
+        taps[0:C, b * PAIR + C : (b + 1) * PAIR] = zero
+        taps[3 * C :, b * PAIR : b * PAIR + C] = zero
+        for a in range(3):
             if back:
                 block = weight[l, 2 - a, 2 - b].astype(F32).T.astype(BF)
             else:
                 block = weight[l, a, b]
             for half in range(2):
-                start = (a + half) * TAPS + b * C
-                taps[start : start + C, half * C : half * C + C] = block
+                start = b * PAIR + half * C
+                taps[(a + half) * C : (a + half + 1) * C, start : start + C] = block
 
 
 def first_kernel(ice, low, high, mask, weight, bias, hidden, slope, ocean, xp, taps):
@@ -168,16 +167,16 @@
 
     def ice_row(r):
         if r < 0:
-            return low[r + 6]
+            return low[(r + 6) * C : (r + 7) * C, :]
         if r >= ROWS:
-            return high[r - ROWS]
+            return high[(r - ROWS) * C : (r - ROWS + 1) * C, :]
         return ice[r]
 
     for p in range(22):
         row = 2 * p - 6
         store_pair(xp, p, jnp.concatenate([ice_row(row), ice_row(row + 1)], axis=1).astype(F32))
-    before = low[9, 0:ROWS, :].astype(F32)[ROWS - PAD :]
-    after = high[9, 0:ROWS, :].astype(F32)[:PAD]
+    before = low[9 * C : 9 * C + 2 * PAD, :].astype(F32)[:PAD]
+    after = high[9 * C : 9 * C + 2 * PAD, :].astype(F32)[:PAD]
     cells = jnp.concatenate([before, mask[...].astype(F32), after], axis=0)
     cells = jnp.concatenate([cells, jnp.zeros((C - EXT, C), F32)], axis=0).T
     for r in range(-5, 37):
@@ -192,14 +191,14 @@
         slope[pair_rows(p), :] = (cell - moved * tangent).astype(BF)
         hidden[pair_rows(p), :] = (centre(xp, p) + moved).astype(BF)
 
-    layer(xp, taps, 21, 4, finish)
+    layer(xp, taps, 21, STEP, finish)
 
 
 def main_kernel(*refs):
     messages = refs[:SENT]
     (col_map, lift, bias, hidden, slope0, ocean, sens, low, high, weight) = refs[SENT : SENT + 10]
     imitated, act0, grad1, project = refs[SENT + 10 : SENT + 14]
-    ice, lifted, diag, xa, xb, slope1, slope2, grads, out_rows, turned, *taps = refs[SENT + 14 :]
+    ice, lifted, diag, xa, xb, slope1, slope2, grads, out_rows, turned, shown, sem, *taps = refs[SENT + 14 :]
     w1f, w2f, w2b, w1b = taps
     for n, (l, back) in enumerate(((1, False), (2, False), (2, True), (1, True))):
         fill_taps(taps[n], weight, l, back)
@@ -228,8 +227,7 @@
     for p in range(21):
         row = 2 * p - 5
         add = jnp.concatenate([lifted_row(row), lifted_row(row + 1)], axis=1)
-        value = (hidden[pair_rows(p), :].astype(F32) + add).astype(BF)
-        store_pair(xa, p, value.astype(F32))
+        store_pair(xa, p, hidden[pair_rows(p), :].astype(F32) + add)
 
     def bias_of(l):
         return jnp.concatenate([bias[l : l + 1, :], bias[l : l + 1, :]], axis=1)
@@ -241,10 +239,9 @@
         cell = two_rows(ocean, 2 * p + 1)
         moved = cell * tangent
         slope1[pair_rows(p), :] = (cell - moved * tangent).astype(BF)
-        value = (centre(xa, p) + moved).astype(BF)
-        store_pair(xb, p, value.astype(F32))
-
-    layer(xa, w1f, 20, 4, finish1)
+        store_pair(xb, p, centre(xa, p) + moved)
+
+    layer(xa, w1f, 20, STEP, finish1)
 
     def finish2(p, total):
         tangent = jnp.tanh(total + bias2)
@@ -252,17 +249,20 @@
         moved = cell * tangent
         slope2[pair_rows(p), :] = (cell - moved * tangent).astype(BF)
         value = (centre(xb, p) + moved).astype(BF)
-        out_rows[pair_rows(2 * p), :] = value[:, :C]
-        out_rows[pair_rows(2 * p + 1), :] = value[:, C:]
-
-    layer(xb, w2f, 19, 4, finish2)
-    imitated[...] = out_rows[3 * C : 35 * C, :].reshape(ROWS, C, C)
+        for half in range(2):
+            row = 2 * p + half - 3
+            if 0 <= row < ROWS:
+                shown[row] = value[:, half * C : half * C + C]
+
+    layer(xb, w2f, 19, STEP, finish2)
+    copy = pltpu.make_async_copy(shown, imitated, sem)
+    copy.start()
 
     def sens_row(r):
         if r < 0:
-            return low[r + 9]
+            return low[(r + 9) * C : (r + 10) * C, :]
         if r >= ROWS:
-            return high[r - ROWS + 6]
+            return high[(r - ROWS + 6) * C : (r - ROWS + 7) * C, :]
         return sens[r]
 
     for p in range(19):
@@ -278,7 +278,7 @@
         grads[pair_rows(2 * p + 1), :] = total[:, C:]
         store_pair(xb, p, total * slope1[pair_rows(p + 1), :].astype(F32))
 
-    layer(xa, w2b, 18, 4, finish3)
+    layer(xa, w2b, 18, STEP, finish3)
 
     def finish4(p, total):
         total += two_rows(grads, 2 * p + 1)
@@ -286,7 +286,7 @@
         grad1[pair_rows(2 * p), :] = total[:, :C]
         grad1[pair_rows(2 * p + 1), :] = total[:, C:]
 
-    layer(xb, w1b, 17, 4, finish4)
+    layer(xb, w1b, 17, STEP, finish4)
     short = jnp.concatenate([lift[...].astype(F32), jnp.zeros((FP - F, C), F32)], axis=0).astype(BF)
     nt = (((1,), (1,)), ((), ()))
     for r in range(ROWS):
@@ -295,6 +295,7 @@
     ice[0:ROWS] = fine_dot(ice[0:ROWS].reshape(ROWS * FP, C), col_map[...], nt).reshape(ROWS, FP, C)
     for f in range(F):
         project[f * ROWS : (f + 1) * ROWS, :] = ice[0:ROWS, f, :].astype(BF)
+    copy.wait()
 
 
 def last_kernel(act0, grad1, weight, out, xp, taps):
@@ -307,7 +308,7 @@
         out[2 * p] = total[:, :C].astype(BF)
         out[2 * p + 1] = total[:, C:].astype(BF)
 
-    layer(xp, taps, 16, 4, finish)
+    layer(xp, taps, 16, STEP, finish)
 
 
 def scatter_kernel(planes, scatter, own, mate, *refs):
@@ -354,21 +355,36 @@
     def by_mate(step):
         return [(i, i ^ step) for i in range(count)]
 
+    def spread(array, above):
+        array = jnp.pad(array.T, ((K * above, K - K * above), (0, C - ROWS)))
+        return jnp.broadcast_to(array[None], (count, 2 * K, C))
+
+    ident = (spread(owner_device, 0) * 4 + spread(panel_slot, 0)) * 8 + spread(row_offset, 0)
+    table = ident.astype(F32) + spread(intersection_weight, 1)
+    ready = table
+    table = lax.all_to_all(table, "tile", 0, 0, tiled=True)
     fields = forcing.transpose(0, 2, 1, 3).reshape(F * ROWS, C)
     blocks = [fields] + [lax.ppermute(fields, "tile", by_plane(z)) for z in range(1, planes)]
-
-    ident = (owner_device * 4 + panel_slot) * 8 + row_offset
-    table = jnp.concatenate([ident.T.astype(F32), intersection_weight.T], axis=0)
-    table = jnp.pad(table, ((0, 0), (0, C - ROWS)))
-    table = jnp.broadcast_to(table[None], (count, 2 * K, C))
-    ready = table
-    table = lax.all_to_all(table, "tile", 0, 0, tiled=True)
     own_column = jnp.concatenate(blocks, axis=0)
     mate_column = lax.ppermute(own_column, "tile", by_mate(1))
 
-    cells = jnp.pad(ocean_mask, ((0, C - ROWS), (0, 0)))[None].astype(BF)
-    to_next = jnp.concatenate([ice_state[ROWS - 6 :], sensitivity[ROWS - 3 :], cells], axis=0)
-    to_last = jnp.concatenate([ice_state[:6], sensitivity[:3], cells], axis=0)
+    rows_sent = 9 * C + 2 * PAD
+
+    def window(array, start, size, place):
+        array = lax.slice_in_dim(array, start, start + size)
+        return jnp.pad(array, ((place, rows_sent - place - size), (0, 0)))
+
+    def edge(arrays, ice_row, sens_row, mask_row):
+        ice, sens, mask = arrays
+        return (
+            window(ice.reshape(ROWS * C, C), ice_row * C, 6 * C, 0)
+            + window(sens.reshape(ROWS * C, C), sens_row * C, 3 * C, 6 * C)
+            + jnp.where(window(mask, mask_row, PAD, 9 * C) == 1, 1.0, 0.0).astype(BF)
+        )
+
+    arrays = (ice_state, sensitivity, ocean_mask)
+    to_next = edge(arrays, ROWS - 6, ROWS - 3, ROWS - PAD)
+    to_last = edge(lax.optimization_barrier(arrays), 0, 0, 0)
     picks, scatter = pl.pallas_call(
         functools.partial(pick_kernel, planes),
         out_shape=(shape(SENT * EXT, 2 * planes * ROWS), shape(planes * ROWS, GROUP * ROWS)),
@@ -393,7 +409,7 @@
     hidden, slope0, ocean = pl.pallas_call(
         first_kernel,
         out_shape=(shape(21 * C, PAIR), shape(21 * C, PAIR), shape(42 * C, C)),
-        scratch_shapes=[pltpu.VMEM((22 * C, 2 * TAPS), BF), pltpu.VMEM((4 * TAPS, PAIR), BF)],
+        scratch_shapes=[pltpu.VMEM((22 * C, PAIR), BF), pltpu.VMEM((4 * C, 3 * PAIR), BF)],
         compiler_params=params(14),
         name="first_layer",
         cost_estimate=pl.CostEstimate(flops=4 * 10**9, bytes_accessed=8 * MIB, transcendentals=10**6),
@@ -407,19 +423,23 @@
             shape(34 * C, C, dtype=F32),
             shape(F * ROWS, C),
         ),
+        out_specs=(pl.BlockSpec(memory_space=pltpu.HBM),)
+        + (pl.BlockSpec(memory_space=pltpu.VMEM),) * 3,
         scratch_shapes=[
             pltpu.VMEM((EXT, FP, C), F32),
             pltpu.VMEM((EXT // GROUP * C, GROUP * C), F32),
             pltpu.VMEM((C, GROUP * C), BF),
-            pltpu.VMEM((21 * C, 2 * TAPS), BF),
-            pltpu.VMEM((20 * C, 2 * TAPS), BF),
+            pltpu.VMEM((21 * C, PAIR), BF),
+            pltpu.VMEM((20 * C, PAIR), BF),
             pltpu.VMEM((20 * C, PAIR), BF),
             pltpu.VMEM((19 * C, PAIR), BF),
             pltpu.VMEM((36 * C, C), F32),
             pltpu.VMEM((38 * C, C), BF),
             pltpu.VMEM((EXT // GROUP * C, C), BF),
+            pltpu.VMEM((ROWS, C, C), BF),
+            pltpu.SemaphoreType.DMA(()),
         ]
-        + [pltpu.VMEM((4 * TAPS, PAIR), BF)] * 4,
+        + [pltpu.VMEM((4 * C, 3 * PAIR), BF)] * 4,
         compiler_params=params(32),
         name="middle_layers",
         cost_estimate=pl.CostEstimate(flops=12 * 10**9, bytes_accessed=16 * MIB, transcendentals=10**6),
@@ -455,7 +475,7 @@
     state_grad = pl.pallas_call(
         last_kernel,
         out_shape=shape(ROWS, C, C),
-        scratch_shapes=[pltpu.VMEM((17 * C, 2 * TAPS), BF), pltpu.VMEM((4 * TAPS, PAIR), BF)],
+        scratch_shapes=[pltpu.VMEM((17 * C, PAIR), BF), pltpu.VMEM((4 * C, 3 * PAIR), BF)],
         compiler_params=params(14),
         name="last_adjoint",
         cost_estimate=pl.CostEstimate(flops=3 * 10**9, bytes_accessed=6 * MIB, transcendentals=0),

time: 71.4 us -> 65.8 us (0.922)
  Pallas kernels: 20.4 us -> 18 us
  local copies, waits for them, and re-layouts: 2.77 us -> 0.79 us
  other arithmetic: 3.78 us -> 2.33 us
  waiting for transfers between devices: 13.2 us -> 14.2 us
  starting transfers between devices: 30 us -> 29.2 us
    slice x2 -> x12, local copies, waits for them, and re-layouts: 2 us -> 0.04 us  [window(): array = lax.slice_in_dim(array, start, start + size)]
    pallas_call x1, Pallas kernels: 12.5 us -> 10.6 us  [body(): pl.pallas_call(main_kernel, out_shape=(shape(ROWS, C, C), shape(17 * C, P...]
    concatenate x2 -> x0, other arithmetic: 1.61 us -> none  [the longest x1 0.92 us: body(): to_last = jnp.concatenate([ice_state[:6], sensitivity[:3], cells], axis=0)]
    add x0 -> x2, other arithmetic: none -> 1.59 us  [the longest x1 0.85 us: edge(): window(ice.reshape(ROWS * C, C), ice_row * C, 6 * C, 0)]
    all_to_all x1, waiting for transfers between devices: 0.01 us -> 1.41 us  [body(): table = lax.all_to_all(table, 'tile', 0, 0, tiled=True)]
    ppermute x3, starting transfers between devices: 4.37 us -> 3.55 us  [body(): lax.ppermute(messages[s], 'tile', by_mate(2 * s))]
    another operation x1 -> x0, other arithmetic: 0.72 us -> none
    convert_element_type x1 -> x0, other arithmetic: 0.72 us -> none  [body(): ident.T.astype(F32)]
  transfers between devices with their start and end apart: 17 -> 17, of which waited for: 6 -> 6; matrix products, arithmetic and copies ran while one was open for 8% -> 4% of each run, Pallas kernels for 11% -> 11%
where the time goes in v2:
time: 65.8 us; the launch traced here: 65.5 us
  starting transfers between devices  29.2 us (44%)
  Pallas kernels  18 us (27%)
  waiting for transfers between devices  14.2 us (22%)
  other arithmetic  2.33 us (4%)
  between operations  0.95 us (1%)
  local copies, waits for them, and re-layouts  0.79 us (1%)
    pallas_call x1, Pallas kernels, body(): pl.pallas_call(main_kernel, out_shape=(shape(ROWS, C, C), shape(17 * C, P...  10.6 us
    ppermute x3, starting transfers between devices, body(): lax.ppermute(fields, 'tile', by_plane(z))  6.12 us
    all_to_all x1, starting transfers between devices, body(): table = lax.all_to_all(table, 'tile', 0, 0, tiled=True)  5.06 us
    ppermute x3, starting transfers between devices, body(): lax.ppermute(sums[z], 'tile', by_plane(-z))  4.58 us
    ppermute x3, starting transfers between devices, body(): lax.ppermute(project, 'tile', by_mate(2 * s))  4.07 us
    ppermute x3, waiting for transfers between devices, body(): lax.ppermute(sums[z], 'tile', by_plane(-z))  4.05 us
    ppermute x3, waiting for transfers between devices, body(): lax.ppermute(project, 'tile', by_mate(2 * s))  3.8 us
    ppermute x3, starting transfers between devices, body(): lax.ppermute(messages[s], 'tile', by_mate(2 * s))  3.55 us
  transfers between devices with their start and end apart: 17, of which 6 were waited for; matrix products, arithmetic and copies ran while one was open for 4% of the time, Pallas kernels for 11%

profile of v2, /device:TPU:0, one launch (start us, length us, event | category | flops | bytes accessed | tf_op | source)
XLA Modules:
  0.0 65.5 jit_solution(15609436895363343327)
XLA Ops:
  0.6 0.0 slice-start.4
  0.7 0.0 slice-start
  0.7 5.1 %collective-permute-start.2 = (bf16[320,128]{1,0:T(8,128)(2,1)}, bf16[320,128]{1,0:T(8,128)(2,1)S(1)}, u32[]{:S(2)}, u32[]{:S(2)}) collective-permute-start(bf16[320,128]{1,0:T(8,128)(2,1)} %bitcast.19), channel_id=1, source_target_pairs={{0,24},{1,25},{2,26},{3,27},{4,28},{5,29},{6,30},{7,31},{8,0},{9,1... | collective-permute-start | bytes 245768 | tf_op jit(solution)/shard_map/ppermute | solution.py:367
  5.8 1.0 %collective-permute-start = (bf16[320,128]{1,0:T(8,128)(2,1)}, bf16[320,128]{1,0:T(8,128)(2,1)S(1)}, u32[]{:S(2)}, u32[]{:S(2)}) collective-permute-start(bf16[320,128]{1,0:T(8,128)(2,1)} %bitcast.21), channel_id=1, source_target_pairs={{0,8},{1,9},{2,10},{3,11},{4,12},{5,13},{6,14},{7,15},{8,16},{9,17... | collective-permute-start | bytes 245768 | tf_op jit(solution)/shard_map/ppermute | solution.py:367
  6.8 0.7 %pad_add_fusion = f32[8,128]{1,0:T(8,128)S(1)} fusion(f32[4,32]{1,0:T(4,128)} %bitcast.23, s32[4,32]{1,0:T(4,128)} %bitcast.24, s32[4,32]{1,0:T(4,128)} %bitcast.25, s32[4,32]{1,0:T(4,128)} %bitcast.26), kind=kLoop, calls=%fused_computation.12 | loop fusion | flops 6144 | bytes 6144 | tf_op jit(solution)/shard_map/add | solution.py:363
  7.6 0.7 %broadcast_in_dim.10 = f32[32,8,128]{2,1,0:T(8,128)} broadcast(f32[8,128]{1,0:T(8,128)S(1)} %pad_add_fusion), dimensions={1,2} | broadcast | bytes 135168 | tf_op jit(solution)/shard_map/broadcast_in_dim | solution.py:360
  8.2 5.1 %all-to-all-start = ((f32[32,8,128]{2,1,0:T(8,128)}), f32[32,8,128]{2,1,0:T(8,128)S(1)}, u32[]{:S(2)}, u32[]{:S(2)}) async-start(f32[32,8,128]{2,1,0:T(8,128)} %broadcast_in_dim.10), calls=%async_computation | async-start | bytes 262144 | tf_op jit(solution)/shard_map/all_to_all | solution.py:365
  13.4 0.9 %fusion = (bf16[1168,128]{1,0:T(8,128)(2,1)}, bf16[1168,128]{1,0:T(8,128)(2,1)}) fusion(s32[8,128]{1,0:T(8,128)S(1)} %slice-done.4, bf16[384,128]{1,0:T(8,128)(2,1)S(1)} %bitcast.16, bf16[768,128]{1,0:T(8,128)(2,1)S(1)} %bitcast.14, s32[8,128]{1,0:T(8,128)S(1)} %slice-done.5, bf16[384,128]{1,0:T(8,128)(2,1)S(1)} %bitcast.17, bf16[768,128]{1,0:T(8,128)(2,1)S(1)} %bitcast.15), kind=kLoop, calls=%fused_computation.5 | loop fusion | flops 2691072 | bytes 1196032 | tf_op jit(solution)/shard_map/add | solution.py:380
  14.2 2.2 %collective-permute-start.7 = (bf16[1168,128]{1,0:T(8,128)(2,1)}, bf16[1168,128]{1,0:T(8,128)(2,1)S(1)}, u32[]{:S(2)}, u32[]{:S(2)}) collective-permute-start(bf16[1168,128]{1,0:T(8,128)(2,1)} %get-tuple-element.38), channel_id=1, source_target_pairs={{0,1},{1,2},{2,3},{3,4},{4,5},{5,6},{6,7},{7,8},{8,9},{9,10},{10,1... | collective-permute-start | bytes 897032 | tf_op jit(solution)/shard_map/ppermute | solution.py:404
  16.4 1.3 %collective-permute-start.8 = (bf16[1168,128]{1,0:T(8,128)(2,1)}, bf16[1168,128]{1,0:T(8,128)(2,1)S(1)}, u32[]{:S(2)}, u32[]{:S(2)}) collective-permute-start(bf16[1168,128]{1,0:T(8,128)(2,1)} %get-tuple-element.39), channel_id=1, source_target_pairs={{1,0},{2,1},{3,2},{4,3},{5,4},{6,5},{7,6},{8,7},{9,8},{10,9},{11,1... | collective-permute-start | bytes 897032 | tf_op jit(solution)/shard_map/ppermute | solution.py:405
  17.8 2.3 %collective-permute-start.3 = (bf16[1280,128]{1,0:T(8,128)(2,1)S(1)}, bf16[1280,128]{1,0:T(8,128)(2,1)S(1)}, u32[]{:S(2)}, u32[]{:S(2)}) collective-permute-start(bf16[1280,128]{1,0:T(8,128)(2,1)S(1)} %pad_maximum_fusion.own), channel_id=1, source_target_pairs={{0,1},{1,0},{2,3},{3,2},{4,5},{5,4},{6,7},{7,6},{8,9},{9,8},{10,11... | collective-permute-start | bytes 983048 | tf_op jit(solution)/shard_map/ppermute | solution.py:369
  20.1 1.4 %all-to-all-done.table = f32[32,8,128]{2,1,0:T(8,128)S(1)} async-done(((f32[32,8,128]{2,1,0:T(8,128)}), f32[32,8,128]{2,1,0:T(8,128)S(1)}, u32[]{:S(2)}, u32[]{:S(2)}) %all-to-all-start) | async-done | bytes 131104 | tf_op jit(solution)/shard_map/all_to_all | solution.py:365
  21.5 0.9 %picks.1 = (bf16[192,256]{1,0:T(8,128)(2,1)S(1)}, bf16[128,256]{1,0:T(8,128)(2,1)S(1)}) custom-call(f32[32,8,128]{2,1,0:T(8,128)S(1)} %all-to-all-done.table), custom_call_target="tpu_custom_call" | custom-call | flops 10000000000 | bytes 1048576 | tf_op jit(solution)/shard_map/picks/pallas_call | solution.py:388
  22.4 0.5 messages.1
  22.9 1.0 %collective-permute-start.4 = (bf16[480,128]{1,0:T(8,128)(2,1)S(1)}, bf16[480,128]{1,0:T(8,128)(2,1)S(1)}, u32[]{:S(2)}, u32[]{:S(2)}) collective-permute-start(bf16[480,128]{1,0:T(8,128)(2,1)S(1)} %get-tuple-element.32), channel_id=1, source_target_pairs={{0,2},{1,3},{2,0},{3,1},{4,6},{5,7},{6,4},{7,5},{8,10},{9,11},{10,... | collective-permute-start | bytes 368648 | tf_op jit(solution)/shard_map/ppermute | solution.py:407
  23.9 1.5 %collective-permute-start.5 = (bf16[480,128]{1,0:T(8,128)(2,1)S(1)}, bf16[480,128]{1,0:T(8,128)(2,1)S(1)}, u32[]{:S(2)}, u32[]{:S(2)}) collective-permute-start(bf16[480,128]{1,0:T(8,128)(2,1)S(1)} %get-tuple-element.33), channel_id=1, source_target_pairs={{0,4},{1,5},{2,6},{3,7},{4,0},{5,1},{6,2},{7,3},{8,12},{9,13},{10,... | collective-permute-start | bytes 368648 | tf_op jit(solution)/shard_map/ppermute | solution.py:407
  25.4 1.1 %collective-permute-start.6 = (bf16[480,128]{1,0:T(8,128)(2,1)S(1)}, bf16[480,128]{1,0:T(8,128)(2,1)S(1)}, u32[]{:S(2)}, u32[]{:S(2)}) collective-permute-start(bf16[480,128]{1,0:T(8,128)(2,1)S(1)} %get-tuple-element.34), channel_id=1, source_target_pairs={{0,6},{1,7},{2,4},{3,5},{4,2},{5,3},{6,0},{7,1},{8,14},{9,15},{10,... | collective-permute-start | bytes 368648 | tf_op jit(solution)/shard_map/ppermute | solution.py:407
  26.5 2.8 %first_layer.1 = (bf16[2688,256]{1,0:T(8,128)(2,1)S(1)}, bf16[2688,256]{1,0:T(8,128)(2,1)S(1)}, bf16[5376,128]{1,0:T(8,128)(2,1)S(1)}) custom-call(bf16[32,128,128]{2,1,0:T(8,128)(2,1)S(1)} %copy-done, bf16[1168,128]{1,0:T(8,128)(2,1)S(1)} %collective-permute-done.7.low.refs_11_, bf16[1168,128]{1,0:T(8,128)(2,1)S(1)} %collective-permute-done.8.high.refs_12_, ...), custom_call_target="tpu_custom_call" | custom-call | flops 4000000000 | bytes 8388608 | tf_op jit(solution)/shard_map/first_layer/pallas_call | solution.py:409
  29.3 1.4 %collective-permute-done.4.refs_1_ = bf16[480,128]{1,0:T(8,128)(2,1)S(1)} collective-permute-done((bf16[480,128]{1,0:T(8,128)(2,1)S(1)}, bf16[480,128]{1,0:T(8,128)(2,1)S(1)}, u32[]{:S(2)}, u32[]{:S(2)}) %collective-permute-start.4) | collective-permute-done | bytes 122912 | tf_op jit(solution)/shard_map/ppermute | solution.py:407
  30.7 1.9 %collective-permute-done.6.refs_3_ = bf16[480,128]{1,0:T(8,128)(2,1)S(1)} collective-permute-done((bf16[480,128]{1,0:T(8,128)(2,1)S(1)}, bf16[480,128]{1,0:T(8,128)(2,1)S(1)}, u32[]{:S(2)}, u32[]{:S(2)}) %collective-permute-start.6) | collective-permute-done | bytes 122912 | tf_op jit(solution)/shard_map/ppermute | solution.py:407
  32.7 10.6 %middle_layers.1 = (bf16[32,128,128]{2,1,0:T(8,128)(2,1)}, bf16[2176,256]{1,0:T(8,128)(2,1)S(1)}, f32[4352,128]{1,0:T(8,128)S(1)}, bf16[320,128]{1,0:T(8,128)(2,1)S(1)}) custom-call(bf16[480,128]{1,0:T(8,128)(2,1)S(1)} %get-tuple-element.31.refs_0_, bf16[480,128]{1,0:T(8,128)(2,1)S(1)} %collective-permute-done.4.refs_1_, ...), custom_call_target="tpu_custom_call" | custom-call | flops 12000000000 | bytes 16777216 | tf_op jit(solution)/shard_map/middle_layers/pallas_call | solution.py:418
  43.2 3.4 %collective-permute-start.11 = (bf16[320,128]{1,0:T(8,128)(2,1)S(1)}, bf16[320,128]{1,0:T(8,128)(2,1)S(1)}, u32[]{:S(2)}, u32[]{:S(2)}) collective-permute-start(bf16[320,128]{1,0:T(8,128)(2,1)S(1)} %get-tuple-element.46), channel_id=1, source_target_pairs={{0,6},{1,7},{2,4},{3,5},{4,2},{5,3},{6,0},{7,1},{8,14},{9,15},{10,... | collective-permute-start | bytes 245768 | tf_op jit(solution)/shard_map/ppermute | solution.py:459
  46.7 0.6 collective-permute-start.9
  47.3 3.8 %collective-permute-done.9 = bf16[320,128]{1,0:T(8,128)(2,1)S(1)} collective-permute-done((bf16[320,128]{1,0:T(8,128)(2,1)S(1)}, bf16[320,128]{1,0:T(8,128)(2,1)S(1)}, u32[]{:S(2)}, u32[]{:S(2)}) %collective-permute-start.9) | collective-permute-done | bytes 81952 | tf_op jit(solution)/shard_map/ppermute | solution.py:459
  51.2 0.1 collective-permute-start.12
  51.3 1.6 %collective-permute-done.12.mate = bf16[1280,128]{1,0:T(8,128)(2,1)S(1)} collective-permute-done((bf16[1280,128]{1,0:T(8,128)(2,1)S(1)}, bf16[1280,128]{1,0:T(8,128)(2,1)S(1)}, u32[]{:S(2)}, u32[]{:S(2)}) %collective-permute-start.12) | collective-permute-done | bytes 327712 | tf_op jit(solution)/shard_map/ppermute | solution.py:461
  52.9 0.4 scatter.1
  53.3 3.5 %collective-permute-start.13 = (bf16[320,128]{1,0:T(8,128)(2,1)S(1)}, bf16[320,128]{1,0:T(8,128)(2,1)S(1)}, u32[]{:S(2)}, u32[]{:S(2)}) collective-permute-start(bf16[320,128]{1,0:T(8,128)(2,1)S(1)} %get-tuple-element.54), channel_id=1, source_target_pairs={{0,24},{1,25},{2,26},{3,27},{4,28},{5,29},{6,30},{7,31},{8,0},{9,1... | collective-permute-start | bytes 245768 | tf_op jit(solution)/shard_map/ppermute | solution.py:474
  56.8 1.1 %collective-permute-start.15 = (bf16[320,128]{1,0:T(8,128)(2,1)S(1)}, bf16[320,128]{1,0:T(8,128)(2,1)S(1)}, u32[]{:S(2)}, u32[]{:S(2)}) collective-permute-start(bf16[320,128]{1,0:T(8,128)(2,1)S(1)} %get-tuple-element.56), channel_id=1, source_target_pairs={{0,8},{1,9},{2,10},{3,11},{4,12},{5,13},{6,14},{7,15},{8,16},{9,17... | collective-permute-start | bytes 245768 | tf_op jit(solution)/shard_map/ppermute | solution.py:474
  57.8 2.9 %last_adjoint.1 = bf16[32,128,128]{2,1,0:T(8,128)(2,1)} custom-call(bf16[2176,256]{1,0:T(8,128)(2,1)S(1)} %get-tuple-element.51.act0, f32[4352,128]{1,0:T(8,128)S(1)} %get-tuple-element.52.grad1, bf16[3,3,3,128,128]{4,3,2,1,0:T(8,128)(2,1)S(1)} %copy-done.3), custom_call_target="tpu_custom_call" | custom-call | flops 3000000000 | bytes 6291456 | tf_op jit(solution)/shard_map/last_adjoint/pallas_call | solution.py:475
  60.7 4.0 %collective-permute-done.14 = bf16[320,128]{1,0:T(8,128)(2,1)S(1)} collective-permute-done((bf16[320,128]{1,0:T(8,128)(2,1)S(1)}, bf16[320,128]{1,0:T(8,128)(2,1)S(1)}, u32[]{:S(2)}, u32[]{:S(2)}) %collective-permute-start.14) | collective-permute-done | bytes 81952 | tf_op jit(solution)/shard_map/ppermute | solution.py:474
  64.8 0.7 %convert_add_fusion = f32[320,128]{1,0:T(8,128)} fusion(bf16[320,128]{1,0:T(8,128)(2,1)S(1)} %collective-permute-done.15, bf16[320,128]{1,0:T(8,128)(2,1)S(1)} %collective-permute-done.14, bf16[320,128]{1,0:T(8,128)(2,1)S(1)} %collective-permute-done.13, bf16[320,128]{1,0:T(8,128)(2,1)S(1)} %get-tuple-element.53), kind=kLoop, calls=%fused_computation.7 | loop fusion | flops 286720 | bytes 491520 | tf_op jit(solution)/shard_map/add | solution.py:484
  (45 shorter events, 0.2 us)
Async XLA Ops:
  0.6 12.7 %slice-start.4 = ((s32[32,128]{1,0:T(8,128)}), s32[8,128]{1,0:T(8,128)S(1)}, s32[]{:S(2)}) async-start(s32[32,128]{1,0:T(8,128)} %mask.1), calls=%async_computation.5 | async-start | bytes 8192 | tf_op jit(solution)/shard_map/slice | solution.py:374
  0.6 12.7 %slice-start.5 = ((s32[32,128]{1,0:T(8,128)}), s32[8,128]{1,0:T(8,128)S(1)}, s32[]{:S(2)}) async-start(s32[32,128]{1,0:T(8,128)} %mask.1), calls=%async_computation.6 | async-start | bytes 8192 | tf_op jit(solution)/shard_map/slice | solution.py:374
  0.7 12.7 %slice-start.2 = ((bf16[32,128,128]{2,1,0:T(8,128)(2,1)}), bf16[3,128,128]{2,1,0:T(8,128)(2,1)S(1)}, s32[]{:S(2)}) async-start(bf16[32,128,128]{2,1,0:T(8,128)(2,1)} %refs_10_.1), calls=%async_computation.3 | async-start | bytes 196608 | tf_op jit(solution)/shard_map/slice | solution.py:374
  0.7 12.7 %slice-start.3 = ((bf16[32,128,128]{2,1,0:T(8,128)(2,1)}), bf16[3,128,128]{2,1,0:T(8,128)(2,1)S(1)}, s32[]{:S(2)}) async-start(bf16[32,128,128]{2,1,0:T(8,128)(2,1)} %refs_10_.1), calls=%async_computation.4 | async-start | bytes 196608 | tf_op jit(solution)/shard_map/slice | solution.py:374
  0.7 12.7 %slice-start = ((bf16[32,128,128]{2,1,0:T(8,128)(2,1)}), bf16[6,128,128]{2,1,0:T(8,128)(2,1)S(1)}, s32[]{:S(2)}) async-start(bf16[32,128,128]{2,1,0:T(8,128)(2,1)} %ice.1), calls=%async_computation.1 | async-start | bytes 393216 | tf_op jit(solution)/shard_map/slice | solution.py:374
  0.7 12.7 %slice-start.1 = ((bf16[32,128,128]{2,1,0:T(8,128)(2,1)}), bf16[6,128,128]{2,1,0:T(8,128)(2,1)S(1)}, s32[]{:S(2)}) async-start(bf16[32,128,128]{2,1,0:T(8,128)(2,1)} %ice.1), calls=%async_computation.2 | async-start | bytes 393216 | tf_op jit(solution)/shard_map/slice | solution.py:374
  0.7 17.0 %collective-permute-start.2 = (bf16[320,128]{1,0:T(8,128)(2,1)}, bf16[320,128]{1,0:T(8,128)(2,1)S(1)}, u32[]{:S(2)}, u32[]{:S(2)}) collective-permute-start(bf16[320,128]{1,0:T(8,128)(2,1)} %bitcast.19), channel_id=1, source_target_pairs={{0,24},{1,25},{2,26},{3,27},{4,28},{5,29},{6,30},{7,31},{8,0},{9,1... | collective-permute-start | bytes 245768 | tf_op jit(solution)/shard_map/ppermute | solution.py:367
  5.8 11.9 %collective-permute-start.1 = (bf16[320,128]{1,0:T(8,128)(2,1)}, bf16[320,128]{1,0:T(8,128)(2,1)S(1)}, u32[]{:S(2)}, u32[]{:S(2)}) collective-permute-start(bf16[320,128]{1,0:T(8,128)(2,1)} %bitcast.20), channel_id=1, source_target_pairs={{0,16},{1,17},{2,18},{3,19},{4,20},{5,21},{6,22},{7,23},{8,24},{9,... | collective-permute-start | bytes 245768 | tf_op jit(solution)/shard_map/ppermute | solution.py:367
  5.8 11.9 %collective-permute-start = (bf16[320,128]{1,0:T(8,128)(2,1)}, bf16[320,128]{1,0:T(8,128)(2,1)S(1)}, u32[]{:S(2)}, u32[]{:S(2)}) collective-permute-start(bf16[320,128]{1,0:T(8,128)(2,1)} %bitcast.21), channel_id=1, source_target_pairs={{0,8},{1,9},{2,10},{3,11},{4,12},{5,13},{6,14},{7,15},{8,16},{9,17... | collective-permute-start | bytes 245768 | tf_op jit(solution)/shard_map/ppermute | solution.py:367
  7.6 10.2 %copy-start.7 = (bf16[4,8,10,128]{3,1,2,0:T(8,128)(2,1)S(1)}, bf16[4,8,10,128]{3,1,2,0:T(8,128)(2,1)}, u32[]{:S(2)}) copy-start(bf16[4,8,10,128]{3,1,2,0:T(8,128)(2,1)} %param.12) | copy-start | bytes 245764
  8.2 13.3 %all-to-all-start = ((f32[32,8,128]{2,1,0:T(8,128)}), f32[32,8,128]{2,1,0:T(8,128)S(1)}, u32[]{:S(2)}, u32[]{:S(2)}) async-start(f32[32,8,128]{2,1,0:T(8,128)} %broadcast_in_dim.10), calls=%async_computation | async-start | bytes 262144 | tf_op jit(solution)/shard_map/all_to_all | solution.py:365
  14.2 12.3 %collective-permute-start.7 = (bf16[1168,128]{1,0:T(8,128)(2,1)}, bf16[1168,128]{1,0:T(8,128)(2,1)S(1)}, u32[]{:S(2)}, u32[]{:S(2)}) collective-permute-start(bf16[1168,128]{1,0:T(8,128)(2,1)} %get-tuple-element.38), channel_id=1, source_target_pairs={{0,1},{1,2},{2,3},{3,4},{4,5},{5,6},{6,7},{7,8},{8,9},{9,10},{10,1... | collective-permute-start | bytes 897032 | tf_op jit(solution)/shard_map/ppermute | solution.py:404
  16.4 10.1 %collective-permute-start.8 = (bf16[1168,128]{1,0:T(8,128)(2,1)}, bf16[1168,128]{1,0:T(8,128)(2,1)S(1)}, u32[]{:S(2)}, u32[]{:S(2)}) collective-permute-start(bf16[1168,128]{1,0:T(8,128)(2,1)} %get-tuple-element.39), channel_id=1, source_target_pairs={{1,0},{2,1},{3,2},{4,3},{5,4},{6,5},{7,6},{8,7},{9,8},{10,9},{11,1... | collective-permute-start | bytes 897032 | tf_op jit(solution)/shard_map/ppermute | solution.py:405
  17.8 8.7 %copy-start = (bf16[32,128,128]{2,1,0:T(8,128)(2,1)S(1)}, bf16[32,128,128]{2,1,0:T(8,128)(2,1)}, u32[]{:S(2)}) copy-start(bf16[32,128,128]{2,1,0:T(8,128)(2,1)} %ice.1) | copy-start | bytes 3145732
  17.8 8.7 %copy-start.2 = (s32[32,128]{1,0:T(8,128)S(1)}, s32[32,128]{1,0:T(8,128)}, u32[]{:S(2)}) copy-start(s32[32,128]{1,0:T(8,128)} %mask.1) | copy-start | bytes 49156
  17.8 8.7 %copy-start.3 = (bf16[3,3,3,128,128]{4,3,2,1,0:T(8,128)(2,1)S(1)}, bf16[3,3,3,128,128]{4,3,2,1,0:T(8,128)(2,1)}, u32[]{:S(2)}) copy-start(bf16[3,3,3,128,128]{4,3,2,1,0:T(8,128)(2,1)} %weight.3) | copy-start | bytes 2654212
  17.8 8.7 %copy-start.6 = (f32[3,128]{1,0:T(4,128)S(1)}, f32[3,128]{1,0:T(4,128)}, u32[]{:S(2)}) copy-start(f32[3,128]{1,0:T(4,128)} %refs_6_.1) | copy-start | bytes 4612
  17.8 4.6 %collective-permute-start.3 = (bf16[1280,128]{1,0:T(8,128)(2,1)S(1)}, bf16[1280,128]{1,0:T(8,128)(2,1)S(1)}, u32[]{:S(2)}, u32[]{:S(2)}) collective-permute-start(bf16[1280,128]{1,0:T(8,128)(2,1)S(1)} %pad_maximum_fusion.own), channel_id=1, source_target_pairs={{0,1},{1,0},{2,3},{3,2},{4,5},{5,4},{6,7},{7,6},{8,9},{9,8},{10,11... | collective-permute-start | bytes 983048 | tf_op jit(solution)/shard_map/ppermute | solution.py:369
  22.9 7.8 %collective-permute-start.4 = (bf16[480,128]{1,0:T(8,128)(2,1)S(1)}, bf16[480,128]{1,0:T(8,128)(2,1)S(1)}, u32[]{:S(2)}, u32[]{:S(2)}) collective-permute-start(bf16[480,128]{1,0:T(8,128)(2,1)S(1)} %get-tuple-element.32), channel_id=1, source_target_pairs={{0,2},{1,3},{2,0},{3,1},{4,6},{5,7},{6,4},{7,5},{8,10},{9,11},{10,... | collective-permute-start | bytes 368648 | tf_op jit(solution)/shard_map/ppermute | solution.py:407
  23.9 6.8 %collective-permute-start.5 = (bf16[480,128]{1,0:T(8,128)(2,1)S(1)}, bf16[480,128]{1,0:T(8,128)(2,1)S(1)}, u32[]{:S(2)}, u32[]{:S(2)}) collective-permute-start(bf16[480,128]{1,0:T(8,128)(2,1)S(1)} %get-tuple-element.33), channel_id=1, source_target_pairs={{0,4},{1,5},{2,6},{3,7},{4,0},{5,1},{6,2},{7,3},{8,12},{9,13},{10,... | collective-permute-start | bytes 368648 | tf_op jit(solution)/shard_map/ppermute | solution.py:407
  25.4 7.3 %copy-start.1 = (bf16[32,128,128]{2,1,0:T(8,128)(2,1)S(1)}, bf16[32,128,128]{2,1,0:T(8,128)(2,1)}, u32[]{:S(2)}) copy-start(bf16[32,128,128]{2,1,0:T(8,128)(2,1)} %refs_10_.1) | copy-start | bytes 3145732
  25.4 7.3 %copy-start.4 = (f32[128,128]{1,0:T(8,128)S(1)}, f32[128,128]{1,0:T(8,128)}, u32[]{:S(2)}) copy-start(f32[128,128]{1,0:T(8,128)} %refs_4_.1) | copy-start | bytes 196612
  25.4 7.3 %copy-start.5 = (bf16[10,128]{1,0:T(8,128)(2,1)S(1)}, bf16[10,128]{1,0:T(8,128)(2,1)}, u32[]{:S(2)}) copy-start(bf16[10,128]{1,0:T(8,128)(2,1)} %refs_5_.1) | copy-start | bytes 7684
  25.4 7.2 %collective-permute-start.6 = (bf16[480,128]{1,0:T(8,128)(2,1)S(1)}, bf16[480,128]{1,0:T(8,128)(2,1)S(1)}, u32[]{:S(2)}, u32[]{:S(2)}) collective-permute-start(bf16[480,128]{1,0:T(8,128)(2,1)S(1)} %get-tuple-element.34), channel_id=1, source_target_pairs={{0,6},{1,7},{2,4},{3,5},{4,2},{5,3},{6,0},{7,1},{8,14},{9,15},{10,... | collective-permute-start | bytes 368648 | tf_op jit(solution)/shard_map/ppermute | solution.py:407
  43.2 7.9 %collective-permute-start.11 = (bf16[320,128]{1,0:T(8,128)(2,1)S(1)}, bf16[320,128]{1,0:T(8,128)(2,1)S(1)}, u32[]{:S(2)}, u32[]{:S(2)}) collective-permute-start(bf16[320,128]{1,0:T(8,128)(2,1)S(1)} %get-tuple-element.46), channel_id=1, source_target_pairs={{0,6},{1,7},{2,4},{3,5},{4,2},{5,3},{6,0},{7,1},{8,14},{9,15},{10,... | collective-permute-start | bytes 245768 | tf_op jit(solution)/shard_map/ppermute | solution.py:459
  46.7 4.5 %collective-permute-start.10 = (bf16[320,128]{1,0:T(8,128)(2,1)S(1)}, bf16[320,128]{1,0:T(8,128)(2,1)S(1)}, u32[]{:S(2)}, u32[]{:S(2)}) collective-permute-start(bf16[320,128]{1,0:T(8,128)(2,1)S(1)} %get-tuple-element.46), channel_id=1, source_target_pairs={{0,4},{1,5},{2,6},{3,7},{4,0},{5,1},{6,2},{7,3},{8,12},{9,13},{10,... | collective-permute-start | bytes 245768 | tf_op jit(solution)/shard_map/ppermute | solution.py:459
  46.7 4.4 %collective-permute-start.9 = (bf16[320,128]{1,0:T(8,128)(2,1)S(1)}, bf16[320,128]{1,0:T(8,128)(2,1)S(1)}, u32[]{:S(2)}, u32[]{:S(2)}) collective-permute-start(bf16[320,128]{1,0:T(8,128)(2,1)S(1)} %get-tuple-element.46), channel_id=1, source_target_pairs={{0,2},{1,3},{2,0},{3,1},{4,6},{5,7},{6,4},{7,5},{8,10},{9,11},{10,... | collective-permute-start | bytes 245768 | tf_op jit(solution)/shard_map/ppermute | solution.py:459
  51.2 1.7 %collective-permute-start.12 = (bf16[1280,128]{1,0:T(8,128)(2,1)S(1)}, bf16[1280,128]{1,0:T(8,128)(2,1)S(1)}, u32[]{:S(2)}, u32[]{:S(2)}) collective-permute-start(bf16[1280,128]{1,0:T(8,128)(2,1)S(1)} %constant_dynamic-update-slice_fusion.own), channel_id=1, source_target_pairs={{0,1},{1,0},{2,3},{3,2},{4,5},{5,4},{6,7},{7,6},{8,9},{9,8},{10,11... | collective-permute-start | bytes 983048 | tf_op jit(solution)/shard_map/ppermute | solution.py:461
  53.3 7.5 %collective-permute-start.13 = (bf16[320,128]{1,0:T(8,128)(2,1)S(1)}, bf16[320,128]{1,0:T(8,128)(2,1)S(1)}, u32[]{:S(2)}, u32[]{:S(2)}) collective-permute-start(bf16[320,128]{1,0:T(8,128)(2,1)S(1)} %get-tuple-element.54), channel_id=1, source_target_pairs={{0,24},{1,25},{2,26},{3,27},{4,28},{5,29},{6,30},{7,31},{8,0},{9,1... | collective-permute-start | bytes 245768 | tf_op jit(solution)/shard_map/ppermute | solution.py:474
  56.8 8.0 %collective-permute-start.14 = (bf16[320,128]{1,0:T(8,128)(2,1)S(1)}, bf16[320,128]{1,0:T(8,128)(2,1)S(1)}, u32[]{:S(2)}, u32[]{:S(2)}) collective-permute-start(bf16[320,128]{1,0:T(8,128)(2,1)S(1)} %get-tuple-element.55), channel_id=1, source_target_pairs={{0,16},{1,17},{2,18},{3,19},{4,20},{5,21},{6,22},{7,23},{8,24},{9,... | collective-permute-start | bytes 245768 | tf_op jit(solution)/shard_map/ppermute | solution.py:474
  56.8 8.0 %collective-permute-start.15 = (bf16[320,128]{1,0:T(8,128)(2,1)S(1)}, bf16[320,128]{1,0:T(8,128)(2,1)S(1)}, u32[]{:S(2)}, u32[]{:S(2)}) collective-permute-start(bf16[320,128]{1,0:T(8,128)(2,1)S(1)} %get-tuple-element.56), channel_id=1, source_target_pairs={{0,8},{1,9},{2,10},{3,11},{4,12},{5,13},{6,14},{7,15},{8,16},{9,17... | collective-permute-start | bytes 245768 | tf_op jit(solution)/shard_map/ppermute | solution.py:474

commit v3 on v2

--- a/solution.py
+++ b/solution.py
@@ -113,7 +113,7 @@
     return ((from_plane * GROUP + from_spot) * ROWS + lane % ROWS).astype(F32)
 
 
-def pick_kernel(planes, table, picks, scatter):
+def pick_kernel(planes, table, picks):
     me = lax.axis_index("tile")
     plane, spot = me // GROUP, me % GROUP
     count = planes * GROUP
@@ -126,6 +126,11 @@
         inside = jnp.logical_and(device >= 0, device < count)
         parts.append(jnp.where(inside, picked(columns, place, ident, start, size), 0.0))
     picks[...] = jnp.concatenate(parts, axis=0).astype(BF)
+
+
+def matrix_kernel(planes, table, scatter):
+    me = lax.axis_index("tile")
+    plane, spot = me // GROUP, me % GROUP
     ident = source_ident(planes, plane, spot, 1)
     columns = column_tables(table, [plane * GROUP + (spot ^ s) for s in range(GROUP)])
     parts = [picked(columns, s, ident, 0, ROWS) for s in range(GROUP)]
@@ -162,22 +167,27 @@
                 taps[(a + half) * C : (a + half + 1) * C, start : start + C] = block
 
 
-def first_kernel(ice, low, high, mask, weight, bias, hidden, slope, ocean, xp, taps):
+def edge_rows(pair, other, start, size):
+    odd = lax.rem(lax.axis_index("tile"), 2) == 1
+    mine, next_one = pair[start : start + size, :].astype(F32), other[start : start + size, :].astype(F32)
+    return jnp.where(odd, mine, next_one), jnp.where(odd, next_one, mine)
+
+
+def first_kernel(ice, pair, other, mask, weight, bias, hidden, slope, ocean, xp, taps):
     fill_taps(taps, weight, 0, False)
 
     def ice_row(r):
         if r < 0:
-            return low[(r + 6) * C : (r + 7) * C, :]
+            return edge_rows(pair, other, (r + 6) * C, C)[0]
         if r >= ROWS:
-            return high[(r - ROWS) * C : (r - ROWS + 1) * C, :]
-        return ice[r]
+            return edge_rows(pair, other, (r - ROWS) * C, C)[1]
+        return ice[r].astype(F32)
 
     for p in range(22):
         row = 2 * p - 6
-        store_pair(xp, p, jnp.concatenate([ice_row(row), ice_row(row + 1)], axis=1).astype(F32))
-    before = low[9 * C : 9 * C + 2 * PAD, :].astype(F32)[:PAD]
-    after = high[9 * C : 9 * C + 2 * PAD, :].astype(F32)[:PAD]
-    cells = jnp.concatenate([before, mask[...].astype(F32), after], axis=0)
+        store_pair(xp, p, jnp.concatenate([ice_row(row), ice_row(row + 1)], axis=1))
+    before, after = edge_rows(pair, other, 9 * C, 2 * PAD)
+    cells = jnp.concatenate([before[:PAD], mask[...].astype(F32), after[:PAD]], axis=0)
     cells = jnp.concatenate([cells, jnp.zeros((C - EXT, C), F32)], axis=0).T
     for r in range(-5, 37):
         column = jnp.broadcast_to(cells[:, r + PAD : r + PAD + 1], (C, C))
@@ -196,7 +206,7 @@
 
 def main_kernel(*refs):
     messages = refs[:SENT]
-    (col_map, lift, bias, hidden, slope0, ocean, sens, low, high, weight) = refs[SENT : SENT + 10]
+    (col_map, lift, bias, hidden, slope0, ocean, sens, pair, other, weight) = refs[SENT : SENT + 10]
     imitated, act0, grad1, project = refs[SENT + 10 : SENT + 14]
     ice, lifted, diag, xa, xb, slope1, slope2, grads, out_rows, turned, shown, sem, *taps = refs[SENT + 14 :]
     w1f, w2f, w2b, w1b = taps
@@ -260,17 +270,17 @@
 
     def sens_row(r):
         if r < 0:
-            return low[(r + 9) * C : (r + 10) * C, :]
+            return edge_rows(pair, other, (r + 9) * C, C)[0]
         if r >= ROWS:
-            return high[(r - ROWS + 6) * C : (r - ROWS + 7) * C, :]
-        return sens[r]
+            return edge_rows(pair, other, (r - ROWS + 6) * C, C)[1]
+        return sens[r].astype(F32)
 
     for p in range(19):
         row = 2 * p - 3
-        value = jnp.concatenate([sens_row(row), sens_row(row + 1)], axis=1).astype(F32)
+        value = jnp.concatenate([sens_row(row), sens_row(row + 1)], axis=1)
         store_pair(xa, p, value * slope2[pair_rows(p), :].astype(F32))
-        out_rows[pair_rows(2 * p), :] = sens_row(row)
-        out_rows[pair_rows(2 * p + 1), :] = sens_row(row + 1)
+        out_rows[pair_rows(2 * p), :] = value[:, :C].astype(BF)
+        out_rows[pair_rows(2 * p + 1), :] = value[:, C:].astype(BF)
 
     def finish3(p, total):
         total += two_rows(out_rows, 2 * p + 1)
@@ -385,9 +395,9 @@
     arrays = (ice_state, sensitivity, ocean_mask)
     to_next = edge(arrays, ROWS - 6, ROWS - 3, ROWS - PAD)
     to_last = edge(lax.optimization_barrier(arrays), 0, 0, 0)
-    picks, scatter = pl.pallas_call(
+    picks = pl.pallas_call(
         functools.partial(pick_kernel, planes),
-        out_shape=(shape(SENT * EXT, 2 * planes * ROWS), shape(planes * ROWS, GROUP * ROWS)),
+        out_shape=shape(SENT * EXT, 2 * planes * ROWS),
         compiler_params=params(4),
         name="picks",
         cost_estimate=pl.CostEstimate(flops=10**10, bytes_accessed=MIB, transcendentals=0),
@@ -399,10 +409,12 @@
         compiler_params=params(10),
         name="messages",
     )(picks, own_column, mate_column)
-    to_next, to_last, _ = lax.optimization_barrier((to_next, to_last, ready))
-    forward = [(i, i + 1) for i in range(count - 1)]
-    low = lax.ppermute(to_next, "tile", forward)
-    high = lax.ppermute(to_last, "tile", [(b, a) for a, b in forward])
+    odd = lax.rem(lax.axis_index("tile"), 2) == 1
+    to_pair, to_other = jnp.where(odd, to_last, to_next), jnp.where(odd, to_next, to_last)
+    to_pair, to_other, _ = lax.optimization_barrier((to_pair, to_other, ready))
+    pair = lax.ppermute(to_pair, "tile", by_mate(1))
+    across = [(i, i + 1) for i in range(1, count - 1, 2)]
+    other = lax.ppermute(to_other, "tile", across + [(b, a) for a, b in across])
     messages = [messages[0]] + [
         lax.ppermute(messages[s], "tile", by_mate(2 * s)) for s in range(1, SENT)
     ]
@@ -413,7 +425,7 @@
         compiler_params=params(14),
         name="first_layer",
         cost_estimate=pl.CostEstimate(flops=4 * 10**9, bytes_accessed=8 * MIB, transcendentals=10**6),
-    )(ice_state, low, high, ocean_mask, conv_weight, conv_bias)
+    )(ice_state, pair, other, ocean_mask, conv_weight, conv_bias)
 
     imitated, act0, grad1, project = pl.pallas_call(
         main_kernel,
@@ -452,10 +464,18 @@
         slope0,
         ocean,
         sensitivity,
-        low,
-        high,
+        pair,
+        other,
         conv_weight,
     )
+    table, project = lax.optimization_barrier((table, project))
+    scatter = pl.pallas_call(
+        functools.partial(matrix_kernel, planes),
+        out_shape=shape(planes * ROWS, GROUP * ROWS),
+        compiler_params=params(4),
+        name="matrix",
+        cost_estimate=pl.CostEstimate(flops=10**9, bytes_accessed=MIB, transcendentals=0),
+    )(table)
     projects = [project] + [lax.ppermute(project, "tile", by_mate(2 * s)) for s in range(1, SENT)]
     own_projects = jnp.concatenate(projects, axis=0)
     mate_projects = lax.ppermute(own_projects, "tile", by_mate(1))

time: 65.8 us -> 65.5 us (level)
  starting transfers between devices: 29.2 us -> 27.9 us
  Pallas kernels: 18 us -> 18.8 us
    ppermute x2, starting transfers between devices: 3.45 us -> 0.92 us  [the longest x1 0.67 us: body(): other = lax.ppermute(to_other, 'tile', across + [(b, a) for a, b in across])]
    all_to_all x1, waiting for transfers between devices: 1.41 us -> 3.21 us  [body(): table = lax.all_to_all(table, 'tile', 0, 0, tiled=True)]
    ppermute x3, waiting for transfers between devices: 3.33 us -> 1.59 us  [body(): lax.ppermute(messages[s], 'tile', by_mate(2 * s))]
    select_n x0 -> x1, other arithmetic: none -> 0.94 us  [body(): jnp.where(odd, to_next, to_last)]
    add x1 -> x0, other arithmetic: 0.85 us -> none  [edge(): window(ice.reshape(ROWS * C, C), ice_row * C, 6 * C, 0)]
    ppermute x1, starting transfers between devices: 2.31 us -> 3.07 us  [body(): mate_column = lax.ppermute(own_column, 'tile', by_mate(1))]
  transfers between devices with their start and end apart: 17 -> 17, of which waited for: 6 -> 5; matrix products, arithmetic and copies ran while one was open for 4% -> 4% of each run, Pallas kernels for 11% -> 11%
where the time goes in v3:
time: 65.5 us; the launch traced here: 65.2 us
  starting transfers between devices  27.9 us (43%)
  Pallas kernels  18.8 us (29%)
  waiting for transfers between devices  14.3 us (22%)
  other arithmetic  2.41 us (4%)
  between operations  0.96 us (1%)
  local copies, waits for them, and re-layouts  0.79 us (1%)
    pallas_call x1, Pallas kernels, body(): pl.pallas_call(main_kernel, out_shape=(shape(ROWS, C, C), shape(17 * C, P...  11.1 us
    ppermute x3, starting transfers between devices, body(): lax.ppermute(fields, 'tile', by_plane(z))  6.12 us
    all_to_all x1, starting transfers between devices, body(): table = lax.all_to_all(table, 'tile', 0, 0, tiled=True)  5.06 us
    ppermute x3, starting transfers between devices, body(): lax.ppermute(project, 'tile', by_mate(2 * s))  4.66 us
    ppermute x3, starting transfers between devices, body(): lax.ppermute(sums[z], 'tile', by_plane(-z))  4.47 us
    ppermute x3, waiting for transfers between devices, body(): lax.ppermute(project, 'tile', by_mate(2 * s))  4.43 us
    ppermute x3, waiting for transfers between devices, body(): lax.ppermute(sums[z], 'tile', by_plane(-z))  4.05 us
    ppermute x3, starting transfers between devices, body(): lax.ppermute(messages[s], 'tile', by_mate(2 * s))  3.55 us
  transfers between devices with their start and end apart: 17, of which 5 were waited for; matrix products, arithmetic and copies ran while one was open for 4% of the time, Pallas kernels for 11%

profile of v3, /device:TPU:0, one launch (start us, length us, event | category | flops | bytes accessed | tf_op | source)
XLA Modules:
  0.0 65.2 jit_solution(14726440071965953277)
XLA Ops:
  0.6 0.0 slice-start.4
  0.7 0.0 slice-start.2
  0.7 5.1 %collective-permute-start.2 = (bf16[320,128]{1,0:T(8,128)(2,1)}, bf16[320,128]{1,0:T(8,128)(2,1)S(1)}, u32[]{:S(2)}, u32[]{:S(2)}) collective-permute-start(bf16[320,128]{1,0:T(8,128)(2,1)} %bitcast.19), channel_id=1, source_target_pairs={{0,24},{1,25},{2,26},{3,27},{4,28},{5,29},{6,30},{7,31},{8,0},{9,1... | collective-permute-start | bytes 245768 | tf_op jit(solution)/shard_map/ppermute | solution.py:377
  5.8 1.0 %collective-permute-start = (bf16[320,128]{1,0:T(8,128)(2,1)}, bf16[320,128]{1,0:T(8,128)(2,1)S(1)}, u32[]{:S(2)}, u32[]{:S(2)}) collective-permute-start(bf16[320,128]{1,0:T(8,128)(2,1)} %bitcast.21), channel_id=1, source_target_pairs={{0,8},{1,9},{2,10},{3,11},{4,12},{5,13},{6,14},{7,15},{8,16},{9,17... | collective-permute-start | bytes 245768 | tf_op jit(solution)/shard_map/ppermute | solution.py:377
  6.8 0.7 %pad_add_fusion = f32[8,128]{1,0:T(8,128)S(1)} fusion(f32[4,32]{1,0:T(4,128)} %bitcast.23, s32[4,32]{1,0:T(4,128)} %bitcast.24, s32[4,32]{1,0:T(4,128)} %bitcast.25, s32[4,32]{1,0:T(4,128)} %bitcast.26), kind=kLoop, calls=%fused_computation.14 | loop fusion | flops 6144 | bytes 6144 | tf_op jit(solution)/shard_map/add | solution.py:373
  7.6 0.7 %broadcast_in_dim.10 = f32[32,8,128]{2,1,0:T(8,128)} broadcast(f32[8,128]{1,0:T(8,128)S(1)} %pad_add_fusion), dimensions={1,2} | broadcast | bytes 135168 | tf_op jit(solution)/shard_map/broadcast_in_dim | solution.py:370
  8.2 5.1 %all-to-all-start = ((f32[32,8,128]{2,1,0:T(8,128)}), f32[32,8,128]{2,1,0:T(8,128)S(1)}, u32[]{:S(2)}, u32[]{:S(2)}) async-start(f32[32,8,128]{2,1,0:T(8,128)} %broadcast_in_dim.10), calls=%async_computation | async-start | bytes 262144 | tf_op jit(solution)/shard_map/all_to_all | solution.py:375
  13.4 0.9 %broadcast_select_fusion = (bf16[1168,128]{1,0:T(8,128)(2,1)}, bf16[1168,128]{1,0:T(8,128)(2,1)}) fusion(pred[]{:T(512)S(6)} %eq.9, s32[8,128]{1,0:T(8,128)S(1)} %slice-done.4, bf16[384,128]{1,0:T(8,128)(2,1)S(1)} %bitcast.16, bf16[768,128]{1,0:T(8,128)(2,1)S(1)} %bitcast.14, s32[8,128]{1,0:T(8,128)S(1)} %slice-done.5, bf16[384,128]{1,0:T(8,128)(2,1)S(1)} %bitcast.17, ...), kind=kLoop, calls=%fused_computation.7 | loop fusion | flops 2990080 | bytes 1196033 | tf_op jit(solution)/shard_map/jit(_where)/select_n | solution.py:413
  14.3 0.3 collective-permute-start.7
  14.6 0.7 %collective-permute-start.8 = (bf16[1168,128]{1,0:T(8,128)(2,1)}, bf16[1168,128]{1,0:T(8,128)(2,1)S(1)}, u32[]{:S(2)}, u32[]{:S(2)}) collective-permute-start(bf16[1168,128]{1,0:T(8,128)(2,1)} %get-tuple-element.38), channel_id=1, source_target_pairs={{1,2},{3,4},{5,6},{7,8},{9,10},{11,12},{13,14},{15,16},{17,18},{19... | collective-permute-start | bytes 897032 | tf_op jit(solution)/shard_map/ppermute | solution.py:417
  15.3 3.1 %collective-permute-start.3 = (bf16[1280,128]{1,0:T(8,128)(2,1)S(1)}, bf16[1280,128]{1,0:T(8,128)(2,1)S(1)}, u32[]{:S(2)}, u32[]{:S(2)}) collective-permute-start(bf16[1280,128]{1,0:T(8,128)(2,1)S(1)} %pad_maximum_fusion.own), channel_id=1, source_target_pairs={{0,1},{1,0},{2,3},{3,2},{4,5},{5,4},{6,7},{7,6},{8,9},{9,8},{10,11... | collective-permute-start | bytes 983048 | tf_op jit(solution)/shard_map/ppermute | solution.py:379
  18.4 3.2 %all-to-all-done.table = f32[32,8,128]{2,1,0:T(8,128)S(1)} async-done(((f32[32,8,128]{2,1,0:T(8,128)}), f32[32,8,128]{2,1,0:T(8,128)S(1)}, u32[]{:S(2)}, u32[]{:S(2)}) %all-to-all-start) | async-done | bytes 131104 | tf_op jit(solution)/shard_map/all_to_all | solution.py:375
  21.6 0.5 picks.1
  22.1 0.5 messages.1
  22.6 0.4 collective-permute-start.4
  23.0 1.0 %collective-permute-start.5 = (bf16[480,128]{1,0:T(8,128)(2,1)S(1)}, bf16[480,128]{1,0:T(8,128)(2,1)S(1)}, u32[]{:S(2)}, u32[]{:S(2)}) collective-permute-start(bf16[480,128]{1,0:T(8,128)(2,1)S(1)} %get-tuple-element.32), channel_id=1, source_target_pairs={{0,4},{1,5},{2,6},{3,7},{4,0},{5,1},{6,2},{7,3},{8,12},{9,13},{10,... | collective-permute-start | bytes 368648 | tf_op jit(solution)/shard_map/ppermute | solution.py:419
  24.0 2.2 %collective-permute-start.6 = (bf16[480,128]{1,0:T(8,128)(2,1)S(1)}, bf16[480,128]{1,0:T(8,128)(2,1)S(1)}, u32[]{:S(2)}, u32[]{:S(2)}) collective-permute-start(bf16[480,128]{1,0:T(8,128)(2,1)S(1)} %get-tuple-element.33), channel_id=1, source_target_pairs={{0,6},{1,7},{2,4},{3,5},{4,2},{5,3},{6,0},{7,1},{8,14},{9,15},{10,... | collective-permute-start | bytes 368648 | tf_op jit(solution)/shard_map/ppermute | solution.py:419
  26.2 2.9 %first_layer.1 = (bf16[2688,256]{1,0:T(8,128)(2,1)S(1)}, bf16[2688,256]{1,0:T(8,128)(2,1)S(1)}, bf16[5376,128]{1,0:T(8,128)(2,1)S(1)}) custom-call(bf16[32,128,128]{2,1,0:T(8,128)(2,1)S(1)} %copy-done, bf16[1168,128]{1,0:T(8,128)(2,1)S(1)} %collective-permute-done.7.pair.refs_11_, bf16[1168,128]{1,0:T(8,128)(2,1)S(1)} %collective-permute-done.8.other.refs_12_, ...), custom_call_target="tpu_custom_call" | custom-call | flops 4000000000 | bytes 8388608 | tf_op jit(solution)/shard_map/first_layer/pallas_call | solution.py:421
  29.1 1.6 %collective-permute-done.5.refs_2_ = bf16[480,128]{1,0:T(8,128)(2,1)S(1)} collective-permute-done((bf16[480,128]{1,0:T(8,128)(2,1)S(1)}, bf16[480,128]{1,0:T(8,128)(2,1)S(1)}, u32[]{:S(2)}, u32[]{:S(2)}) %collective-permute-start.5) | collective-permute-done | bytes 122912 | tf_op jit(solution)/shard_map/ppermute | solution.py:419
  30.8 11.1 %middle_layers.1 = (bf16[32,128,128]{2,1,0:T(8,128)(2,1)}, bf16[2176,256]{1,0:T(8,128)(2,1)S(1)}, f32[4352,128]{1,0:T(8,128)S(1)}, bf16[320,128]{1,0:T(8,128)(2,1)S(1)}) custom-call(bf16[480,128]{1,0:T(8,128)(2,1)S(1)} %get-tuple-element.30.refs_0_, bf16[480,128]{1,0:T(8,128)(2,1)S(1)} %collective-permute-done.4.refs_1_, ...), custom_call_target="tpu_custom_call" | custom-call | flops 12000000000 | bytes 16777216 | tf_op jit(solution)/shard_map/middle_layers/pallas_call | solution.py:430
  41.8 2.7 %collective-permute-start.11 = (bf16[320,128]{1,0:T(8,128)(2,1)S(1)}, bf16[320,128]{1,0:T(8,128)(2,1)S(1)}, u32[]{:S(2)}, u32[]{:S(2)}) collective-permute-start(bf16[320,128]{1,0:T(8,128)(2,1)S(1)} %get-tuple-element.46), channel_id=1, source_target_pairs={{0,6},{1,7},{2,4},{3,5},{4,2},{5,3},{6,0},{7,1},{8,14},{9,15},{10,... | collective-permute-start | bytes 245768 | tf_op jit(solution)/shard_map/ppermute | solution.py:479
  44.5 2.0 %collective-permute-start.10 = (bf16[320,128]{1,0:T(8,128)(2,1)S(1)}, bf16[320,128]{1,0:T(8,128)(2,1)S(1)}, u32[]{:S(2)}, u32[]{:S(2)}) collective-permute-start(bf16[320,128]{1,0:T(8,128)(2,1)S(1)} %get-tuple-element.46), channel_id=1, source_target_pairs={{0,4},{1,5},{2,6},{3,7},{4,0},{5,1},{6,2},{7,3},{8,12},{9,13},{10,... | collective-permute-start | bytes 245768 | tf_op jit(solution)/shard_map/ppermute | solution.py:479
  46.5 4.4 %collective-permute-done.9 = bf16[320,128]{1,0:T(8,128)(2,1)S(1)} collective-permute-done((bf16[320,128]{1,0:T(8,128)(2,1)S(1)}, bf16[320,128]{1,0:T(8,128)(2,1)S(1)}, u32[]{:S(2)}, u32[]{:S(2)}) %collective-permute-start.9) | collective-permute-done | bytes 81952 | tf_op jit(solution)/shard_map/ppermute | solution.py:479
  51.0 0.1 collective-permute-start.12
  51.1 0.6 matrix.1.scatter
  51.7 1.0 %collective-permute-done.12.mate = bf16[1280,128]{1,0:T(8,128)(2,1)S(1)} collective-permute-done((bf16[1280,128]{1,0:T(8,128)(2,1)S(1)}, bf16[1280,128]{1,0:T(8,128)(2,1)S(1)}, u32[]{:S(2)}, u32[]{:S(2)}) %collective-permute-start.12) | collective-permute-done | bytes 327712 | tf_op jit(solution)/shard_map/ppermute | solution.py:481
  52.7 0.4 scatter.1
  53.1 3.4 %collective-permute-start.13 = (bf16[320,128]{1,0:T(8,128)(2,1)S(1)}, bf16[320,128]{1,0:T(8,128)(2,1)S(1)}, u32[]{:S(2)}, u32[]{:S(2)}) collective-permute-start(bf16[320,128]{1,0:T(8,128)(2,1)S(1)} %get-tuple-element.54), channel_id=1, source_target_pairs={{0,24},{1,25},{2,26},{3,27},{4,28},{5,29},{6,30},{7,31},{8,0},{9,1... | collective-permute-start | bytes 245768 | tf_op jit(solution)/shard_map/ppermute | solution.py:494
  56.5 1.1 %collective-permute-start.15 = (bf16[320,128]{1,0:T(8,128)(2,1)S(1)}, bf16[320,128]{1,0:T(8,128)(2,1)S(1)}, u32[]{:S(2)}, u32[]{:S(2)}) collective-permute-start(bf16[320,128]{1,0:T(8,128)(2,1)S(1)} %get-tuple-element.56), channel_id=1, source_target_pairs={{0,8},{1,9},{2,10},{3,11},{4,12},{5,13},{6,14},{7,15},{8,16},{9,17... | collective-permute-start | bytes 245768 | tf_op jit(solution)/shard_map/ppermute | solution.py:494
  57.6 2.9 %last_adjoint.1 = bf16[32,128,128]{2,1,0:T(8,128)(2,1)} custom-call(bf16[2176,256]{1,0:T(8,128)(2,1)S(1)} %get-tuple-element.51.act0, f32[4352,128]{1,0:T(8,128)S(1)} %get-tuple-element.52.grad1, bf16[3,3,3,128,128]{4,3,2,1,0:T(8,128)(2,1)S(1)} %copy-done.3), custom_call_target="tpu_custom_call" | custom-call | flops 3000000000 | bytes 6291456 | tf_op jit(solution)/shard_map/last_adjoint/pallas_call | solution.py:495
  60.5 4.0 %collective-permute-done.14 = bf16[320,128]{1,0:T(8,128)(2,1)S(1)} collective-permute-done((bf16[320,128]{1,0:T(8,128)(2,1)S(1)}, bf16[320,128]{1,0:T(8,128)(2,1)S(1)}, u32[]{:S(2)}, u32[]{:S(2)}) %collective-permute-start.14) | collective-permute-done | bytes 81952 | tf_op jit(solution)/shard_map/ppermute | solution.py:494
  64.5 0.7 %convert_add_fusion = f32[320,128]{1,0:T(8,128)} fusion(bf16[320,128]{1,0:T(8,128)(2,1)S(1)} %collective-permute-done.15, bf16[320,128]{1,0:T(8,128)(2,1)S(1)} %collective-permute-done.14, bf16[320,128]{1,0:T(8,128)(2,1)S(1)} %collective-permute-done.13, bf16[320,128]{1,0:T(8,128)(2,1)S(1)} %get-tuple-element.53), kind=kLoop, calls=%fused_computation.9 | loop fusion | flops 286720 | bytes 491520 | tf_op jit(solution)/shard_map/add | solution.py:504
  (46 shorter events, 0.2 us)
Async XLA Ops:
  0.6 12.7 %slice-start.4 = ((s32[32,128]{1,0:T(8,128)}), s32[8,128]{1,0:T(8,128)S(1)}, s32[]{:S(2)}) async-start(s32[32,128]{1,0:T(8,128)} %mask.1), calls=%async_computation.5 | async-start | bytes 8192 | tf_op jit(solution)/shard_map/slice | solution.py:384
  0.6 12.7 %slice-start.5 = ((s32[32,128]{1,0:T(8,128)}), s32[8,128]{1,0:T(8,128)S(1)}, s32[]{:S(2)}) async-start(s32[32,128]{1,0:T(8,128)} %mask.1), calls=%async_computation.6 | async-start | bytes 8192 | tf_op jit(solution)/shard_map/slice | solution.py:384
  0.7 12.7 %slice-start.2 = ((bf16[32,128,128]{2,1,0:T(8,128)(2,1)}), bf16[3,128,128]{2,1,0:T(8,128)(2,1)S(1)}, s32[]{:S(2)}) async-start(bf16[32,128,128]{2,1,0:T(8,128)(2,1)} %refs_10_.1), calls=%async_computation.3 | async-start | bytes 196608 | tf_op jit(solution)/shard_map/slice | solution.py:384
  0.7 12.7 %slice-start.3 = ((bf16[32,128,128]{2,1,0:T(8,128)(2,1)}), bf16[3,128,128]{2,1,0:T(8,128)(2,1)S(1)}, s32[]{:S(2)}) async-start(bf16[32,128,128]{2,1,0:T(8,128)(2,1)} %refs_10_.1), calls=%async_computation.4 | async-start | bytes 196608 | tf_op jit(solution)/shard_map/slice | solution.py:384
  0.7 12.7 %slice-start = ((bf16[32,128,128]{2,1,0:T(8,128)(2,1)}), bf16[6,128,128]{2,1,0:T(8,128)(2,1)S(1)}, s32[]{:S(2)}) async-start(bf16[32,128,128]{2,1,0:T(8,128)(2,1)} %ice.1), calls=%async_computation.1 | async-start | bytes 393216 | tf_op jit(solution)/shard_map/slice | solution.py:384
  0.7 12.7 %slice-start.1 = ((bf16[32,128,128]{2,1,0:T(8,128)(2,1)}), bf16[6,128,128]{2,1,0:T(8,128)(2,1)S(1)}, s32[]{:S(2)}) async-start(bf16[32,128,128]{2,1,0:T(8,128)(2,1)} %ice.1), calls=%async_computation.2 | async-start | bytes 393216 | tf_op jit(solution)/shard_map/slice | solution.py:384
  0.7 14.5 %collective-permute-start.2 = (bf16[320,128]{1,0:T(8,128)(2,1)}, bf16[320,128]{1,0:T(8,128)(2,1)S(1)}, u32[]{:S(2)}, u32[]{:S(2)}) collective-permute-start(bf16[320,128]{1,0:T(8,128)(2,1)} %bitcast.19), channel_id=1, source_target_pairs={{0,24},{1,25},{2,26},{3,27},{4,28},{5,29},{6,30},{7,31},{8,0},{9,1... | collective-permute-start | bytes 245768 | tf_op jit(solution)/shard_map/ppermute | solution.py:377
  5.8 9.4 %collective-permute-start.1 = (bf16[320,128]{1,0:T(8,128)(2,1)}, bf16[320,128]{1,0:T(8,128)(2,1)S(1)}, u32[]{:S(2)}, u32[]{:S(2)}) collective-permute-start(bf16[320,128]{1,0:T(8,128)(2,1)} %bitcast.20), channel_id=1, source_target_pairs={{0,16},{1,17},{2,18},{3,19},{4,20},{5,21},{6,22},{7,23},{8,24},{9,... | collective-permute-start | bytes 245768 | tf_op jit(solution)/shard_map/ppermute | solution.py:377
  5.8 9.4 %collective-permute-start = (bf16[320,128]{1,0:T(8,128)(2,1)}, bf16[320,128]{1,0:T(8,128)(2,1)S(1)}, u32[]{:S(2)}, u32[]{:S(2)}) collective-permute-start(bf16[320,128]{1,0:T(8,128)(2,1)} %bitcast.21), channel_id=1, source_target_pairs={{0,8},{1,9},{2,10},{3,11},{4,12},{5,13},{6,14},{7,15},{8,16},{9,17... | collective-permute-start | bytes 245768 | tf_op jit(solution)/shard_map/ppermute | solution.py:377
  8.2 7.0 %copy-start.7 = (bf16[4,8,10,128]{3,1,2,0:T(8,128)(2,1)S(1)}, bf16[4,8,10,128]{3,1,2,0:T(8,128)(2,1)}, u32[]{:S(2)}) copy-start(bf16[4,8,10,128]{3,1,2,0:T(8,128)(2,1)} %param.12) | copy-start | bytes 245764
  8.2 13.4 %all-to-all-start = ((f32[32,8,128]{2,1,0:T(8,128)}), f32[32,8,128]{2,1,0:T(8,128)S(1)}, u32[]{:S(2)}, u32[]{:S(2)}) async-start(f32[32,8,128]{2,1,0:T(8,128)} %broadcast_in_dim.10), calls=%async_computation | async-start | bytes 262144 | tf_op jit(solution)/shard_map/all_to_all | solution.py:375
  14.3 11.9 %collective-permute-start.7 = (bf16[1168,128]{1,0:T(8,128)(2,1)}, bf16[1168,128]{1,0:T(8,128)(2,1)S(1)}, u32[]{:S(2)}, u32[]{:S(2)}) collective-permute-start(bf16[1168,128]{1,0:T(8,128)(2,1)} %get-tuple-element.37), channel_id=1, source_target_pairs={{0,1},{1,0},{2,3},{3,2},{4,5},{5,4},{6,7},{7,6},{8,9},{9,8},{10,11... | collective-permute-start | bytes 897032 | tf_op jit(solution)/shard_map/ppermute | solution.py:415
  14.6 11.6 %collective-permute-start.8 = (bf16[1168,128]{1,0:T(8,128)(2,1)}, bf16[1168,128]{1,0:T(8,128)(2,1)S(1)}, u32[]{:S(2)}, u32[]{:S(2)}) collective-permute-start(bf16[1168,128]{1,0:T(8,128)(2,1)} %get-tuple-element.38), channel_id=1, source_target_pairs={{1,2},{3,4},{5,6},{7,8},{9,10},{11,12},{13,14},{15,16},{17,18},{19... | collective-permute-start | bytes 897032 | tf_op jit(solution)/shard_map/ppermute | solution.py:417
  15.3 10.9 %copy-start = (bf16[32,128,128]{2,1,0:T(8,128)(2,1)S(1)}, bf16[32,128,128]{2,1,0:T(8,128)(2,1)}, u32[]{:S(2)}) copy-start(bf16[32,128,128]{2,1,0:T(8,128)(2,1)} %ice.1) | copy-start | bytes 3145732
  15.3 10.9 %copy-start.2 = (s32[32,128]{1,0:T(8,128)S(1)}, s32[32,128]{1,0:T(8,128)}, u32[]{:S(2)}) copy-start(s32[32,128]{1,0:T(8,128)} %mask.1) | copy-start | bytes 49156
  15.3 10.9 %copy-start.3 = (bf16[3,3,3,128,128]{4,3,2,1,0:T(8,128)(2,1)S(1)}, bf16[3,3,3,128,128]{4,3,2,1,0:T(8,128)(2,1)}, u32[]{:S(2)}) copy-start(bf16[3,3,3,128,128]{4,3,2,1,0:T(8,128)(2,1)} %weight.3) | copy-start | bytes 2654212
  15.3 10.9 %copy-start.6 = (f32[3,128]{1,0:T(4,128)S(1)}, f32[3,128]{1,0:T(4,128)}, u32[]{:S(2)}) copy-start(f32[3,128]{1,0:T(4,128)} %refs_6_.1) | copy-start | bytes 4612
  15.3 6.8 %collective-permute-start.3 = (bf16[1280,128]{1,0:T(8,128)(2,1)S(1)}, bf16[1280,128]{1,0:T(8,128)(2,1)S(1)}, u32[]{:S(2)}, u32[]{:S(2)}) collective-permute-start(bf16[1280,128]{1,0:T(8,128)(2,1)S(1)} %pad_maximum_fusion.own), channel_id=1, source_target_pairs={{0,1},{1,0},{2,3},{3,2},{4,5},{5,4},{6,7},{7,6},{8,9},{9,8},{10,11... | collective-permute-start | bytes 983048 | tf_op jit(solution)/shard_map/ppermute | solution.py:379
  22.6 6.5 %collective-permute-start.4 = (bf16[480,128]{1,0:T(8,128)(2,1)S(1)}, bf16[480,128]{1,0:T(8,128)(2,1)S(1)}, u32[]{:S(2)}, u32[]{:S(2)}) collective-permute-start(bf16[480,128]{1,0:T(8,128)(2,1)S(1)} %get-tuple-element.31), channel_id=1, source_target_pairs={{0,2},{1,3},{2,0},{3,1},{4,6},{5,7},{6,4},{7,5},{8,10},{9,11},{10,... | collective-permute-start | bytes 368648 | tf_op jit(solution)/shard_map/ppermute | solution.py:419
  23.0 7.7 %collective-permute-start.5 = (bf16[480,128]{1,0:T(8,128)(2,1)S(1)}, bf16[480,128]{1,0:T(8,128)(2,1)S(1)}, u32[]{:S(2)}, u32[]{:S(2)}) collective-permute-start(bf16[480,128]{1,0:T(8,128)(2,1)S(1)} %get-tuple-element.32), channel_id=1, source_target_pairs={{0,4},{1,5},{2,6},{3,7},{4,0},{5,1},{6,2},{7,3},{8,12},{9,13},{10,... | collective-permute-start | bytes 368648 | tf_op jit(solution)/shard_map/ppermute | solution.py:419
  24.0 6.7 %copy-start.1 = (bf16[32,128,128]{2,1,0:T(8,128)(2,1)S(1)}, bf16[32,128,128]{2,1,0:T(8,128)(2,1)}, u32[]{:S(2)}) copy-start(bf16[32,128,128]{2,1,0:T(8,128)(2,1)} %refs_10_.1) | copy-start | bytes 3145732
  24.0 6.7 %copy-start.4 = (f32[128,128]{1,0:T(8,128)S(1)}, f32[128,128]{1,0:T(8,128)}, u32[]{:S(2)}) copy-start(f32[128,128]{1,0:T(8,128)} %refs_4_.1) | copy-start | bytes 196612
  24.0 6.7 %copy-start.5 = (bf16[10,128]{1,0:T(8,128)(2,1)S(1)}, bf16[10,128]{1,0:T(8,128)(2,1)}, u32[]{:S(2)}) copy-start(bf16[10,128]{1,0:T(8,128)(2,1)} %refs_5_.1) | copy-start | bytes 7684
  24.0 6.7 %collective-permute-start.6 = (bf16[480,128]{1,0:T(8,128)(2,1)S(1)}, bf16[480,128]{1,0:T(8,128)(2,1)S(1)}, u32[]{:S(2)}, u32[]{:S(2)}) collective-permute-start(bf16[480,128]{1,0:T(8,128)(2,1)S(1)} %get-tuple-element.33), channel_id=1, source_target_pairs={{0,6},{1,7},{2,4},{3,5},{4,2},{5,3},{6,0},{7,1},{8,14},{9,15},{10,... | collective-permute-start | bytes 368648 | tf_op jit(solution)/shard_map/ppermute | solution.py:419
  41.8 9.2 %collective-permute-start.11 = (bf16[320,128]{1,0:T(8,128)(2,1)S(1)}, bf16[320,128]{1,0:T(8,128)(2,1)S(1)}, u32[]{:S(2)}, u32[]{:S(2)}) collective-permute-start(bf16[320,128]{1,0:T(8,128)(2,1)S(1)} %get-tuple-element.46), channel_id=1, source_target_pairs={{0,6},{1,7},{2,4},{3,5},{4,2},{5,3},{6,0},{7,1},{8,14},{9,15},{10,... | collective-permute-start | bytes 245768 | tf_op jit(solution)/shard_map/ppermute | solution.py:479
  44.5 6.5 %collective-permute-start.10 = (bf16[320,128]{1,0:T(8,128)(2,1)S(1)}, bf16[320,128]{1,0:T(8,128)(2,1)S(1)}, u32[]{:S(2)}, u32[]{:S(2)}) collective-permute-start(bf16[320,128]{1,0:T(8,128)(2,1)S(1)} %get-tuple-element.46), channel_id=1, source_target_pairs={{0,4},{1,5},{2,6},{3,7},{4,0},{5,1},{6,2},{7,3},{8,12},{9,13},{10,... | collective-permute-start | bytes 245768 | tf_op jit(solution)/shard_map/ppermute | solution.py:479
  46.5 4.4 %collective-permute-start.9 = (bf16[320,128]{1,0:T(8,128)(2,1)S(1)}, bf16[320,128]{1,0:T(8,128)(2,1)S(1)}, u32[]{:S(2)}, u32[]{:S(2)}) collective-permute-start(bf16[320,128]{1,0:T(8,128)(2,1)S(1)} %get-tuple-element.46), channel_id=1, source_target_pairs={{0,2},{1,3},{2,0},{3,1},{4,6},{5,7},{6,4},{7,5},{8,10},{9,11},{10,... | collective-permute-start | bytes 245768 | tf_op jit(solution)/shard_map/ppermute | solution.py:479
  51.0 1.7 %collective-permute-start.12 = (bf16[1280,128]{1,0:T(8,128)(2,1)S(1)}, bf16[1280,128]{1,0:T(8,128)(2,1)S(1)}, u32[]{:S(2)}, u32[]{:S(2)}) collective-permute-start(bf16[1280,128]{1,0:T(8,128)(2,1)S(1)} %constant_dynamic-update-slice_fusion.own), channel_id=1, source_target_pairs={{0,1},{1,0},{2,3},{3,2},{4,5},{5,4},{6,7},{7,6},{8,9},{9,8},{10,11... | collective-permute-start | bytes 983048 | tf_op jit(solution)/shard_map/ppermute | solution.py:481
  53.1 7.4 %collective-permute-start.13 = (bf16[320,128]{1,0:T(8,128)(2,1)S(1)}, bf16[320,128]{1,0:T(8,128)(2,1)S(1)}, u32[]{:S(2)}, u32[]{:S(2)}) collective-permute-start(bf16[320,128]{1,0:T(8,128)(2,1)S(1)} %get-tuple-element.54), channel_id=1, source_target_pairs={{0,24},{1,25},{2,26},{3,27},{4,28},{5,29},{6,30},{7,31},{8,0},{9,1... | collective-permute-start | bytes 245768 | tf_op jit(solution)/shard_map/ppermute | solution.py:494
  56.5 8.0 %collective-permute-start.14 = (bf16[320,128]{1,0:T(8,128)(2,1)S(1)}, bf16[320,128]{1,0:T(8,128)(2,1)S(1)}, u32[]{:S(2)}, u32[]{:S(2)}) collective-permute-start(bf16[320,128]{1,0:T(8,128)(2,1)S(1)} %get-tuple-element.55), channel_id=1, source_target_pairs={{0,16},{1,17},{2,18},{3,19},{4,20},{5,21},{6,22},{7,23},{8,24},{9,... | collective-permute-start | bytes 245768 | tf_op jit(solution)/shard_map/ppermute | solution.py:494
  56.5 8.0 %collective-permute-start.15 = (bf16[320,128]{1,0:T(8,128)(2,1)S(1)}, bf16[320,128]{1,0:T(8,128)(2,1)S(1)}, u32[]{:S(2)}, u32[]{:S(2)}) collective-permute-start(bf16[320,128]{1,0:T(8,128)(2,1)S(1)} %get-tuple-element.56), channel_id=1, source_target_pairs={{0,8},{1,9},{2,10},{3,11},{4,12},{5,13},{6,14},{7,15},{8,16},{9,17... | collective-permute-start | bytes 245768 | tf_op jit(solution)/shard_map/ppermute | solution.py:494

commit v4 on v3

--- a/solution.py
+++ b/solution.py
@@ -113,7 +113,7 @@
     return ((from_plane * GROUP + from_spot) * ROWS + lane % ROWS).astype(F32)
 
 
-def pick_kernel(planes, table, picks):
+def pick_kernel(planes, table, picks, scatter):
     me = lax.axis_index("tile")
     plane, spot = me // GROUP, me % GROUP
     count = planes * GROUP
@@ -126,11 +126,6 @@
         inside = jnp.logical_and(device >= 0, device < count)
         parts.append(jnp.where(inside, picked(columns, place, ident, start, size), 0.0))
     picks[...] = jnp.concatenate(parts, axis=0).astype(BF)
-
-
-def matrix_kernel(planes, table, scatter):
-    me = lax.axis_index("tile")
-    plane, spot = me // GROUP, me % GROUP
     ident = source_ident(planes, plane, spot, 1)
     columns = column_tables(table, [plane * GROUP + (spot ^ s) for s in range(GROUP)])
     parts = [picked(columns, s, ident, 0, ROWS) for s in range(GROUP)]
@@ -395,9 +390,9 @@
     arrays = (ice_state, sensitivity, ocean_mask)
     to_next = edge(arrays, ROWS - 6, ROWS - 3, ROWS - PAD)
     to_last = edge(lax.optimization_barrier(arrays), 0, 0, 0)
-    picks = pl.pallas_call(
+    picks, scatter = pl.pallas_call(
         functools.partial(pick_kernel, planes),
-        out_shape=shape(SENT * EXT, 2 * planes * ROWS),
+        out_shape=(shape(SENT * EXT, 2 * planes * ROWS), shape(planes * ROWS, GROUP * ROWS)),
         compiler_params=params(4),
         name="picks",
         cost_estimate=pl.CostEstimate(flops=10**10, bytes_accessed=MIB, transcendentals=0),
@@ -468,14 +463,6 @@
         other,
         conv_weight,
     )
-    table, project = lax.optimization_barrier((table, project))
-    scatter = pl.pallas_call(
-        functools.partial(matrix_kernel, planes),
-        out_shape=shape(planes * ROWS, GROUP * ROWS),
-        compiler_params=params(4),
-        name="matrix",
-        cost_estimate=pl.CostEstimate(flops=10**9, bytes_accessed=MIB, transcendentals=0),
-    )(table)
     projects = [project] + [lax.ppermute(project, "tile", by_mate(2 * s)) for s in range(1, SENT)]
     own_projects = jnp.concatenate(projects, axis=0)
     mate_projects = lax.ppermute(own_projects, "tile", by_mate(1))

time: 65.5 us -> 65.1 us (level)
  waiting for transfers between devices: 14.3 us -> 15 us
where the time goes in v4:
time: 65.1 us; the launch traced here: 64.9 us
  starting transfers between devices  27.5 us (42%)
  Pallas kernels  18.2 us (28%)
  waiting for transfers between devices  15 us (23%)
  other arithmetic  2.41 us (4%)
  between operations  0.96 us (1%)
  local copies, waits for them, and re-layouts  0.79 us (1%)
    pallas_call x1, Pallas kernels, body(): pl.pallas_call(main_kernel, out_shape=(shape(ROWS, C, C), shape(17 * C, P...  10.7 us
    ppermute x3, starting transfers between devices, body(): lax.ppermute(fields, 'tile', by_plane(z))  6.12 us
    all_to_all x1, starting transfers between devices, body(): table = lax.all_to_all(table, 'tile', 0, 0, tiled=True)  5.06 us
    ppermute x3, starting transfers between devices, body(): lax.ppermute(sums[z], 'tile', by_plane(-z))  4.48 us
    ppermute x3, waiting for transfers between devices, body(): lax.ppermute(project, 'tile', by_mate(2 * s))  4.43 us
    ppermute x3, starting transfers between devices, body(): lax.ppermute(project, 'tile', by_mate(2 * s))  4.25 us
    ppermute x3, waiting for transfers between devices, body(): lax.ppermute(sums[z], 'tile', by_plane(-z))  4.06 us
    ppermute x3, starting transfers between devices, body(): lax.ppermute(messages[s], 'tile', by_mate(2 * s))  3.55 us
  transfers between devices with their start and end apart: 17, of which 5 were waited for; matrix products, arithmetic and copies ran while one was open for 4% of the time, Pallas kernels for 11%

profile of v4, /device:TPU:0, one launch (start us, length us, event | category | flops | bytes accessed | tf_op | source)
XLA Modules:
  0.0 64.9 jit_solution(11030846211483982240)
XLA Ops:
  0.6 0.0 slice-start.4
  0.7 0.0 slice-start.2
  0.7 0.0 slice-start
  0.7 5.1 %collective-permute-start.2 = (bf16[320,128]{1,0:T(8,128)(2,1)}, bf16[320,128]{1,0:T(8,128)(2,1)S(1)}, u32[]{:S(2)}, u32[]{:S(2)}) collective-permute-start(bf16[320,128]{1,0:T(8,128)(2,1)} %bitcast.19), channel_id=1, source_target_pairs={{0,24},{1,25},{2,26},{3,27},{4,28},{5,29},{6,30},{7,31},{8,0},{9,1... | collective-permute-start | bytes 245768 | tf_op jit(solution)/shard_map/ppermute | solution.py:372
  5.8 1.0 %collective-permute-start = (bf16[320,128]{1,0:T(8,128)(2,1)}, bf16[320,128]{1,0:T(8,128)(2,1)S(1)}, u32[]{:S(2)}, u32[]{:S(2)}) collective-permute-start(bf16[320,128]{1,0:T(8,128)(2,1)} %bitcast.21), channel_id=1, source_target_pairs={{0,8},{1,9},{2,10},{3,11},{4,12},{5,13},{6,14},{7,15},{8,16},{9,17... | collective-permute-start | bytes 245768 | tf_op jit(solution)/shard_map/ppermute | solution.py:372
  6.8 0.7 %pad_add_fusion = f32[8,128]{1,0:T(8,128)S(1)} fusion(f32[4,32]{1,0:T(4,128)} %bitcast.23, s32[4,32]{1,0:T(4,128)} %bitcast.24, s32[4,32]{1,0:T(4,128)} %bitcast.25, s32[4,32]{1,0:T(4,128)} %bitcast.26), kind=kLoop, calls=%fused_computation.14 | loop fusion | flops 6144 | bytes 6144 | tf_op jit(solution)/shard_map/add | solution.py:368
  7.6 0.7 %broadcast_in_dim.10 = f32[32,8,128]{2,1,0:T(8,128)} broadcast(f32[8,128]{1,0:T(8,128)S(1)} %pad_add_fusion), dimensions={1,2} | broadcast | bytes 135168 | tf_op jit(solution)/shard_map/broadcast_in_dim | solution.py:365
  8.2 5.1 %all-to-all-start = ((f32[32,8,128]{2,1,0:T(8,128)}), f32[32,8,128]{2,1,0:T(8,128)S(1)}, u32[]{:S(2)}, u32[]{:S(2)}) async-start(f32[32,8,128]{2,1,0:T(8,128)} %broadcast_in_dim.10), calls=%async_computation | async-start | bytes 262144 | tf_op jit(solution)/shard_map/all_to_all | solution.py:370
  13.4 0.9 %broadcast_select_fusion = (bf16[1168,128]{1,0:T(8,128)(2,1)}, bf16[1168,128]{1,0:T(8,128)(2,1)}) fusion(pred[]{:T(512)S(6)} %eq.9, s32[8,128]{1,0:T(8,128)S(1)} %slice-done.4, bf16[384,128]{1,0:T(8,128)(2,1)S(1)} %bitcast.16, bf16[768,128]{1,0:T(8,128)(2,1)S(1)} %bitcast.14, s32[8,128]{1,0:T(8,128)S(1)} %slice-done.5, bf16[384,128]{1,0:T(8,128)(2,1)S(1)} %bitcast.17, ...), kind=kLoop, calls=%fused_computation.7 | loop fusion | flops 2990080 | bytes 1196033 | tf_op jit(solution)/shard_map/jit(_where)/select_n | solution.py:408
  14.3 0.3 collective-permute-start.7
  14.6 0.7 %collective-permute-start.8 = (bf16[1168,128]{1,0:T(8,128)(2,1)}, bf16[1168,128]{1,0:T(8,128)(2,1)S(1)}, u32[]{:S(2)}, u32[]{:S(2)}) collective-permute-start(bf16[1168,128]{1,0:T(8,128)(2,1)} %get-tuple-element.39), channel_id=1, source_target_pairs={{1,2},{3,4},{5,6},{7,8},{9,10},{11,12},{13,14},{15,16},{17,18},{19... | collective-permute-start | bytes 897032 | tf_op jit(solution)/shard_map/ppermute | solution.py:412
  15.3 3.1 %collective-permute-start.3 = (bf16[1280,128]{1,0:T(8,128)(2,1)S(1)}, bf16[1280,128]{1,0:T(8,128)(2,1)S(1)}, u32[]{:S(2)}, u32[]{:S(2)}) collective-permute-start(bf16[1280,128]{1,0:T(8,128)(2,1)S(1)} %pad_maximum_fusion.own), channel_id=1, source_target_pairs={{0,1},{1,0},{2,3},{3,2},{4,5},{5,4},{6,7},{7,6},{8,9},{9,8},{10,11... | collective-permute-start | bytes 983048 | tf_op jit(solution)/shard_map/ppermute | solution.py:374
  18.4 3.2 %all-to-all-done.table = f32[32,8,128]{2,1,0:T(8,128)S(1)} async-done(((f32[32,8,128]{2,1,0:T(8,128)}), f32[32,8,128]{2,1,0:T(8,128)S(1)}, u32[]{:S(2)}, u32[]{:S(2)}) %all-to-all-start) | async-done | bytes 131104 | tf_op jit(solution)/shard_map/all_to_all | solution.py:370
  21.6 0.9 %picks.1 = (bf16[192,256]{1,0:T(8,128)(2,1)S(1)}, bf16[128,256]{1,0:T(8,128)(2,1)S(1)}) custom-call(f32[32,8,128]{2,1,0:T(8,128)S(1)} %all-to-all-done.table), custom_call_target="tpu_custom_call" | custom-call | flops 10000000000 | bytes 1048576 | tf_op jit(solution)/shard_map/picks/pallas_call | solution.py:393
  22.5 0.5 messages.1
  23.0 0.4 collective-permute-start.4
  23.4 1.0 %collective-permute-start.5 = (bf16[480,128]{1,0:T(8,128)(2,1)S(1)}, bf16[480,128]{1,0:T(8,128)(2,1)S(1)}, u32[]{:S(2)}, u32[]{:S(2)}) collective-permute-start(bf16[480,128]{1,0:T(8,128)(2,1)S(1)} %get-tuple-element.33), channel_id=1, source_target_pairs={{0,4},{1,5},{2,6},{3,7},{4,0},{5,1},{6,2},{7,3},{8,12},{9,13},{10,... | collective-permute-start | bytes 368648 | tf_op jit(solution)/shard_map/ppermute | solution.py:414
  24.4 2.2 %collective-permute-start.6 = (bf16[480,128]{1,0:T(8,128)(2,1)S(1)}, bf16[480,128]{1,0:T(8,128)(2,1)S(1)}, u32[]{:S(2)}, u32[]{:S(2)}) collective-permute-start(bf16[480,128]{1,0:T(8,128)(2,1)S(1)} %get-tuple-element.34), channel_id=1, source_target_pairs={{0,6},{1,7},{2,4},{3,5},{4,2},{5,3},{6,0},{7,1},{8,14},{9,15},{10,... | collective-permute-start | bytes 368648 | tf_op jit(solution)/shard_map/ppermute | solution.py:414
  26.6 2.8 %first_layer.1 = (bf16[2688,256]{1,0:T(8,128)(2,1)S(1)}, bf16[2688,256]{1,0:T(8,128)(2,1)S(1)}, bf16[5376,128]{1,0:T(8,128)(2,1)S(1)}) custom-call(bf16[32,128,128]{2,1,0:T(8,128)(2,1)S(1)} %copy-done, bf16[1168,128]{1,0:T(8,128)(2,1)S(1)} %collective-permute-done.7.pair.refs_11_, bf16[1168,128]{1,0:T(8,128)(2,1)S(1)} %collective-permute-done.8.other.refs_12_, ...), custom_call_target="tpu_custom_call" | custom-call | flops 4000000000 | bytes 8388608 | tf_op jit(solution)/shard_map/first_layer/pallas_call | solution.py:416
  29.4 1.7 %collective-permute-done.5.refs_2_ = bf16[480,128]{1,0:T(8,128)(2,1)S(1)} collective-permute-done((bf16[480,128]{1,0:T(8,128)(2,1)S(1)}, bf16[480,128]{1,0:T(8,128)(2,1)S(1)}, u32[]{:S(2)}, u32[]{:S(2)}) %collective-permute-start.5) | collective-permute-done | bytes 122912 | tf_op jit(solution)/shard_map/ppermute | solution.py:414
  31.2 10.7 %middle_layers.1 = (bf16[32,128,128]{2,1,0:T(8,128)(2,1)}, bf16[2176,256]{1,0:T(8,128)(2,1)S(1)}, f32[4352,128]{1,0:T(8,128)S(1)}, bf16[320,128]{1,0:T(8,128)(2,1)S(1)}) custom-call(bf16[480,128]{1,0:T(8,128)(2,1)S(1)} %get-tuple-element.31.refs_0_, bf16[480,128]{1,0:T(8,128)(2,1)S(1)} %collective-permute-done.4.refs_1_, ...), custom_call_target="tpu_custom_call" | custom-call | flops 12000000000 | bytes 16777216 | tf_op jit(solution)/shard_map/middle_layers/pallas_call | solution.py:425
  41.9 2.7 %collective-permute-start.11 = (bf16[320,128]{1,0:T(8,128)(2,1)S(1)}, bf16[320,128]{1,0:T(8,128)(2,1)S(1)}, u32[]{:S(2)}, u32[]{:S(2)}) collective-permute-start(bf16[320,128]{1,0:T(8,128)(2,1)S(1)} %get-tuple-element.46), channel_id=1, source_target_pairs={{0,6},{1,7},{2,4},{3,5},{4,2},{5,3},{6,0},{7,1},{8,14},{9,15},{10,... | collective-permute-start | bytes 245768 | tf_op jit(solution)/shard_map/ppermute | solution.py:466
  44.5 1.6 %collective-permute-start.10 = (bf16[320,128]{1,0:T(8,128)(2,1)S(1)}, bf16[320,128]{1,0:T(8,128)(2,1)S(1)}, u32[]{:S(2)}, u32[]{:S(2)}) collective-permute-start(bf16[320,128]{1,0:T(8,128)(2,1)S(1)} %get-tuple-element.46), channel_id=1, source_target_pairs={{0,4},{1,5},{2,6},{3,7},{4,0},{5,1},{6,2},{7,3},{8,12},{9,13},{10,... | collective-permute-start | bytes 245768 | tf_op jit(solution)/shard_map/ppermute | solution.py:466
  46.2 4.4 %collective-permute-done.9 = bf16[320,128]{1,0:T(8,128)(2,1)S(1)} collective-permute-done((bf16[320,128]{1,0:T(8,128)(2,1)S(1)}, bf16[320,128]{1,0:T(8,128)(2,1)S(1)}, u32[]{:S(2)}, u32[]{:S(2)}) %collective-permute-start.9) | collective-permute-done | bytes 81952 | tf_op jit(solution)/shard_map/ppermute | solution.py:466
  50.7 0.1 collective-permute-start.12
  50.7 1.6 %collective-permute-done.12.mate = bf16[1280,128]{1,0:T(8,128)(2,1)S(1)} collective-permute-done((bf16[1280,128]{1,0:T(8,128)(2,1)S(1)}, bf16[1280,128]{1,0:T(8,128)(2,1)S(1)}, u32[]{:S(2)}, u32[]{:S(2)}) %collective-permute-start.12) | collective-permute-done | bytes 327712 | tf_op jit(solution)/shard_map/ppermute | solution.py:468
  52.4 0.4 scatter.1
  52.7 3.4 %collective-permute-start.13 = (bf16[320,128]{1,0:T(8,128)(2,1)S(1)}, bf16[320,128]{1,0:T(8,128)(2,1)S(1)}, u32[]{:S(2)}, u32[]{:S(2)}) collective-permute-start(bf16[320,128]{1,0:T(8,128)(2,1)S(1)} %get-tuple-element.54), channel_id=1, source_target_pairs={{0,24},{1,25},{2,26},{3,27},{4,28},{5,29},{6,30},{7,31},{8,0},{9,1... | collective-permute-start | bytes 245768 | tf_op jit(solution)/shard_map/ppermute | solution.py:481
  56.1 1.1 %collective-permute-start.15 = (bf16[320,128]{1,0:T(8,128)(2,1)S(1)}, bf16[320,128]{1,0:T(8,128)(2,1)S(1)}, u32[]{:S(2)}, u32[]{:S(2)}) collective-permute-start(bf16[320,128]{1,0:T(8,128)(2,1)S(1)} %get-tuple-element.56), channel_id=1, source_target_pairs={{0,8},{1,9},{2,10},{3,11},{4,12},{5,13},{6,14},{7,15},{8,16},{9,17... | collective-permute-start | bytes 245768 | tf_op jit(solution)/shard_map/ppermute | solution.py:481
  57.2 2.9 %last_adjoint.1 = bf16[32,128,128]{2,1,0:T(8,128)(2,1)} custom-call(bf16[2176,256]{1,0:T(8,128)(2,1)S(1)} %get-tuple-element.51.act0, f32[4352,128]{1,0:T(8,128)S(1)} %get-tuple-element.52.grad1, bf16[3,3,3,128,128]{4,3,2,1,0:T(8,128)(2,1)S(1)} %copy-done.3), custom_call_target="tpu_custom_call" | custom-call | flops 3000000000 | bytes 6291456 | tf_op jit(solution)/shard_map/last_adjoint/pallas_call | solution.py:482
  60.1 4.1 %collective-permute-done.14 = bf16[320,128]{1,0:T(8,128)(2,1)S(1)} collective-permute-done((bf16[320,128]{1,0:T(8,128)(2,1)S(1)}, bf16[320,128]{1,0:T(8,128)(2,1)S(1)}, u32[]{:S(2)}, u32[]{:S(2)}) %collective-permute-start.14) | collective-permute-done | bytes 81952 | tf_op jit(solution)/shard_map/ppermute | solution.py:481
  64.2 0.7 %convert_add_fusion = f32[320,128]{1,0:T(8,128)} fusion(bf16[320,128]{1,0:T(8,128)(2,1)S(1)} %collective-permute-done.15, bf16[320,128]{1,0:T(8,128)(2,1)S(1)} %collective-permute-done.14, bf16[320,128]{1,0:T(8,128)(2,1)S(1)} %collective-permute-done.13, bf16[320,128]{1,0:T(8,128)(2,1)S(1)} %get-tuple-element.53), kind=kLoop, calls=%fused_computation.9 | loop fusion | flops 286720 | bytes 491520 | tf_op jit(solution)/shard_map/add | solution.py:491
  (45 shorter events, 0.2 us)
Async XLA Ops:
  0.6 12.7 %slice-start.4 = ((s32[32,128]{1,0:T(8,128)}), s32[8,128]{1,0:T(8,128)S(1)}, s32[]{:S(2)}) async-start(s32[32,128]{1,0:T(8,128)} %mask.1), calls=%async_computation.5 | async-start | bytes 8192 | tf_op jit(solution)/shard_map/slice | solution.py:379
  0.6 12.7 %slice-start.5 = ((s32[32,128]{1,0:T(8,128)}), s32[8,128]{1,0:T(8,128)S(1)}, s32[]{:S(2)}) async-start(s32[32,128]{1,0:T(8,128)} %mask.1), calls=%async_computation.6 | async-start | bytes 8192 | tf_op jit(solution)/shard_map/slice | solution.py:379
  0.7 12.7 %slice-start.2 = ((bf16[32,128,128]{2,1,0:T(8,128)(2,1)}), bf16[3,128,128]{2,1,0:T(8,128)(2,1)S(1)}, s32[]{:S(2)}) async-start(bf16[32,128,128]{2,1,0:T(8,128)(2,1)} %refs_10_.1), calls=%async_computation.3 | async-start | bytes 196608 | tf_op jit(solution)/shard_map/slice | solution.py:379
  0.7 12.7 %slice-start.3 = ((bf16[32,128,128]{2,1,0:T(8,128)(2,1)}), bf16[3,128,128]{2,1,0:T(8,128)(2,1)S(1)}, s32[]{:S(2)}) async-start(bf16[32,128,128]{2,1,0:T(8,128)(2,1)} %refs_10_.1), calls=%async_computation.4 | async-start | bytes 196608 | tf_op jit(solution)/shard_map/slice | solution.py:379
  0.7 12.7 %slice-start = ((bf16[32,128,128]{2,1,0:T(8,128)(2,1)}), bf16[6,128,128]{2,1,0:T(8,128)(2,1)S(1)}, s32[]{:S(2)}) async-start(bf16[32,128,128]{2,1,0:T(8,128)(2,1)} %ice.1), calls=%async_computation.1 | async-start | bytes 393216 | tf_op jit(solution)/shard_map/slice | solution.py:379
  0.7 12.7 %slice-start.1 = ((bf16[32,128,128]{2,1,0:T(8,128)(2,1)}), bf16[6,128,128]{2,1,0:T(8,128)(2,1)S(1)}, s32[]{:S(2)}) async-start(bf16[32,128,128]{2,1,0:T(8,128)(2,1)} %ice.1), calls=%async_computation.2 | async-start | bytes 393216 | tf_op jit(solution)/shard_map/slice | solution.py:379
  0.7 14.5 %collective-permute-start.2 = (bf16[320,128]{1,0:T(8,128)(2,1)}, bf16[320,128]{1,0:T(8,128)(2,1)S(1)}, u32[]{:S(2)}, u32[]{:S(2)}) collective-permute-start(bf16[320,128]{1,0:T(8,128)(2,1)} %bitcast.19), channel_id=1, source_target_pairs={{0,24},{1,25},{2,26},{3,27},{4,28},{5,29},{6,30},{7,31},{8,0},{9,1... | collective-permute-start | bytes 245768 | tf_op jit(solution)/shard_map/ppermute | solution.py:372
  5.8 9.4 %collective-permute-start.1 = (bf16[320,128]{1,0:T(8,128)(2,1)}, bf16[320,128]{1,0:T(8,128)(2,1)S(1)}, u32[]{:S(2)}, u32[]{:S(2)}) collective-permute-start(bf16[320,128]{1,0:T(8,128)(2,1)} %bitcast.20), channel_id=1, source_target_pairs={{0,16},{1,17},{2,18},{3,19},{4,20},{5,21},{6,22},{7,23},{8,24},{9,... | collective-permute-start | bytes 245768 | tf_op jit(solution)/shard_map/ppermute | solution.py:372
  5.8 9.4 %collective-permute-start = (bf16[320,128]{1,0:T(8,128)(2,1)}, bf16[320,128]{1,0:T(8,128)(2,1)S(1)}, u32[]{:S(2)}, u32[]{:S(2)}) collective-permute-start(bf16[320,128]{1,0:T(8,128)(2,1)} %bitcast.21), channel_id=1, source_target_pairs={{0,8},{1,9},{2,10},{3,11},{4,12},{5,13},{6,14},{7,15},{8,16},{9,17... | collective-permute-start | bytes 245768 | tf_op jit(solution)/shard_map/ppermute | solution.py:372
  8.2 7.0 %copy-start.7 = (bf16[4,8,10,128]{3,1,2,0:T(8,128)(2,1)S(1)}, bf16[4,8,10,128]{3,1,2,0:T(8,128)(2,1)}, u32[]{:S(2)}) copy-start(bf16[4,8,10,128]{3,1,2,0:T(8,128)(2,1)} %param.12) | copy-start | bytes 245764
  8.2 13.4 %all-to-all-start = ((f32[32,8,128]{2,1,0:T(8,128)}), f32[32,8,128]{2,1,0:T(8,128)S(1)}, u32[]{:S(2)}, u32[]{:S(2)}) async-start(f32[32,8,128]{2,1,0:T(8,128)} %broadcast_in_dim.10), calls=%async_computation | async-start | bytes 262144 | tf_op jit(solution)/shard_map/all_to_all | solution.py:370
  14.3 12.3 %collective-permute-start.7 = (bf16[1168,128]{1,0:T(8,128)(2,1)}, bf16[1168,128]{1,0:T(8,128)(2,1)S(1)}, u32[]{:S(2)}, u32[]{:S(2)}) collective-permute-start(bf16[1168,128]{1,0:T(8,128)(2,1)} %get-tuple-element.38), channel_id=1, source_target_pairs={{0,1},{1,0},{2,3},{3,2},{4,5},{5,4},{6,7},{7,6},{8,9},{9,8},{10,11... | collective-permute-start | bytes 897032 | tf_op jit(solution)/shard_map/ppermute | solution.py:410
  14.6 12.0 %collective-permute-start.8 = (bf16[1168,128]{1,0:T(8,128)(2,1)}, bf16[1168,128]{1,0:T(8,128)(2,1)S(1)}, u32[]{:S(2)}, u32[]{:S(2)}) collective-permute-start(bf16[1168,128]{1,0:T(8,128)(2,1)} %get-tuple-element.39), channel_id=1, source_target_pairs={{1,2},{3,4},{5,6},{7,8},{9,10},{11,12},{13,14},{15,16},{17,18},{19... | collective-permute-start | bytes 897032 | tf_op jit(solution)/shard_map/ppermute | solution.py:412
  15.3 11.3 %copy-start = (bf16[32,128,128]{2,1,0:T(8,128)(2,1)S(1)}, bf16[32,128,128]{2,1,0:T(8,128)(2,1)}, u32[]{:S(2)}) copy-start(bf16[32,128,128]{2,1,0:T(8,128)(2,1)} %ice.1) | copy-start | bytes 3145732
  15.3 11.3 %copy-start.2 = (s32[32,128]{1,0:T(8,128)S(1)}, s32[32,128]{1,0:T(8,128)}, u32[]{:S(2)}) copy-start(s32[32,128]{1,0:T(8,128)} %mask.1) | copy-start | bytes 49156
  15.3 11.3 %copy-start.3 = (bf16[3,3,3,128,128]{4,3,2,1,0:T(8,128)(2,1)S(1)}, bf16[3,3,3,128,128]{4,3,2,1,0:T(8,128)(2,1)}, u32[]{:S(2)}) copy-start(bf16[3,3,3,128,128]{4,3,2,1,0:T(8,128)(2,1)} %weight.3) | copy-start | bytes 2654212
  15.3 11.3 %copy-start.6 = (f32[3,128]{1,0:T(4,128)S(1)}, f32[3,128]{1,0:T(4,128)}, u32[]{:S(2)}) copy-start(f32[3,128]{1,0:T(4,128)} %refs_6_.1) | copy-start | bytes 4612
  15.3 7.2 %collective-permute-start.3 = (bf16[1280,128]{1,0:T(8,128)(2,1)S(1)}, bf16[1280,128]{1,0:T(8,128)(2,1)S(1)}, u32[]{:S(2)}, u32[]{:S(2)}) collective-permute-start(bf16[1280,128]{1,0:T(8,128)(2,1)S(1)} %pad_maximum_fusion.own), channel_id=1, source_target_pairs={{0,1},{1,0},{2,3},{3,2},{4,5},{5,4},{6,7},{7,6},{8,9},{9,8},{10,11... | collective-permute-start | bytes 983048 | tf_op jit(solution)/shard_map/ppermute | solution.py:374
  23.0 6.4 %collective-permute-start.4 = (bf16[480,128]{1,0:T(8,128)(2,1)S(1)}, bf16[480,128]{1,0:T(8,128)(2,1)S(1)}, u32[]{:S(2)}, u32[]{:S(2)}) collective-permute-start(bf16[480,128]{1,0:T(8,128)(2,1)S(1)} %get-tuple-element.32), channel_id=1, source_target_pairs={{0,2},{1,3},{2,0},{3,1},{4,6},{5,7},{6,4},{7,5},{8,10},{9,11},{10,... | collective-permute-start | bytes 368648 | tf_op jit(solution)/shard_map/ppermute | solution.py:414
  23.4 7.7 %collective-permute-start.5 = (bf16[480,128]{1,0:T(8,128)(2,1)S(1)}, bf16[480,128]{1,0:T(8,128)(2,1)S(1)}, u32[]{:S(2)}, u32[]{:S(2)}) collective-permute-start(bf16[480,128]{1,0:T(8,128)(2,1)S(1)} %get-tuple-element.33), channel_id=1, source_target_pairs={{0,4},{1,5},{2,6},{3,7},{4,0},{5,1},{6,2},{7,3},{8,12},{9,13},{10,... | collective-permute-start | bytes 368648 | tf_op jit(solution)/shard_map/ppermute | solution.py:414
  24.4 6.7 %copy-start.1 = (bf16[32,128,128]{2,1,0:T(8,128)(2,1)S(1)}, bf16[32,128,128]{2,1,0:T(8,128)(2,1)}, u32[]{:S(2)}) copy-start(bf16[32,128,128]{2,1,0:T(8,128)(2,1)} %refs_10_.1) | copy-start | bytes 3145732
  24.4 6.7 %copy-start.4 = (f32[128,128]{1,0:T(8,128)S(1)}, f32[128,128]{1,0:T(8,128)}, u32[]{:S(2)}) copy-start(f32[128,128]{1,0:T(8,128)} %refs_4_.1) | copy-start | bytes 196612
  24.4 6.7 %copy-start.5 = (bf16[10,128]{1,0:T(8,128)(2,1)S(1)}, bf16[10,128]{1,0:T(8,128)(2,1)}, u32[]{:S(2)}) copy-start(bf16[10,128]{1,0:T(8,128)(2,1)} %refs_5_.1) | copy-start | bytes 7684
  24.4 6.7 %collective-permute-start.6 = (bf16[480,128]{1,0:T(8,128)(2,1)S(1)}, bf16[480,128]{1,0:T(8,128)(2,1)S(1)}, u32[]{:S(2)}, u32[]{:S(2)}) collective-permute-start(bf16[480,128]{1,0:T(8,128)(2,1)S(1)} %get-tuple-element.34), channel_id=1, source_target_pairs={{0,6},{1,7},{2,4},{3,5},{4,2},{5,3},{6,0},{7,1},{8,14},{9,15},{10,... | collective-permute-start | bytes 368648 | tf_op jit(solution)/shard_map/ppermute | solution.py:414
  41.9 8.7 %collective-permute-start.11 = (bf16[320,128]{1,0:T(8,128)(2,1)S(1)}, bf16[320,128]{1,0:T(8,128)(2,1)S(1)}, u32[]{:S(2)}, u32[]{:S(2)}) collective-permute-start(bf16[320,128]{1,0:T(8,128)(2,1)S(1)} %get-tuple-element.46), channel_id=1, source_target_pairs={{0,6},{1,7},{2,4},{3,5},{4,2},{5,3},{6,0},{7,1},{8,14},{9,15},{10,... | collective-permute-start | bytes 245768 | tf_op jit(solution)/shard_map/ppermute | solution.py:466
  44.5 6.0 %collective-permute-start.10 = (bf16[320,128]{1,0:T(8,128)(2,1)S(1)}, bf16[320,128]{1,0:T(8,128)(2,1)S(1)}, u32[]{:S(2)}, u32[]{:S(2)}) collective-permute-start(bf16[320,128]{1,0:T(8,128)(2,1)S(1)} %get-tuple-element.46), channel_id=1, source_target_pairs={{0,4},{1,5},{2,6},{3,7},{4,0},{5,1},{6,2},{7,3},{8,12},{9,13},{10,... | collective-permute-start | bytes 245768 | tf_op jit(solution)/shard_map/ppermute | solution.py:466
  46.1 4.4 %collective-permute-start.9 = (bf16[320,128]{1,0:T(8,128)(2,1)S(1)}, bf16[320,128]{1,0:T(8,128)(2,1)S(1)}, u32[]{:S(2)}, u32[]{:S(2)}) collective-permute-start(bf16[320,128]{1,0:T(8,128)(2,1)S(1)} %get-tuple-element.46), channel_id=1, source_target_pairs={{0,2},{1,3},{2,0},{3,1},{4,6},{5,7},{6,4},{7,5},{8,10},{9,11},{10,... | collective-permute-start | bytes 245768 | tf_op jit(solution)/shard_map/ppermute | solution.py:466
  50.7 1.7 %collective-permute-start.12 = (bf16[1280,128]{1,0:T(8,128)(2,1)S(1)}, bf16[1280,128]{1,0:T(8,128)(2,1)S(1)}, u32[]{:S(2)}, u32[]{:S(2)}) collective-permute-start(bf16[1280,128]{1,0:T(8,128)(2,1)S(1)} %constant_dynamic-update-slice_fusion.own), channel_id=1, source_target_pairs={{0,1},{1,0},{2,3},{3,2},{4,5},{5,4},{6,7},{7,6},{8,9},{9,8},{10,11... | collective-permute-start | bytes 983048 | tf_op jit(solution)/shard_map/ppermute | solution.py:468
  52.7 7.4 %collective-permute-start.13 = (bf16[320,128]{1,0:T(8,128)(2,1)S(1)}, bf16[320,128]{1,0:T(8,128)(2,1)S(1)}, u32[]{:S(2)}, u32[]{:S(2)}) collective-permute-start(bf16[320,128]{1,0:T(8,128)(2,1)S(1)} %get-tuple-element.54), channel_id=1, source_target_pairs={{0,24},{1,25},{2,26},{3,27},{4,28},{5,29},{6,30},{7,31},{8,0},{9,1... | collective-permute-start | bytes 245768 | tf_op jit(solution)/shard_map/ppermute | solution.py:481
  56.1 8.0 %collective-permute-start.14 = (bf16[320,128]{1,0:T(8,128)(2,1)S(1)}, bf16[320,128]{1,0:T(8,128)(2,1)S(1)}, u32[]{:S(2)}, u32[]{:S(2)}) collective-permute-start(bf16[320,128]{1,0:T(8,128)(2,1)S(1)} %get-tuple-element.55), channel_id=1, source_target_pairs={{0,16},{1,17},{2,18},{3,19},{4,20},{5,21},{6,22},{7,23},{8,24},{9,... | collective-permute-start | bytes 245768 | tf_op jit(solution)/shard_map/ppermute | solution.py:481
  56.1 8.0 %collective-permute-start.15 = (bf16[320,128]{1,0:T(8,128)(2,1)S(1)}, bf16[320,128]{1,0:T(8,128)(2,1)S(1)}, u32[]{:S(2)}, u32[]{:S(2)}) collective-permute-start(bf16[320,128]{1,0:T(8,128)(2,1)S(1)} %get-tuple-element.56), channel_id=1, source_target_pairs={{0,8},{1,9},{2,10},{3,11},{4,12},{5,13},{6,14},{7,15},{8,16},{9,17... | collective-permute-start | bytes 245768 | tf_op jit(solution)/shard_map/ppermute | solution.py:481

commit v5 on v4

--- a/solution.py
+++ b/solution.py
@@ -14,6 +14,8 @@
 ROWS = 32
 EXT = 48
 PAD = 8
+SEEN = 42
+SHIP = 432
 GROUP = 8
 SENT = GROUP // 2
 STEP = 1
@@ -133,7 +135,7 @@
 
 
 def message_kernel(planes, picks, own, mate, *refs):
-    outs, wide = refs[:-1], refs[-1]
+    outs, wide, packed = refs[:-2], refs[-2], refs[-1]
     sources = planes * ROWS
     for side, block in enumerate((own, mate)):
         value = block[...].astype(F32)
@@ -142,9 +144,12 @@
                 value, f
             ).astype(BF)
     for f in range(F):
-        found = dot(picks[...], wide[:, f * C : (f + 1) * C]).astype(BF)
-        for n, out in enumerate(outs):
-            out[f * EXT : (f + 1) * EXT, :] = found[n * EXT : (n + 1) * EXT]
+        found = dot(picks[...], wide[:, f * C : (f + 1) * C])
+        for n in range(SENT):
+            packed[n, f * SEEN : (f + 1) * SEEN, :] = found[n * EXT + 3 : n * EXT + 3 + SEEN]
+    for n, out in enumerate(outs):
+        packed[n, F * SEEN :, :] = jnp.zeros((SHIP - F * SEEN, C), F32)
+        out[...] = packed[n].astype(BF)
 
 
 def fill_taps(taps, weight, l, back):
@@ -208,12 +213,12 @@
     for n, (l, back) in enumerate(((1, False), (2, False), (2, True), (1, True))):
         fill_taps(taps[n], weight, l, back)
     ice[...] = jnp.zeros(ice.shape, F32)
+    total = messages[0][...].astype(F32)
+    for s in range(1, SENT):
+        total += messages[s][...].astype(F32)
+    lifted[0:SHIP, 0:C] = total
     for f in range(F):
-        rows = slice(f * EXT, (f + 1) * EXT)
-        total = messages[0][rows, :].astype(F32)
-        for s in range(1, SENT):
-            total += messages[s][rows, :].astype(F32)
-        ice[:, f, :] = fine_dot(total, col_map[...])
+        ice[3 : 3 + SEEN, f, :] = fine_dot(lifted[f * SEEN : (f + 1) * SEEN, 0:C], col_map[...])
     diag[...] = jnp.zeros(diag.shape, BF)
     for j in range(GROUP):
         diag[j * FP : j * FP + F, j * C : (j + 1) * C] = lift[...]
@@ -399,8 +404,8 @@
     )(table)
     messages = pl.pallas_call(
         functools.partial(message_kernel, planes),
-        out_shape=tuple(shape(F * EXT, C) for _ in range(SENT)),
-        scratch_shapes=[pltpu.VMEM((2 * planes * ROWS, F * C), BF)],
+        out_shape=tuple(shape(SHIP, C) for _ in range(SENT)),
+        scratch_shapes=[pltpu.VMEM((2 * planes * ROWS, F * C), BF), pltpu.VMEM((SENT, SHIP, C), F32)],
         compiler_params=params(10),
         name="messages",
     )(picks, own_column, mate_column)

time: 65.1 us -> 65 us (level)
  no operation moved by 1% of the time
where the time goes in v5:
time: 65 us; the launch traced here: 64.8 us
  starting transfers between devices  27.4 us (42%)
  Pallas kernels  18.8 us (29%)
  waiting for transfers between devices  14.4 us (22%)
  other arithmetic  2.41 us (4%)
  between operations  0.96 us (1%)
  local copies, waits for them, and re-layouts  0.79 us (1%)
    pallas_call x1, Pallas kernels, body(): pl.pallas_call(main_kernel, out_shape=(shape(ROWS, C, C), shape(17 * C, P...  11.2 us
    ppermute x3, starting transfers between devices, body(): lax.ppermute(fields, 'tile', by_plane(z))  6.12 us
    all_to_all x1, starting transfers between devices, body(): table = lax.all_to_all(table, 'tile', 0, 0, tiled=True)  5.06 us
    ppermute x3, starting transfers between devices, body(): lax.ppermute(sums[z], 'tile', by_plane(-z))  4.48 us
    ppermute x3, waiting for transfers between devices, body(): lax.ppermute(project, 'tile', by_mate(2 * s))  4.43 us
    ppermute x3, starting transfers between devices, body(): lax.ppermute(project, 'tile', by_mate(2 * s))  4.17 us
    ppermute x3, waiting for transfers between devices, body(): lax.ppermute(sums[z], 'tile', by_plane(-z))  4.06 us
    ppermute x3, starting transfers between devices, body(): lax.ppermute(messages[s], 'tile', by_mate(2 * s))  3.55 us
  transfers between devices with their start and end apart: 17, of which 5 were waited for; matrix products, arithmetic and copies ran while one was open for 4% of the time, Pallas kernels for 11%

profile of v5, /device:TPU:0, one launch (start us, length us, event | category | flops | bytes accessed | tf_op | source)
XLA Modules:
  0.0 64.8 jit_solution(6219748230896201370)
XLA Ops:
  0.6 0.0 slice-start.4
  0.7 0.0 slice-start.2
  0.7 0.0 slice-start
  0.7 5.1 %collective-permute-start.2 = (bf16[320,128]{1,0:T(8,128)(2,1)}, bf16[320,128]{1,0:T(8,128)(2,1)S(1)}, u32[]{:S(2)}, u32[]{:S(2)}) collective-permute-start(bf16[320,128]{1,0:T(8,128)(2,1)} %bitcast.19), channel_id=1, source_target_pairs={{0,24},{1,25},{2,26},{3,27},{4,28},{5,29},{6,30},{7,31},{8,0},{9,1... | collective-permute-start | bytes 245768 | tf_op jit(solution)/shard_map/ppermute | solution.py:377
  5.8 1.0 %collective-permute-start = (bf16[320,128]{1,0:T(8,128)(2,1)}, bf16[320,128]{1,0:T(8,128)(2,1)S(1)}, u32[]{:S(2)}, u32[]{:S(2)}) collective-permute-start(bf16[320,128]{1,0:T(8,128)(2,1)} %bitcast.21), channel_id=1, source_target_pairs={{0,8},{1,9},{2,10},{3,11},{4,12},{5,13},{6,14},{7,15},{8,16},{9,17... | collective-permute-start | bytes 245768 | tf_op jit(solution)/shard_map/ppermute | solution.py:377
  6.8 0.7 %pad_add_fusion = f32[8,128]{1,0:T(8,128)S(1)} fusion(f32[4,32]{1,0:T(4,128)} %bitcast.23, s32[4,32]{1,0:T(4,128)} %bitcast.24, s32[4,32]{1,0:T(4,128)} %bitcast.25, s32[4,32]{1,0:T(4,128)} %bitcast.26), kind=kLoop, calls=%fused_computation.14 | loop fusion | flops 6144 | bytes 6144 | tf_op jit(solution)/shard_map/add | solution.py:373
  7.6 0.7 %broadcast_in_dim.10 = f32[32,8,128]{2,1,0:T(8,128)} broadcast(f32[8,128]{1,0:T(8,128)S(1)} %pad_add_fusion), dimensions={1,2} | broadcast | bytes 135168 | tf_op jit(solution)/shard_map/broadcast_in_dim | solution.py:370
  8.2 5.1 %all-to-all-start = ((f32[32,8,128]{2,1,0:T(8,128)}), f32[32,8,128]{2,1,0:T(8,128)S(1)}, u32[]{:S(2)}, u32[]{:S(2)}) async-start(f32[32,8,128]{2,1,0:T(8,128)} %broadcast_in_dim.10), calls=%async_computation | async-start | bytes 262144 | tf_op jit(solution)/shard_map/all_to_all | solution.py:375
  13.4 0.9 %broadcast_select_fusion = (bf16[1168,128]{1,0:T(8,128)(2,1)}, bf16[1168,128]{1,0:T(8,128)(2,1)}) fusion(pred[]{:T(512)S(6)} %eq.9, s32[8,128]{1,0:T(8,128)S(1)} %slice-done.4, bf16[384,128]{1,0:T(8,128)(2,1)S(1)} %bitcast.16, bf16[768,128]{1,0:T(8,128)(2,1)S(1)} %bitcast.14, s32[8,128]{1,0:T(8,128)S(1)} %slice-done.5, bf16[384,128]{1,0:T(8,128)(2,1)S(1)} %bitcast.17, ...), kind=kLoop, calls=%fused_computation.7 | loop fusion | flops 2990080 | bytes 1196033 | tf_op jit(solution)/shard_map/jit(_where)/select_n | solution.py:413
  14.3 0.3 collective-permute-start.7
  14.6 0.7 %collective-permute-start.8 = (bf16[1168,128]{1,0:T(8,128)(2,1)}, bf16[1168,128]{1,0:T(8,128)(2,1)S(1)}, u32[]{:S(2)}, u32[]{:S(2)}) collective-permute-start(bf16[1168,128]{1,0:T(8,128)(2,1)} %get-tuple-element.39), channel_id=1, source_target_pairs={{1,2},{3,4},{5,6},{7,8},{9,10},{11,12},{13,14},{15,16},{17,18},{19... | collective-permute-start | bytes 897032 | tf_op jit(solution)/shard_map/ppermute | solution.py:417
  15.3 3.1 %collective-permute-start.3 = (bf16[1280,128]{1,0:T(8,128)(2,1)S(1)}, bf16[1280,128]{1,0:T(8,128)(2,1)S(1)}, u32[]{:S(2)}, u32[]{:S(2)}) collective-permute-start(bf16[1280,128]{1,0:T(8,128)(2,1)S(1)} %pad_maximum_fusion.own), channel_id=1, source_target_pairs={{0,1},{1,0},{2,3},{3,2},{4,5},{5,4},{6,7},{7,6},{8,9},{9,8},{10,11... | collective-permute-start | bytes 983048 | tf_op jit(solution)/shard_map/ppermute | solution.py:379
  18.4 3.2 %all-to-all-done.table = f32[32,8,128]{2,1,0:T(8,128)S(1)} async-done(((f32[32,8,128]{2,1,0:T(8,128)}), f32[32,8,128]{2,1,0:T(8,128)S(1)}, u32[]{:S(2)}, u32[]{:S(2)}) %all-to-all-start) | async-done | bytes 131104 | tf_op jit(solution)/shard_map/all_to_all | solution.py:375
  21.6 0.9 %picks.1 = (bf16[192,256]{1,0:T(8,128)(2,1)S(1)}, bf16[128,256]{1,0:T(8,128)(2,1)S(1)}) custom-call(f32[32,8,128]{2,1,0:T(8,128)S(1)} %all-to-all-done.table), custom_call_target="tpu_custom_call" | custom-call | flops 10000000000 | bytes 1048576 | tf_op jit(solution)/shard_map/picks/pallas_call | solution.py:398
  22.5 0.6 messages.1
  23.1 0.4 collective-permute-start.4
  23.5 1.0 %collective-permute-start.5 = (bf16[432,128]{1,0:T(8,128)(2,1)S(1)}, bf16[432,128]{1,0:T(8,128)(2,1)S(1)}, u32[]{:S(2)}, u32[]{:S(2)}) collective-permute-start(bf16[432,128]{1,0:T(8,128)(2,1)S(1)} %get-tuple-element.33), channel_id=1, source_target_pairs={{0,4},{1,5},{2,6},{3,7},{4,0},{5,1},{6,2},{7,3},{8,12},{9,13},{10,... | collective-permute-start | bytes 331784 | tf_op jit(solution)/shard_map/ppermute | solution.py:419
  24.5 2.2 %collective-permute-start.6 = (bf16[432,128]{1,0:T(8,128)(2,1)S(1)}, bf16[432,128]{1,0:T(8,128)(2,1)S(1)}, u32[]{:S(2)}, u32[]{:S(2)}) collective-permute-start(bf16[432,128]{1,0:T(8,128)(2,1)S(1)} %get-tuple-element.34), channel_id=1, source_target_pairs={{0,6},{1,7},{2,4},{3,5},{4,2},{5,3},{6,0},{7,1},{8,14},{9,15},{10,... | collective-permute-start | bytes 331784 | tf_op jit(solution)/shard_map/ppermute | solution.py:419
  26.7 2.9 %first_layer.1 = (bf16[2688,256]{1,0:T(8,128)(2,1)S(1)}, bf16[2688,256]{1,0:T(8,128)(2,1)S(1)}, bf16[5376,128]{1,0:T(8,128)(2,1)S(1)}) custom-call(bf16[32,128,128]{2,1,0:T(8,128)(2,1)S(1)} %copy-done, bf16[1168,128]{1,0:T(8,128)(2,1)S(1)} %collective-permute-done.7.pair.refs_11_, bf16[1168,128]{1,0:T(8,128)(2,1)S(1)} %collective-permute-done.8.other.refs_12_, ...), custom_call_target="tpu_custom_call" | custom-call | flops 4000000000 | bytes 8388608 | tf_op jit(solution)/shard_map/first_layer/pallas_call | solution.py:421
  29.6 1.1 %collective-permute-done.5.refs_2_ = bf16[432,128]{1,0:T(8,128)(2,1)S(1)} collective-permute-done((bf16[432,128]{1,0:T(8,128)(2,1)S(1)}, bf16[432,128]{1,0:T(8,128)(2,1)S(1)}, u32[]{:S(2)}, u32[]{:S(2)}) %collective-permute-start.5) | collective-permute-done | bytes 110624 | tf_op jit(solution)/shard_map/ppermute | solution.py:419
  30.7 11.2 %middle_layers.1 = (bf16[32,128,128]{2,1,0:T(8,128)(2,1)}, bf16[2176,256]{1,0:T(8,128)(2,1)S(1)}, f32[4352,128]{1,0:T(8,128)S(1)}, bf16[320,128]{1,0:T(8,128)(2,1)S(1)}) custom-call(bf16[432,128]{1,0:T(8,128)(2,1)S(1)} %get-tuple-element.31.refs_0_, bf16[432,128]{1,0:T(8,128)(2,1)S(1)} %collective-permute-done.4.refs_1_, ...), custom_call_target="tpu_custom_call" | custom-call | flops 12000000000 | bytes 16777216 | tf_op jit(solution)/shard_map/middle_layers/pallas_call | solution.py:430
  41.9 2.7 %collective-permute-start.11 = (bf16[320,128]{1,0:T(8,128)(2,1)S(1)}, bf16[320,128]{1,0:T(8,128)(2,1)S(1)}, u32[]{:S(2)}, u32[]{:S(2)}) collective-permute-start(bf16[320,128]{1,0:T(8,128)(2,1)S(1)} %get-tuple-element.46), channel_id=1, source_target_pairs={{0,6},{1,7},{2,4},{3,5},{4,2},{5,3},{6,0},{7,1},{8,14},{9,15},{10,... | collective-permute-start | bytes 245768 | tf_op jit(solution)/shard_map/ppermute | solution.py:471
  44.6 1.5 %collective-permute-start.10 = (bf16[320,128]{1,0:T(8,128)(2,1)S(1)}, bf16[320,128]{1,0:T(8,128)(2,1)S(1)}, u32[]{:S(2)}, u32[]{:S(2)}) collective-permute-start(bf16[320,128]{1,0:T(8,128)(2,1)S(1)} %get-tuple-element.46), channel_id=1, source_target_pairs={{0,4},{1,5},{2,6},{3,7},{4,0},{5,1},{6,2},{7,3},{8,12},{9,13},{10,... | collective-permute-start | bytes 245768 | tf_op jit(solution)/shard_map/ppermute | solution.py:471
  46.1 4.4 %collective-permute-done.9 = bf16[320,128]{1,0:T(8,128)(2,1)S(1)} collective-permute-done((bf16[320,128]{1,0:T(8,128)(2,1)S(1)}, bf16[320,128]{1,0:T(8,128)(2,1)S(1)}, u32[]{:S(2)}, u32[]{:S(2)}) %collective-permute-start.9) | collective-permute-done | bytes 81952 | tf_op jit(solution)/shard_map/ppermute | solution.py:471
  50.6 0.1 collective-permute-start.12
  50.7 1.6 %collective-permute-done.12.mate = bf16[1280,128]{1,0:T(8,128)(2,1)S(1)} collective-permute-done((bf16[1280,128]{1,0:T(8,128)(2,1)S(1)}, bf16[1280,128]{1,0:T(8,128)(2,1)S(1)}, u32[]{:S(2)}, u32[]{:S(2)}) %collective-permute-start.12) | collective-permute-done | bytes 327712 | tf_op jit(solution)/shard_map/ppermute | solution.py:473
  52.3 0.4 scatter.1
  52.7 3.4 %collective-permute-start.13 = (bf16[320,128]{1,0:T(8,128)(2,1)S(1)}, bf16[320,128]{1,0:T(8,128)(2,1)S(1)}, u32[]{:S(2)}, u32[]{:S(2)}) collective-permute-start(bf16[320,128]{1,0:T(8,128)(2,1)S(1)} %get-tuple-element.54), channel_id=1, source_target_pairs={{0,24},{1,25},{2,26},{3,27},{4,28},{5,29},{6,30},{7,31},{8,0},{9,1... | collective-permute-start | bytes 245768 | tf_op jit(solution)/shard_map/ppermute | solution.py:486
  56.1 1.1 %collective-permute-start.15 = (bf16[320,128]{1,0:T(8,128)(2,1)S(1)}, bf16[320,128]{1,0:T(8,128)(2,1)S(1)}, u32[]{:S(2)}, u32[]{:S(2)}) collective-permute-start(bf16[320,128]{1,0:T(8,128)(2,1)S(1)} %get-tuple-element.56), channel_id=1, source_target_pairs={{0,8},{1,9},{2,10},{3,11},{4,12},{5,13},{6,14},{7,15},{8,16},{9,17... | collective-permute-start | bytes 245768 | tf_op jit(solution)/shard_map/ppermute | solution.py:486
  57.1 2.9 %last_adjoint.1 = bf16[32,128,128]{2,1,0:T(8,128)(2,1)} custom-call(bf16[2176,256]{1,0:T(8,128)(2,1)S(1)} %get-tuple-element.51.act0, f32[4352,128]{1,0:T(8,128)S(1)} %get-tuple-element.52.grad1, bf16[3,3,3,128,128]{4,3,2,1,0:T(8,128)(2,1)S(1)} %copy-done.3), custom_call_target="tpu_custom_call" | custom-call | flops 3000000000 | bytes 6291456 | tf_op jit(solution)/shard_map/last_adjoint/pallas_call | solution.py:487
  60.0 4.1 %collective-permute-done.14 = bf16[320,128]{1,0:T(8,128)(2,1)S(1)} collective-permute-done((bf16[320,128]{1,0:T(8,128)(2,1)S(1)}, bf16[320,128]{1,0:T(8,128)(2,1)S(1)}, u32[]{:S(2)}, u32[]{:S(2)}) %collective-permute-start.14) | collective-permute-done | bytes 81952 | tf_op jit(solution)/shard_map/ppermute | solution.py:486
  64.1 0.7 %convert_add_fusion = f32[320,128]{1,0:T(8,128)} fusion(bf16[320,128]{1,0:T(8,128)(2,1)S(1)} %collective-permute-done.15, bf16[320,128]{1,0:T(8,128)(2,1)S(1)} %collective-permute-done.14, bf16[320,128]{1,0:T(8,128)(2,1)S(1)} %collective-permute-done.13, bf16[320,128]{1,0:T(8,128)(2,1)S(1)} %get-tuple-element.53), kind=kLoop, calls=%fused_computation.9 | loop fusion | flops 286720 | bytes 491520 | tf_op jit(solution)/shard_map/add | solution.py:496
  (45 shorter events, 0.2 us)
Async XLA Ops:
  0.6 12.7 %slice-start.4 = ((s32[32,128]{1,0:T(8,128)}), s32[8,128]{1,0:T(8,128)S(1)}, s32[]{:S(2)}) async-start(s32[32,128]{1,0:T(8,128)} %mask.1), calls=%async_computation.5 | async-start | bytes 8192 | tf_op jit(solution)/shard_map/slice | solution.py:384
  0.6 12.7 %slice-start.5 = ((s32[32,128]{1,0:T(8,128)}), s32[8,128]{1,0:T(8,128)S(1)}, s32[]{:S(2)}) async-start(s32[32,128]{1,0:T(8,128)} %mask.1), calls=%async_computation.6 | async-start | bytes 8192 | tf_op jit(solution)/shard_map/slice | solution.py:384
  0.7 12.7 %slice-start.2 = ((bf16[32,128,128]{2,1,0:T(8,128)(2,1)}), bf16[3,128,128]{2,1,0:T(8,128)(2,1)S(1)}, s32[]{:S(2)}) async-start(bf16[32,128,128]{2,1,0:T(8,128)(2,1)} %refs_10_.1), calls=%async_computation.3 | async-start | bytes 196608 | tf_op jit(solution)/shard_map/slice | solution.py:384
  0.7 12.7 %slice-start.3 = ((bf16[32,128,128]{2,1,0:T(8,128)(2,1)}), bf16[3,128,128]{2,1,0:T(8,128)(2,1)S(1)}, s32[]{:S(2)}) async-start(bf16[32,128,128]{2,1,0:T(8,128)(2,1)} %refs_10_.1), calls=%async_computation.4 | async-start | bytes 196608 | tf_op jit(solution)/shard_map/slice | solution.py:384
  0.7 12.7 %slice-start = ((bf16[32,128,128]{2,1,0:T(8,128)(2,1)}), bf16[6,128,128]{2,1,0:T(8,128)(2,1)S(1)}, s32[]{:S(2)}) async-start(bf16[32,128,128]{2,1,0:T(8,128)(2,1)} %ice.1), calls=%async_computation.1 | async-start | bytes 393216 | tf_op jit(solution)/shard_map/slice | solution.py:384
  0.7 12.7 %slice-start.1 = ((bf16[32,128,128]{2,1,0:T(8,128)(2,1)}), bf16[6,128,128]{2,1,0:T(8,128)(2,1)S(1)}, s32[]{:S(2)}) async-start(bf16[32,128,128]{2,1,0:T(8,128)(2,1)} %ice.1), calls=%async_computation.2 | async-start | bytes 393216 | tf_op jit(solution)/shard_map/slice | solution.py:384
  0.7 14.5 %collective-permute-start.2 = (bf16[320,128]{1,0:T(8,128)(2,1)}, bf16[320,128]{1,0:T(8,128)(2,1)S(1)}, u32[]{:S(2)}, u32[]{:S(2)}) collective-permute-start(bf16[320,128]{1,0:T(8,128)(2,1)} %bitcast.19), channel_id=1, source_target_pairs={{0,24},{1,25},{2,26},{3,27},{4,28},{5,29},{6,30},{7,31},{8,0},{9,1... | collective-permute-start | bytes 245768 | tf_op jit(solution)/shard_map/ppermute | solution.py:377
  5.8 9.4 %collective-permute-start.1 = (bf16[320,128]{1,0:T(8,128)(2,1)}, bf16[320,128]{1,0:T(8,128)(2,1)S(1)}, u32[]{:S(2)}, u32[]{:S(2)}) collective-permute-start(bf16[320,128]{1,0:T(8,128)(2,1)} %bitcast.20), channel_id=1, source_target_pairs={{0,16},{1,17},{2,18},{3,19},{4,20},{5,21},{6,22},{7,23},{8,24},{9,... | collective-permute-start | bytes 245768 | tf_op jit(solution)/shard_map/ppermute | solution.py:377
  5.8 9.4 %collective-permute-start = (bf16[320,128]{1,0:T(8,128)(2,1)}, bf16[320,128]{1,0:T(8,128)(2,1)S(1)}, u32[]{:S(2)}, u32[]{:S(2)}) collective-permute-start(bf16[320,128]{1,0:T(8,128)(2,1)} %bitcast.21), channel_id=1, source_target_pairs={{0,8},{1,9},{2,10},{3,11},{4,12},{5,13},{6,14},{7,15},{8,16},{9,17... | collective-permute-start | bytes 245768 | tf_op jit(solution)/shard_map/ppermute | solution.py:377
  8.2 7.0 %copy-start.7 = (bf16[4,8,10,128]{3,1,2,0:T(8,128)(2,1)S(1)}, bf16[4,8,10,128]{3,1,2,0:T(8,128)(2,1)}, u32[]{:S(2)}) copy-start(bf16[4,8,10,128]{3,1,2,0:T(8,128)(2,1)} %param.12) | copy-start | bytes 245764
  8.2 13.4 %all-to-all-start = ((f32[32,8,128]{2,1,0:T(8,128)}), f32[32,8,128]{2,1,0:T(8,128)S(1)}, u32[]{:S(2)}, u32[]{:S(2)}) async-start(f32[32,8,128]{2,1,0:T(8,128)} %broadcast_in_dim.10), calls=%async_computation | async-start | bytes 262144 | tf_op jit(solution)/shard_map/all_to_all | solution.py:375
  14.3 12.4 %collective-permute-start.7 = (bf16[1168,128]{1,0:T(8,128)(2,1)}, bf16[1168,128]{1,0:T(8,128)(2,1)S(1)}, u32[]{:S(2)}, u32[]{:S(2)}) collective-permute-start(bf16[1168,128]{1,0:T(8,128)(2,1)} %get-tuple-element.38), channel_id=1, source_target_pairs={{0,1},{1,0},{2,3},{3,2},{4,5},{5,4},{6,7},{7,6},{8,9},{9,8},{10,11... | collective-permute-start | bytes 897032 | tf_op jit(solution)/shard_map/ppermute | solution.py:415
  14.6 12.1 %collective-permute-start.8 = (bf16[1168,128]{1,0:T(8,128)(2,1)}, bf16[1168,128]{1,0:T(8,128)(2,1)S(1)}, u32[]{:S(2)}, u32[]{:S(2)}) collective-permute-start(bf16[1168,128]{1,0:T(8,128)(2,1)} %get-tuple-element.39), channel_id=1, source_target_pairs={{1,2},{3,4},{5,6},{7,8},{9,10},{11,12},{13,14},{15,16},{17,18},{19... | collective-permute-start | bytes 897032 | tf_op jit(solution)/shard_map/ppermute | solution.py:417
  15.3 11.4 %copy-start = (bf16[32,128,128]{2,1,0:T(8,128)(2,1)S(1)}, bf16[32,128,128]{2,1,0:T(8,128)(2,1)}, u32[]{:S(2)}) copy-start(bf16[32,128,128]{2,1,0:T(8,128)(2,1)} %ice.1) | copy-start | bytes 3145732
  15.3 11.4 %copy-start.2 = (s32[32,128]{1,0:T(8,128)S(1)}, s32[32,128]{1,0:T(8,128)}, u32[]{:S(2)}) copy-start(s32[32,128]{1,0:T(8,128)} %mask.1) | copy-start | bytes 49156
  15.3 11.4 %copy-start.3 = (bf16[3,3,3,128,128]{4,3,2,1,0:T(8,128)(2,1)S(1)}, bf16[3,3,3,128,128]{4,3,2,1,0:T(8,128)(2,1)}, u32[]{:S(2)}) copy-start(bf16[3,3,3,128,128]{4,3,2,1,0:T(8,128)(2,1)} %weight.3) | copy-start | bytes 2654212
  15.3 11.4 %copy-start.6 = (f32[3,128]{1,0:T(4,128)S(1)}, f32[3,128]{1,0:T(4,128)}, u32[]{:S(2)}) copy-start(f32[3,128]{1,0:T(4,128)} %refs_6_.1) | copy-start | bytes 4612
  15.3 7.2 %collective-permute-start.3 = (bf16[1280,128]{1,0:T(8,128)(2,1)S(1)}, bf16[1280,128]{1,0:T(8,128)(2,1)S(1)}, u32[]{:S(2)}, u32[]{:S(2)}) collective-permute-start(bf16[1280,128]{1,0:T(8,128)(2,1)S(1)} %pad_maximum_fusion.own), channel_id=1, source_target_pairs={{0,1},{1,0},{2,3},{3,2},{4,5},{5,4},{6,7},{7,6},{8,9},{9,8},{10,11... | collective-permute-start | bytes 983048 | tf_op jit(solution)/shard_map/ppermute | solution.py:379
  23.1 6.5 %collective-permute-start.4 = (bf16[432,128]{1,0:T(8,128)(2,1)S(1)}, bf16[432,128]{1,0:T(8,128)(2,1)S(1)}, u32[]{:S(2)}, u32[]{:S(2)}) collective-permute-start(bf16[432,128]{1,0:T(8,128)(2,1)S(1)} %get-tuple-element.32), channel_id=1, source_target_pairs={{0,2},{1,3},{2,0},{3,1},{4,6},{5,7},{6,4},{7,5},{8,10},{9,11},{10,... | collective-permute-start | bytes 331784 | tf_op jit(solution)/shard_map/ppermute | solution.py:419
  23.5 7.2 %collective-permute-start.5 = (bf16[432,128]{1,0:T(8,128)(2,1)S(1)}, bf16[432,128]{1,0:T(8,128)(2,1)S(1)}, u32[]{:S(2)}, u32[]{:S(2)}) collective-permute-start(bf16[432,128]{1,0:T(8,128)(2,1)S(1)} %get-tuple-element.33), channel_id=1, source_target_pairs={{0,4},{1,5},{2,6},{3,7},{4,0},{5,1},{6,2},{7,3},{8,12},{9,13},{10,... | collective-permute-start | bytes 331784 | tf_op jit(solution)/shard_map/ppermute | solution.py:419
  24.5 6.2 %copy-start.1 = (bf16[32,128,128]{2,1,0:T(8,128)(2,1)S(1)}, bf16[32,128,128]{2,1,0:T(8,128)(2,1)}, u32[]{:S(2)}) copy-start(bf16[32,128,128]{2,1,0:T(8,128)(2,1)} %refs_10_.1) | copy-start | bytes 3145732
  24.5 6.2 %copy-start.4 = (f32[128,128]{1,0:T(8,128)S(1)}, f32[128,128]{1,0:T(8,128)}, u32[]{:S(2)}) copy-start(f32[128,128]{1,0:T(8,128)} %refs_4_.1) | copy-start | bytes 196612
  24.5 6.2 %copy-start.5 = (bf16[10,128]{1,0:T(8,128)(2,1)S(1)}, bf16[10,128]{1,0:T(8,128)(2,1)}, u32[]{:S(2)}) copy-start(bf16[10,128]{1,0:T(8,128)(2,1)} %refs_5_.1) | copy-start | bytes 7684
  24.5 6.2 %collective-permute-start.6 = (bf16[432,128]{1,0:T(8,128)(2,1)S(1)}, bf16[432,128]{1,0:T(8,128)(2,1)S(1)}, u32[]{:S(2)}, u32[]{:S(2)}) collective-permute-start(bf16[432,128]{1,0:T(8,128)(2,1)S(1)} %get-tuple-element.34), channel_id=1, source_target_pairs={{0,6},{1,7},{2,4},{3,5},{4,2},{5,3},{6,0},{7,1},{8,14},{9,15},{10,... | collective-permute-start | bytes 331784 | tf_op jit(solution)/shard_map/ppermute | solution.py:419
  41.9 8.7 %collective-permute-start.11 = (bf16[320,128]{1,0:T(8,128)(2,1)S(1)}, bf16[320,128]{1,0:T(8,128)(2,1)S(1)}, u32[]{:S(2)}, u32[]{:S(2)}) collective-permute-start(bf16[320,128]{1,0:T(8,128)(2,1)S(1)} %get-tuple-element.46), channel_id=1, source_target_pairs={{0,6},{1,7},{2,4},{3,5},{4,2},{5,3},{6,0},{7,1},{8,14},{9,15},{10,... | collective-permute-start | bytes 245768 | tf_op jit(solution)/shard_map/ppermute | solution.py:471
  44.6 5.9 %collective-permute-start.10 = (bf16[320,128]{1,0:T(8,128)(2,1)S(1)}, bf16[320,128]{1,0:T(8,128)(2,1)S(1)}, u32[]{:S(2)}, u32[]{:S(2)}) collective-permute-start(bf16[320,128]{1,0:T(8,128)(2,1)S(1)} %get-tuple-element.46), channel_id=1, source_target_pairs={{0,4},{1,5},{2,6},{3,7},{4,0},{5,1},{6,2},{7,3},{8,12},{9,13},{10,... | collective-permute-start | bytes 245768 | tf_op jit(solution)/shard_map/ppermute | solution.py:471
  46.1 4.4 %collective-permute-start.9 = (bf16[320,128]{1,0:T(8,128)(2,1)S(1)}, bf16[320,128]{1,0:T(8,128)(2,1)S(1)}, u32[]{:S(2)}, u32[]{:S(2)}) collective-permute-start(bf16[320,128]{1,0:T(8,128)(2,1)S(1)} %get-tuple-element.46), channel_id=1, source_target_pairs={{0,2},{1,3},{2,0},{3,1},{4,6},{5,7},{6,4},{7,5},{8,10},{9,11},{10,... | collective-permute-start | bytes 245768 | tf_op jit(solution)/shard_map/ppermute | solution.py:471
  50.6 1.7 %collective-permute-start.12 = (bf16[1280,128]{1,0:T(8,128)(2,1)S(1)}, bf16[1280,128]{1,0:T(8,128)(2,1)S(1)}, u32[]{:S(2)}, u32[]{:S(2)}) collective-permute-start(bf16[1280,128]{1,0:T(8,128)(2,1)S(1)} %constant_dynamic-update-slice_fusion.own), channel_id=1, source_target_pairs={{0,1},{1,0},{2,3},{3,2},{4,5},{5,4},{6,7},{7,6},{8,9},{9,8},{10,11... | collective-permute-start | bytes 983048 | tf_op jit(solution)/shard_map/ppermute | solution.py:473
  52.7 7.4 %collective-permute-start.13 = (bf16[320,128]{1,0:T(8,128)(2,1)S(1)}, bf16[320,128]{1,0:T(8,128)(2,1)S(1)}, u32[]{:S(2)}, u32[]{:S(2)}) collective-permute-start(bf16[320,128]{1,0:T(8,128)(2,1)S(1)} %get-tuple-element.54), channel_id=1, source_target_pairs={{0,24},{1,25},{2,26},{3,27},{4,28},{5,29},{6,30},{7,31},{8,0},{9,1... | collective-permute-start | bytes 245768 | tf_op jit(solution)/shard_map/ppermute | solution.py:486
  56.1 8.0 %collective-permute-start.14 = (bf16[320,128]{1,0:T(8,128)(2,1)S(1)}, bf16[320,128]{1,0:T(8,128)(2,1)S(1)}, u32[]{:S(2)}, u32[]{:S(2)}) collective-permute-start(bf16[320,128]{1,0:T(8,128)(2,1)S(1)} %get-tuple-element.55), channel_id=1, source_target_pairs={{0,16},{1,17},{2,18},{3,19},{4,20},{5,21},{6,22},{7,23},{8,24},{9,... | collective-permute-start | bytes 245768 | tf_op jit(solution)/shard_map/ppermute | solution.py:486
  56.1 8.0 %collective-permute-start.15 = (bf16[320,128]{1,0:T(8,128)(2,1)S(1)}, bf16[320,128]{1,0:T(8,128)(2,1)S(1)}, u32[]{:S(2)}, u32[]{:S(2)}) collective-permute-start(bf16[320,128]{1,0:T(8,128)(2,1)S(1)} %get-tuple-element.56), channel_id=1, source_target_pairs={{0,8},{1,9},{2,10},{3,11},{4,12},{5,13},{6,14},{7,15},{8,16},{9,17... | collective-permute-start | bytes 245768 | tf_op jit(solution)/shard_map/ppermute | solution.py:486
